TPU v7x, 32 devices: a whole 2x2x4 slice. The times are simulated.
32 devices in a mesh: sect: 2 (over core), gy: 4 (over y, x), gx: 4 (over z).
Axes of the slice: x: 2, y: 2, z: 4, core: 2. Of those that a mesh axis runs over, the one named last changes fastest.
Arguments:
- adjoint_init: float32 [2, 32, 128, 1024], P('sect', None, 'gy', 'gx'), may hold values from -6 to 6
- diffusivity: float32 [2, 128, 1024], P('sect', 'gy', 'gx'), may hold values from 0.02 to 0.12
- mixing: float32 [2, 32, 32], P('sect'), may hold values from -0.75 to 0.75
- coupling: float32 [2, 32, 8], P('sect'), may hold values from -6 to 6
- history: float32 [2, 4, 4, 128, 1024], P('sect', None, None, 'gy', 'gx'), may hold values from -6 to 6
- extract: float32 [4, 32], replicated, may hold values from -3 to 3
- land_mask: int32 [128, 1024], P('gy', 'gx'), may hold values 0 or 1
- regrid: float32 [16, 128, 128], P(('gy', 'gx')), may hold values from -0.5 to 0.5
- atmos_tile_index: int32 [2048, 1], replicated, may hold values from 0 to 15; in each aligned block of 128 rows (0 to 127, 128 to 255, ...) at most 16 rows name the same one
- ocean_block_index: int32 [2048], replicated, may hold values from 0 to 63
- atmos_block_index: int32 [2048], replicated, may hold values from 0 to 63
Outputs:
- adjoint_state: float32 [2, 32, 128, 1024], P('sect', None, 'gy', 'gx')
Inputs may be any that keep to these rules, and one draw needn't show every extreme that they name: `atmos_tile_index`: list rows i*128 to (i+1)*128 - 1 are ocean tile i's entries; among them at most 16 name the same atmosphere tile, and exactly 16 do so for some atmosphere tile.
All inputs are finite; a program needn't handle non-finite values. No bound on the sum of `land_mask` on one device may be relied on, other than what follows from the above.
Results may differ from a plain program's by a relative error of at most 0.0001.
Values sent between devices are 32-bit elements; how exact they have to be, the bound alone decides.
No kernel may reach another device: no remote copies, remote signals or barrier semaphores. Data moves between devices by JAX's collectives and lax.ppermute only.
A program may use at most 64 MiB of HBM per device.

v0:
```python
import math

import jax
import jax.numpy as jnp
from jax import lax
from jax.experimental import pallas as pl
from jax.experimental.pallas import tpu as pltpu
from jax.sharding import PartitionSpec as P

LANES = 128
SUB = 8
F32 = jnp.float32
BF16 = jnp.bfloat16


def full_dot(a, b, dims=(((1,), (0,)), ((), ()))):
    return lax.dot_general(a, b, dims, precision=lax.Precision.HIGHEST, preferred_element_type=F32)


def halves(x):
    high = x.astype(BF16)
    return high, (x - high.astype(F32)).astype(BF16)


def bf_dot(a, b, dims=(((1,), (0,)), ((), ()))):
    return lax.dot_general(a, b, dims, preferred_element_type=F32)


def dot3(a, b):
    (ah, al), (bh, bl) = a, b
    return bf_dot(ah, bh) + (bf_dot(ah, bl) + bf_dot(al, bh))


def grown(matrix):
    rows, cols = matrix.shape
    up = lax.broadcasted_iota(jnp.int32, (rows * SUB, rows), 0) // SUB
    up = (up == lax.broadcasted_iota(jnp.int32, (rows * SUB, rows), 1)).astype(F32)
    out = lax.broadcasted_iota(jnp.int32, (cols, cols * SUB), 1) // SUB
    out = (out == lax.broadcasted_iota(jnp.int32, (cols, cols * SUB), 0)).astype(F32)
    spread = full_dot(full_dot(up, matrix), out)
    i = lax.broadcasted_iota(jnp.int32, spread.shape, 0) % SUB
    j = lax.broadcasted_iota(jnp.int32, spread.shape, 1) % SUB
    return jnp.where(i == j, spread, 0.0)


def lane_ids(rows):
    return lax.broadcasted_iota(jnp.int32, (rows, LANES), 1)


def pack_columns(read, count, rows, tx, hw):
    per = LANES // hw
    ids = lane_ids(rows) // hw
    east, west = [], []
    last = tx // LANES - 1
    for block in range(-(-count // per)):
        e = jnp.zeros((rows, LANES), F32)
        w = jnp.zeros((rows, LANES), F32)
        for place in range(min(per, count - block * per)):
            f = block * per + place
            e_in, w_in = read(f, last), read(f, 0)
            e_shift, w_shift = (place * hw + hw) % LANES, place * hw
            e_in = pltpu.roll(e_in, e_shift, 1) if e_shift else e_in
            w_in = pltpu.roll(w_in, w_shift, 1) if w_shift else w_in
            e = jnp.where(ids == place, e_in, e)
            w = jnp.where(ids == place, w_in, w)
        east.append(e)
        west.append(w)
    return east, west


def side_block(from_west, from_east, f, hw):
    place = f % (LANES // hw)
    ids = lane_ids(from_west.shape[0])
    e_shift, w_shift = (-place * hw) % LANES, (-hw - place * hw) % LANES
    e = pltpu.roll(from_east, e_shift, 1) if e_shift else from_east
    w = pltpu.roll(from_west, w_shift, 1) if w_shift else from_west
    return jnp.where(ids < hw, e, jnp.where(ids >= LANES - hw, w, 0.0))


def pair_rows(a, b, first):
    low = lax.broadcasted_iota(jnp.int32, a.shape, 0) < SUB // 2
    turned = pltpu.roll(b, SUB // 2, 0)
    return jnp.where(low, a, turned) if first else jnp.where(low, turned, a)


def edge_tile(from_north, from_south, odd):
    if odd:
        from_north = pltpu.roll(from_north, SUB // 2, 0)
        from_south = pltpu.roll(from_south, SUB // 2, 0)
    low = lax.broadcasted_iota(jnp.int32, from_north.shape, 0) < SUB // 2
    return jnp.where(low, from_south, from_north)


def send_rows(read, count, ty, north_ref, south_ref):
    for pair in range(-(-count // 2)):
        a, b = 2 * pair, min(2 * pair + 1, count - 1)
        last = ty // SUB - 1
        north_ref[pair] = pair_rows(read(a, 0), read(b, 0), True)
        south_ref[pair] = pair_rows(read(a, last), read(b, last), False)


def ring_lap(p):
    rows, cols = p.shape
    around = pltpu.roll(p, 1, 0) + pltpu.roll(p, rows - 1, 0)
    around = around + pltpu.roll(p, 1, 1) + pltpu.roll(p, cols - 1, 1)
    return around - 4.0 * p


def with_ring(main, packed_west, packed_east, f, north_ref, south_ref, hw):
    bottom = edge_tile(north_ref[f // 2], south_ref[f // 2], f % 2)
    side = side_block(packed_west, packed_east, f, hw)
    return jnp.concatenate([jnp.concatenate([main, bottom], axis=0), side], axis=1)


def sides_with_rows(west_ref, east_ref, north_ref, south_ref, first, blocks, tx):
    west, east = [], []
    per = tx // LANES
    for block in range(blocks):
        lanes = pl.ds((block % per) * LANES, LANES)
        out = []
        for which, ref in enumerate((west_ref, east_ref)):
            f, at = divmod(which * blocks + block, per)
            f = first + f
            cols = pl.ds(at * LANES, LANES)
            tile = edge_tile(north_ref[f // 2, :, cols], south_ref[f // 2, :, cols], f % 2)
            out.append(jnp.concatenate([ref[:, pl.ds(block * LANES, LANES)], tile], axis=0))
        west.append(out[0])
        east.append(out[1])
    return west, east


def packed_reader(west_ref, east_ref, blocks, tx):
    per = tx // LANES

    def read(f, row_tile):
        pieces = []
        for at in range(per):
            which, block = divmod(f * per + at, blocks)
            rows = pl.ds(row_tile * SUB, SUB)
            if which < 2:
                pieces.append((west_ref, east_ref)[which][rows, pl.ds(block * LANES, LANES)])
            else:
                pieces.append(jnp.zeros((SUB, LANES), F32))
        return jnp.concatenate(pieces, axis=1)

    return read, -(-2 * blocks // per)


def call(kernel, outs, *args, smem=(), scratch=(), flops=0):
    space = lambda i: pltpu.SMEM if i in smem else pltpu.VMEM
    nbytes = sum(math.prod(a.shape) * 4 for a in (*args, *outs))
    return pl.pallas_call(
        kernel,
        out_shape=outs,
        in_specs=[pl.BlockSpec(memory_space=space(i)) for i in range(len(args))],
        out_specs=[pl.BlockSpec(memory_space=pltpu.VMEM) for _ in outs],
        scratch_shapes=scratch,
        compiler_params=pltpu.CompilerParams(vmem_limit_bytes=48 * 2**20),
        cost_estimate=pl.CostEstimate(flops=flops, bytes_accessed=nbytes, transcendentals=0),
    )(*args)


def tile_of(ref, g, l):
    block = ref[:, g * SUB : (g + 1) * SUB, l * LANES : (l + 1) * LANES]
    return block.reshape(-1, LANES)


def project_kernel(adj_ref, mask_ref, mix_ref, ext_ref, coup_ref, hist_ref, diff_ref, keep_ref, send_ref):
    _, nc, ty, tx = adj_ref.shape
    _, steps, fields = hist_ref.shape[:3]
    hf = fields // 2
    mix = mix_ref[0]
    rows = ext_ref[...]
    lows, highs = [], []
    for m in range(steps + 1):
        big = grown(rows)
        lows.append(big[: hf * SUB])
        highs.append(big[hf * SUB :])
        if m < steps:
            force = grown(full_dot(rows, coup_ref[0]))
            height, width = hf * SUB, force.shape[1]
            for ref, at in ((keep_ref, 0), (send_ref, height)):
                per = ty // height
                r0, c0 = (m % per) * height, (m // per) * LANES
                ref[(steps + 1) * hf, r0 : r0 + height, c0 : c0 + width] = force[at : at + height]
            rows = rows + full_dot(rows, mix, (((1,), (1,)), ((), ())))
    big = halves(jnp.concatenate(lows + highs, axis=0))
    count = (steps + 1) * hf
    for g in range(ty // SUB):
        for l in range(tx // LANES):
            rs, cs = slice(g * SUB, (g + 1) * SUB), slice(l * LANES, (l + 1) * LANES)
            wet = mask_ref[rs, cs].astype(F32)
            u = (adj_ref[0, :, rs, cs] * wet[None]).reshape(nc * SUB, LANES)
            t = dot3(big, halves(u)).reshape(2 * count, SUB, LANES)
            keep_ref[:count, rs, cs] = t[:count]
            send_ref[:count, rs, cs] = t[count:]
    send_ref[count + 1] = diff_ref[0]
    for k in range(steps):
        for q in range(fields):
            send_ref[count + 2 + k * fields + q] = hist_ref[0, k, q]


def field_places(steps, hf):
    with_halo, without = [], []
    for m in range(steps + 1):
        for q in range(hf):
            (with_halo if m < steps else without).append(("t", m, q))
    for n in range(steps):
        for m in range(steps - n):
            for q in range(hf):
                (with_halo if n + m < steps - 1 else without).append(("g", n, m, q))
    with_halo += ["d", "w"]
    return {key: i for i, key in enumerate(with_halo + without)}, len(with_halo)


def force_kernel(
    places, halo_count, flag_ref, keep_ref, got_ref, hist_ref, diff_ref, mask_ref, main_ref, east_ref, west_ref
):
    _, steps, fields, ty, tx = hist_ref.shape
    hf, hw = fields // 2, steps
    count = (steps + 1) * hf
    ocean = flag_ref[0] == 0
    pick = lambda a, b: jnp.where(ocean, a, b)
    for m in range(steps + 1):
        for q in range(hf):
            main_ref[places["t", m, q]] = pick(keep_ref[m * hf + q], got_ref[m * hf + q])
    main_ref[places["d"]] = pick(diff_ref[0], got_ref[count + 1])
    main_ref[places["w"]] = mask_ref[...].astype(F32)
    height, width = hf * SUB, 2 * fields * SUB
    per = ty // height
    big = []
    for m in range(steps):
        r0, c0 = (m % per) * height, (m // per) * LANES
        at = (count, slice(r0, r0 + height), slice(c0, c0 + width))
        big.append(pick(keep_ref[at], got_ref[at]))
    big = halves(jnp.concatenate(big, axis=0))
    for g in range(ty // SUB):
        for l in range(tx // LANES):
            rs, cs = slice(g * SUB, (g + 1) * SUB), slice(l * LANES, (l + 1) * LANES)
            for n in range(steps):
                k = steps - 1 - n
                own = hist_ref[0, k, :, rs, cs]
                far = got_ref[count + 2 + k * fields : count + 2 + (k + 1) * fields, rs, cs]
                h = jnp.concatenate([pick(own, far), pick(far, own)], axis=0).reshape(-1, LANES)
                top = (steps - n) * height
                out = dot3((big[0][:top], big[1][:top]), halves(h))
                for m in range(steps - n):
                    for q in range(hf):
                        at = (m * hf + q) * SUB
                        main_ref[places["g", n, m, q], rs, cs] = out[at : at + SUB]
    read = lambda f, l: main_ref[f, :, l * LANES : (l + 1) * LANES]
    east, west = pack_columns(read, halo_count, ty, tx, hw)
    for block, (e, w) in enumerate(zip(east, west)):
        east_ref[:, block * LANES : (block + 1) * LANES] = e
        west_ref[:, block * LANES : (block + 1) * LANES] = w


def rows_kernel(halo_count, blocks, main_ref, west_ref, east_ref, north_ref, south_ref):
    _, ty, tx = main_ref.shape
    packed, more = packed_reader(west_ref, east_ref, blocks, tx)

    def read(f, t):
        return main_ref[f, t * SUB : (t + 1) * SUB, :] if f < halo_count else packed(f - halo_count, t)

    send_rows(read, halo_count + more, ty, north_ref, south_ref)


def index_kernel(cap, slots, nb, pos_ref, dest_ref, src_ref, dst_ref, sel_ref, acc_ref):
    tiles, entries = dest_ref.shape
    tile = pos_ref[0]
    count = tiles * cap
    per_row = slots // nb
    place = lambda b: (b % nb) * per_row + b // nb
    row = lax.broadcasted_iota(jnp.int32, (entries, entries), 0)
    col = lax.broadcasted_iota(jnp.int32, (entries, entries), 1)
    dest = dest_ref[pl.ds(tile, 1), :]
    across = jnp.broadcast_to(dest.astype(F32), (entries, entries))
    same = (across == across.T) & (row < col)
    rank = jnp.sum(same.astype(F32), axis=0, keepdims=True).astype(jnp.int32)
    slot = dest * cap + rank
    last = (((1,), (1,)), ((), ()))

    def onehot(size, values):
        ids = lax.broadcasted_iota(jnp.int32, (size, entries), 0)
        return (ids == values).astype(F32).astype(BF16)

    sel_ref[...] = bf_dot(onehot(count, slot), onehot(slots, place(src_ref[pl.ds(tile, 1), :])), last)
    acc_ref[...] = jnp.zeros_like(acc_ref)
    before = (row < col).astype(F32).astype(BF16)

    def source(i, carry):
        mine = dest_ref[pl.ds(i, 1), :] == tile
        mine_f = jnp.broadcast_to(mine.astype(F32), (SUB, entries)).astype(BF16)
        ranks = bf_dot(mine_f, before)[:1].astype(jnp.int32)
        spot = jnp.where(mine, i * cap + ranks, -1)
        acc_ref[...] += bf_dot(onehot(slots, place(dst_ref[pl.ds(i, 1), :])), onehot(count, spot), last)
        return carry

    lax.fori_loop(0, tiles, source, 0)


def surface_kernel(
    places, halo_count, steps, hf, main_ref, west_ref, east_ref, north_ref, south_ref, regrid_ref, sel_ref, out_ref
):
    _, ty, tx = main_ref.shape
    hw = steps
    per = LANES // hw
    blocks = -(-halo_count // per)
    wests, easts = sides_with_rows(west_ref, east_ref, north_ref, south_ref, halo_count, blocks, tx)

    def ext(key):
        f = places[key]
        if f < halo_count:
            return with_ring(main_ref[f], wests[f // per], easts[f // per], f, north_ref, south_ref, hw)
        main = jnp.concatenate([main_ref[f], jnp.zeros((SUB, tx), F32)], axis=0)
        return jnp.concatenate([main, jnp.zeros((ty + SUB, LANES), F32)], axis=1)

    diff, wet = ext("d"), ext("w")
    weights = halves(regrid_ref[0])
    sel = sel_ref[...].astype(BF16)
    surfaces = {}
    for q in range(hf):
        t = [ext(("t", m, q)) for m in range(steps + 1)]
        for n in range(steps):
            t = [wet * (t[m + 1] + ring_lap(diff * t[m]) + ext(("g", n, m, q))) for m in range(steps - n)]
            surfaces[n, q] = t[0]
    for n in range(steps):
        for q in range(hf):
            s = surfaces[n, q]
            s = jnp.concatenate([s[:ty, l * LANES : (l + 1) * LANES] for l in range(tx // LANES)], axis=0)
            s = halves(dot3(halves(s), weights))
            at = (n * hf + q) * LANES
            out_ref[:, at : at + LANES] = bf_dot(sel, s[0]) + bf_dot(sel, s[1])


def gather_kernel(acc_ref, in_ref, out_ref):
    count, ty, tx = out_ref.shape
    acc = acc_ref[...].astype(BF16)
    for i in range(count):
        high, low = halves(in_ref[:, i * LANES : (i + 1) * LANES])
        total = bf_dot(acc, high) + bf_dot(acc, low)
        for l in range(tx // LANES):
            out_ref[i, :, l * LANES : (l + 1) * LANES] = total[l * ty : (l + 1) * ty]


def state_reader(adj_ref, hist_ref, far_ref, far_at, diff_ref, wet):
    _, steps, fields = hist_ref.shape[:3]
    nc = adj_ref.shape[1]
    forced = (steps - 1) * fields
    total = nc + 2 * forced + 2

    def read(f, rows, cols):
        if f < nc:
            return adj_ref[0, f, rows, cols]
        f -= nc
        if f < 2 * forced:
            part, f = divmod(f, forced)
            k, q = divmod(f, fields)
            if part == 0:
                return hist_ref[0, k + 1, q, rows, cols]
            return far_ref[far_at + (k + 1) * fields + q, rows, cols]
        if f == 2 * forced:
            return diff_ref[0, rows, cols]
        return wet(rows, cols)

    return read, total


def own_wet(flag_ref, mask_ref):
    ocean = flag_ref[0] == 0
    return lambda rows, cols: jnp.where(ocean, mask_ref[rows, cols].astype(F32), 1.0)


def state_columns_kernel(far_at, flag_ref, adj_ref, hist_ref, far_ref, diff_ref, mask_ref, east_ref, west_ref):
    ty, tx = mask_ref.shape
    hw = hist_ref.shape[1]
    read, total = state_reader(adj_ref, hist_ref, far_ref, far_at, diff_ref, own_wet(flag_ref, mask_ref))
    at = lambda f, l: read(f, slice(0, ty), slice(l * LANES, (l + 1) * LANES))
    east, west = pack_columns(at, total, ty, tx, hw)
    for block, (e, w) in enumerate(zip(east, west)):
        east_ref[:, block * LANES : (block + 1) * LANES] = e
        west_ref[:, block * LANES : (block + 1) * LANES] = w


def state_rows_kernel(
    far_at, blocks, flag_ref, adj_ref, hist_ref, far_ref, diff_ref, mask_ref, west_ref, east_ref, north_ref, south_ref
):
    ty, tx = mask_ref.shape
    read, total = state_reader(adj_ref, hist_ref, far_ref, far_at, diff_ref, own_wet(flag_ref, mask_ref))
    packed, more = packed_reader(west_ref, east_ref, blocks, tx)

    def at(f, t):
        rows = slice(t * SUB, (t + 1) * SUB)
        return read(f, rows, slice(0, tx)) if f < total else packed(f - total, t)

    send_rows(at, total + more, ty, north_ref, south_ref)


def state_kernel(
    far_at,
    blocks,
    flag_ref,
    adj_ref,
    hist_ref,
    far_ref,
    diff_ref,
    mask_ref,
    west_ref,
    east_ref,
    north_ref,
    south_ref,
    mix_ref,
    coup_ref,
    out_ref,
    ring_ref,
    late_ref,
    state,
    force,
    spread,
):
    ty, tx = mask_ref.shape
    nc = adj_ref.shape[1]
    _, steps, fields = hist_ref.shape[:3]
    hw = steps
    per = LANES // hw
    ocean = flag_ref[0] == 0
    read, total = state_reader(adj_ref, hist_ref, far_ref, far_at, diff_ref, own_wet(flag_ref, mask_ref))
    wests, easts = sides_with_rows(west_ref, east_ref, north_ref, south_ref, total, blocks, tx)

    def ext(f):
        main = read(f, slice(0, ty), slice(0, tx))
        return with_ring(main, wests[f // per], easts[f // per], f, north_ref, south_ref, hw)

    for c in range(nc):
        state[c] = ext(c)
    forced = (steps - 1) * fields
    for k in range(1, steps):
        for q in range(fields):
            force[k, q] = ext(nc + (k - 1) * fields + q)
            force[k, fields + q] = ext(nc + forced + (k - 1) * fields + q)
    for q in range(fields):
        force[0, q, :ty, :tx] = hist_ref[0, 0, q]
        force[0, fields + q, :ty, :tx] = far_ref[far_at + q]
    diff, wet = ext(nc + 2 * forced), ext(nc + 2 * forced + 1)
    ring_ref[...] = diff
    ident = lax.broadcasted_iota(jnp.int32, (nc, nc), 0) == lax.broadcasted_iota(jnp.int32, (nc, nc), 1)
    step_m = mix_ref[0].T + ident.astype(F32)
    coup = coup_ref[0]
    late = coup[:, fields:]
    powers = []
    for i in range(steps):
        powers.append(late)
        late = full_dot(step_m, late)
    columns = []
    for k in range(steps - 1, -1, -1):
        for j in range(k + 1):
            columns.append(math.comb(k, j) * powers[k - j])
    at = 0
    for column in columns:
        late_ref[:, at : at + fields * SUB] = grown(column)
        at += fields * SUB
    first = lax.broadcasted_iota(jnp.int32, coup.shape, 1) < fields
    coup = jnp.where(jnp.logical_or(first, ocean), coup, 0.0)
    mix8, coup8 = halves(grown(step_m)), halves(grown(coup))

    for n in range(steps):
        k = steps - 1 - n
        small = n == steps - 1

        def one(c, carry):
            u = wet * state[c]
            state[c] = u
            spread[c] = ring_lap(diff * u)
            return carry

        lax.fori_loop(0, nc, one, 0)
        for g in range(ty // SUB + (not small)):
            for l in range(tx // LANES + (not small)):
                rs, cs = slice(g * SUB, (g + 1) * SUB), slice(l * LANES, (l + 1) * LANES)
                u = state[:, rs, cs].reshape(nc * SUB, LANES)
                h = force[k, :, rs, cs].reshape(2 * fields * SUB, LANES)
                new = dot3(mix8, halves(u)) + dot3(coup8, halves(h))
                new = new.reshape(nc, SUB, LANES) + spread[:, rs, cs]
                if small:
                    out_ref[:, rs, cs] = new
                else:
                    state[:, rs, cs] = new


def late_fields(steps, fields):
    return [(n, q) for n in range(steps - 1) for q in range(fields)]


def late_main(steps, hf, own_ref, far_ref):
    def read(n, q):
        return far_ref[n * hf + q] if q < hf else own_ref[n * hf + q - hf]

    return read


def late_columns_kernel(steps, own_ref, far_ref, east_ref, west_ref):
    count, ty, tx = own_ref.shape
    hf = count // steps
    todo = late_fields(steps, 2 * hf)

    def read(f, l):
        n, q = todo[f]
        ref, i = (far_ref, n * hf + q) if q < hf else (own_ref, n * hf + q - hf)
        return ref[i, :, l * LANES : (l + 1) * LANES]

    east, west = pack_columns(read, len(todo), ty, tx, steps)
    for block, (e, w) in enumerate(zip(east, west)):
        east_ref[:, block * LANES : (block + 1) * LANES] = e
        west_ref[:, block * LANES : (block + 1) * LANES] = w


def late_rows_kernel(steps, blocks, own_ref, far_ref, west_ref, east_ref, north_ref, south_ref):
    count, ty, tx = own_ref.shape
    hf = count // steps
    todo = late_fields(steps, 2 * hf)
    packed, more = packed_reader(west_ref, east_ref, blocks, tx)

    def read(f, t):
        if f >= len(todo):
            return packed(f - len(todo), t)
        n, q = todo[f]
        ref, i = (far_ref, n * hf + q) if q < hf else (own_ref, n * hf + q - hf)
        return ref[i, t * SUB : (t + 1) * SUB, :]

    send_rows(read, len(todo) + more, ty, north_ref, south_ref)


def late_kernel(
    steps,
    blocks,
    flag_ref,
    base_ref,
    ring_ref,
    late_ref,
    own_ref,
    far_ref,
    west_ref,
    east_ref,
    north_ref,
    south_ref,
    out_ref,
    stack,
):
    count, ty, tx = own_ref.shape
    hf = count // steps
    fields = 2 * hf
    nc = base_ref.shape[0]
    per = LANES // steps
    todo = late_fields(steps, fields)
    read = late_main(steps, hf, own_ref, far_ref)

    @pl.when(flag_ref[0] == 0)
    def _():
        out_ref[0] = base_ref[...]

    @pl.when(flag_ref[0] != 0)
    def _():
        diff = ring_ref[...]
        wests, easts = sides_with_rows(west_ref, east_ref, north_ref, south_ref, len(todo), blocks, tx)
        at = 0
        for n in range(steps):
            k = steps - 1 - n
            for q in range(fields):
                r = read(n, q)
                if k:
                    f = todo.index((n, q))
                    r = with_ring(r, wests[f // per], easts[f // per], f, north_ref, south_ref, steps)
                for j in range(k + 1):
                    stack[at + j * fields + q] = r[:ty, :tx]
                    if j < k:
                        r = ring_lap(diff * r)
            at += (k + 1) * fields
        big = halves(late_ref[...])
        for g in range(ty // SUB):
            for l in range(tx // LANES):
                rs, cs = slice(g * SUB, (g + 1) * SUB), slice(l * LANES, (l + 1) * LANES)
                more = dot3(big, halves(stack[:, rs, cs].reshape(-1, LANES)))
                out_ref[0, :, rs, cs] = base_ref[:, rs, cs] + more.reshape(nc, SUB, LANES)


def shifted(x, axis, by, wrap, sect=None):
    size = lax.axis_size(axis)
    pairs = [(i, (i + by) % size) for i in range(size) if wrap or 0 <= i + by < size]
    if sect is None:
        return lax.ppermute(x, axis, pairs)
    base = sect * size
    return lax.ppermute(x, ("sect", axis), [(base + i, base + j) for i, j in pairs])


def struct(*shape):
    return jax.ShapeDtypeStruct(shape, F32)


def partial(kernel, *args):
    def run(*refs):
        kernel(*args, *refs)

    run.__name__ = kernel.__name__
    return run


def body(
    adjoint_init,
    diffusivity,
    mixing,
    coupling,
    history,
    extract,
    land_mask,
    regrid,
    atmos_tile_index,
    ocean_block_index,
    atmos_block_index,
):
    _, steps, fields, ty, tx = history.shape
    nc = adjoint_init.shape[1]
    hf, hw = fields // 2, steps
    per = LANES // hw
    sect = lax.axis_index("sect").astype(jnp.int32)
    tile = (lax.axis_index("gy") * lax.axis_size("gx") + lax.axis_index("gx")).astype(jnp.int32)
    flag = sect.reshape(1)
    tiles = lax.axis_size("gy") * lax.axis_size("gx")
    entries = ocean_block_index.shape[0] // tiles
    cap = 2 * entries // tiles
    cells = regrid.shape[1]
    slots = ty * tx // cells
    nb = tx // cells

    def exchange(x_after, x_before, axis, wrap, only=None):
        return shifted(x_after, axis, 1, wrap, only), shifted(x_before, axis, -1, wrap, only)

    count = (steps + 1) * hf
    keep, send = call(
        project_kernel,
        [struct(count + 1, ty, tx), struct(count + 2 + steps * fields, ty, tx)],
        adjoint_init, land_mask, mixing, extract, coupling, history, diffusivity,
    )
    got = lax.ppermute(send, "sect", [(0, 1), (1, 0)])
    places, halo_count = field_places(steps, hf)
    blocks = -(-halo_count // per)
    main, east, west = call(
        partial(force_kernel, places, halo_count),
        [struct(len(places), ty, tx), struct(ty, blocks * LANES), struct(ty, blocks * LANES)],
        flag, keep, got, history, diffusivity, land_mask,
        smem=(0,),
    )
    from_west, from_east = exchange(east, west, "gx", True)
    pairs = -(-(halo_count + -(-2 * blocks * LANES // tx)) // 2)
    north, south = call(
        partial(rows_kernel, halo_count, blocks),
        [struct(pairs, SUB, tx)] * 2,
        main, from_west, from_east,
    )
    from_north, from_south = exchange(south, north, "gy", False)
    sel, acc = call(
        partial(index_kernel, cap, slots, nb),
        [struct(tiles * cap, slots), struct(slots, tiles * cap)],
        tile.reshape(1),
        atmos_tile_index.reshape(tiles, entries),
        ocean_block_index.reshape(tiles, entries),
        atmos_block_index.reshape(tiles, entries),
        smem=(0,),
    )
    [packed] = call(
        partial(surface_kernel, places, halo_count, steps, hf),
        [struct(tiles * cap, steps * hf * LANES)],
        main, from_west, from_east, from_north, from_south, regrid, sel,
    )
    arrived = lax.all_to_all(
        packed.reshape(tiles, cap, -1), ("gy", "gx"), split_axis=0, concat_axis=0, tiled=True
    ).reshape(tiles * cap, -1)

    far_at = count + 2
    total = nc + 2 * (steps - 1) * fields + 2
    blocks = -(-total // per)
    east, west = call(
        partial(state_columns_kernel, far_at),
        [struct(ty, blocks * LANES)] * 2,
        flag, adjoint_init, history, got, diffusivity, land_mask,
        smem=(0,),
    )
    from_west, from_east = exchange(east, west, "gx", True)
    pairs = -(-(total + -(-2 * blocks * LANES // tx)) // 2)
    north, south = call(
        partial(state_rows_kernel, far_at, blocks),
        [struct(pairs, SUB, tx)] * 2,
        flag, adjoint_init, history, got, diffusivity, land_mask, from_west, from_east,
        smem=(0,),
    )
    from_north, from_south = exchange(south, north, "gy", False)
    terms = fields * steps * (steps + 1) // 2
    ext = (ty + SUB, tx + LANES)
    base, ring, late = call(
        partial(state_kernel, far_at, blocks),
        [struct(nc, ty, tx), struct(*ext), struct(nc * SUB, terms * SUB)],
        flag, adjoint_init, history, got, diffusivity, land_mask,
        from_west, from_east, from_north, from_south, mixing, coupling,
        smem=(0,),
        scratch=[
            pltpu.VMEM((nc, *ext), F32),
            pltpu.VMEM((steps, 2 * fields, *ext), F32),
            pltpu.VMEM((nc, *ext), F32),
        ],
    )

    [own] = call(gather_kernel, [struct(steps * hf, ty, tx)], acc, arrived)
    far = lax.ppermute(own, "sect", [(0, 1)])
    halo_count = (steps - 1) * fields
    blocks = -(-halo_count // per)
    east, west = call(partial(late_columns_kernel, steps), [struct(ty, blocks * LANES)] * 2, own, far)
    from_west, from_east = exchange(east, west, "gx", True, 1) if False else exchange(east, west, "gx", True)
    pairs = -(-(halo_count + -(-2 * blocks * LANES // tx)) // 2)
    north, south = call(
        partial(late_rows_kernel, steps, blocks), [struct(pairs, SUB, tx)] * 2, own, far, from_west, from_east
    )
    from_north, from_south = exchange(south, north, "gy", False)
    [out] = call(
        partial(late_kernel, steps, blocks),
        [struct(1, nc, ty, tx)],
        flag, base, ring, late, own, far, from_west, from_east, from_north, from_south,
        smem=(0,),
        scratch=[pltpu.VMEM((terms, ty, tx), F32)],
    )
    return out


def solution(mesh):
    placed = (
        P("sect", None, "gy", "gx"),
        P("sect", "gy", "gx"),
        P("sect", None, None),
        P("sect", None, None),
        P("sect", None, None, "gy", "gx"),
        P(),
        P("gy", "gx"),
        P(("gy", "gx"), None, None),
        P(),
        P(),
        P(),
    )
    return jax.shard_map(
        body, mesh=mesh, in_specs=placed, out_specs=P("sect", None, "gy", "gx"), check_vma=False
    )
```

profile of v0, /device:TPU:28, one launch (start us, length us, event | category | flops | bytes accessed | tf_op | source)
XLA Modules:
  0.0 115.9 jit_solution(11318859077744883282)
XLA Ops:
  0.0 0.8 copy.12.coup_ref.refs_11_
  0.8 0.0 copy-start
  0.8 1.2 %copy-done = f32[1,32,32,256]{3,2,1,0:T(8,128)S(1)} copy-done((f32[1,32,32,256]{3,2,1,0:T(8,128)S(1)}, f32[1,32,32,256]{3,2,1,0:T(8,128)}, u32[]{:S(2)}) %copy-start) | copy-done | bytes 1048600
  2.0 1.0 copy-done.2
  3.1 0.8 copy-done.4
  3.8 0.8 copy-done.6
  4.6 3.0 %shard_map.109 = (f32[11,32,256]{2,1,0:T(8,128)S(1)}, f32[28,32,256]{2,1,0:T(8,128)S(1)}) custom-call(f32[1,32,32,256]{3,2,1,0:T(8,128)S(1)} %copy-done, s32[32,256]{1,0:T(8,128)S(1)} %copy-done.4, f32[1,32,32]{2,1,0:T(8,128)S(1)} %copy-done.8, f32[4,32]{1,0:T(4,128)S(1)} %copy-done.13, f32[1,32,8]{2,1,0:T(8,128)S(1)} %copy.12.coup_ref.refs_11_, ...), custom_call_target="tpu_custom_call" | custom-call | bytes 2921984 | tf_op jit(solution)/shard_map/pallas_call | solution.py:152
  7.6 0.1 collective-permute-start
  7.7 2.5 %collective-permute-done.refs_3_.refs_2_ = f32[28,32,256]{2,1,0:T(8,128)S(1)} collective-permute-done((f32[28,32,256]{2,1,0:T(8,128)S(1)}, f32[28,32,256]{2,1,0:T(8,128)S(1)}, u32[]{:S(2)}, u32[]{:S(2)}) %collective-permute-start) | collective-permute-done | bytes 917536 | tf_op jit(solution)/shard_map/ppermute | solution.py:643
  10.2 0.6 shard_map.114
  10.8 0.3 collective-permute-start.5
  11.1 1.8 %collective-permute-start.6 = (f32[32,128]{1,0:T(8,128)S(1)}, f32[32,128]{1,0:T(8,128)S(1)}, u32[]{:S(2)}, u32[]{:S(2)}) collective-permute-start(f32[32,128]{1,0:T(8,128)S(1)} %get-tuple-element.37), channel_id=1, source_target_pairs={{0,3},{1,0},{2,1},{3,2},{4,7},{5,4},{6,5},{7,6},{8,11},{9,8},{10,9... | collective-permute-start | bytes 49160 | tf_op jit(solution)/shard_map/ppermute | solution.py:590
  12.9 1.7 %collective-permute-done.5.refs_1_ = f32[32,128]{1,0:T(8,128)S(1)} collective-permute-done((f32[32,128]{1,0:T(8,128)S(1)}, f32[32,128]{1,0:T(8,128)S(1)}, u32[]{:S(2)}, u32[]{:S(2)}) %collective-permute-start.5) | collective-permute-done | bytes 16416 | tf_op jit(solution)/shard_map/ppermute | solution.py:590
  14.6 2.0 %collective-permute-done.6.refs_2_ = f32[32,128]{1,0:T(8,128)S(1)} collective-permute-done((f32[32,128]{1,0:T(8,128)S(1)}, f32[32,128]{1,0:T(8,128)S(1)}, u32[]{:S(2)}, u32[]{:S(2)}) %collective-permute-start.6) | collective-permute-done | bytes 16416 | tf_op jit(solution)/shard_map/ppermute | solution.py:590
  16.7 3.5 %collective-permute-start.7 = (f32[12,8,256]{2,1,0:T(8,128)S(1)}, f32[12,8,256]{2,1,0:T(8,128)S(1)}, u32[]{:S(2)}, u32[]{:S(2)}) collective-permute-start(f32[12,8,256]{2,1,0:T(8,128)S(1)} %get-tuple-element.38), channel_id=1, source_target_pairs={{0,4},{4,8},{8,12},{1,5},{5,9},{9,13},{2,6},{6,10},{10,14},{3,7},{... | collective-permute-start | bytes 294920 | tf_op jit(solution)/shard_map/ppermute | solution.py:590
  20.2 3.3 %collective-permute-start.8 = (f32[12,8,256]{2,1,0:T(8,128)S(1)}, f32[12,8,256]{2,1,0:T(8,128)S(1)}, u32[]{:S(2)}, u32[]{:S(2)}) collective-permute-start(f32[12,8,256]{2,1,0:T(8,128)S(1)} %get-tuple-element.39), channel_id=1, source_target_pairs={{4,0},{8,4},{12,8},{5,1},{9,5},{13,9},{6,2},{10,6},{14,10},{7,3},{... | collective-permute-start | bytes 294920 | tf_op jit(solution)/shard_map/ppermute | solution.py:590
  23.6 0.0 copy-start.11
  23.6 0.0 copy-start.10
  23.6 0.7 copy-done.11
  24.3 0.0 copy-done.10
  24.3 5.0 %shard_map.113 = (f32[256,64]{1,0:T(8,128)S(1)}, f32[64,256]{1,0:T(8,128)S(1)}) custom-call(s32[1]{0:T(128)} %bitcast.1.refs_0_, s32[16,128]{1,0:T(8,128)S(1)} %bitcast.9, s32[16,128]{1,0:T(8,128)S(1)} %bitcast.10, s32[16,128]{1,0:T(8,128)S(1)} %bitcast.11), custom_call_target="tpu_custom_call" | custom-call | bytes 155652 | tf_op jit(solution)/shard_map/pallas_call | solution.py:152
  29.3 0.0 collective-permute-done.7.refs_3_
  29.3 0.0 collective-permute-done.8.refs_4_
  29.4 1.5 %shard_map.116 = f32[256,1024]{1,0:T(8,128)S(1)} custom-call(f32[32,32,256]{2,1,0:T(8,128)S(1)} %get-tuple-element.35.refs_0_, f32[32,128]{1,0:T(8,128)S(1)} %collective-permute-done.5.refs_1_, f32[32,128]{1,0:T(8,128)S(1)} %collective-permute-done.6.refs_2_, f32[12,8,256]{2,1,0:T(8,128)S(1)} %collective-permute-done.7.refs_3_, ...), custom_call_target="tpu_custom_call" | custom-call | bytes 2457600 | tf_op jit(solution)/shard_map/pallas_call | solution.py:152
  30.8 27.7 %all_to_all.5 = f32[16,16,1024]{2,1,0:T(8,128)S(1)} all-to-all(f32[16,16,1024]{2,1,0:T(8,128)S(1)} %bitcast.7), channel_id=1, replica_groups=mesh['sect'=2,'gy'=4,'gx'=4] {'gy','gx'}, dimensions={0} | all-to-all | bytes 2097152 | tf_op jit(solution)/shard_map/all_to_all | solution.py:674
  58.5 0.3 shard_map.117.refs_0_.refs_4_
  58.8 1.3 %collective-permute-start.9 = (f32[8,32,256]{2,1,0:T(8,128)S(1)}, f32[8,32,256]{2,1,0:T(8,128)S(1)}, u32[]{:S(2)}, u32[]{:S(2)}) collective-permute-start(f32[8,32,256]{2,1,0:T(8,128)S(1)} %shard_map.117.refs_0_.refs_4_), channel_id=1, source_target_pairs={{0,16},{1,17},{2,18},{3,19},{4,20},{5,21},{6,22},{7,23},{8,24},{9,... | collective-permute-start | bytes 786440 | tf_op jit(solution)/shard_map/ppermute | solution.py:712
  60.1 0.6 shard_map.110
  60.7 3.3 %collective-permute-start.1 = (f32[32,256]{1,0:T(8,128)S(1)}, f32[32,256]{1,0:T(8,128)S(1)}, u32[]{:S(2)}, u32[]{:S(2)}) collective-permute-start(f32[32,256]{1,0:T(8,128)S(1)} %get-tuple-element.26), channel_id=1, source_target_pairs={{0,1},{1,2},{2,3},{3,0},{4,5},{5,6},{6,7},{7,4},{8,9},{9,10},{10,1... | collective-permute-start | bytes 98312 | tf_op jit(solution)/shard_map/ppermute | solution.py:590
  64.0 0.0 collective-permute-start.2
  64.0 1.6 %collective-permute-done.1.refs_6_ = f32[32,256]{1,0:T(8,128)S(1)} collective-permute-done((f32[32,256]{1,0:T(8,128)S(1)}, f32[32,256]{1,0:T(8,128)S(1)}, u32[]{:S(2)}, u32[]{:S(2)}) %collective-permute-start.1) | collective-permute-done | bytes 32800 | tf_op jit(solution)/shard_map/ppermute | solution.py:590
  65.6 4.1 %collective-permute-done.2.refs_7_ = f32[32,256]{1,0:T(8,128)S(1)} collective-permute-done((f32[32,256]{1,0:T(8,128)S(1)}, f32[32,256]{1,0:T(8,128)S(1)}, u32[]{:S(2)}, u32[]{:S(2)}) %collective-permute-start.2) | collective-permute-done | bytes 32800 | tf_op jit(solution)/shard_map/ppermute | solution.py:590
  69.7 0.1 shard_map.111
  69.8 2.5 %collective-permute-start.3 = (f32[30,8,256]{2,1,0:T(8,128)S(1)}, f32[30,8,256]{2,1,0:T(8,128)S(1)}, u32[]{:S(2)}, u32[]{:S(2)}) collective-permute-start(f32[30,8,256]{2,1,0:T(8,128)S(1)} %get-tuple-element.28), channel_id=1, source_target_pairs={{0,4},{4,8},{8,12},{1,5},{5,9},{9,13},{2,6},{6,10},{10,14},{3,7},{... | collective-permute-start | bytes 737288 | tf_op jit(solution)/shard_map/ppermute | solution.py:590
  72.2 4.3 %collective-permute-start.4 = (f32[30,8,256]{2,1,0:T(8,128)S(1)}, f32[30,8,256]{2,1,0:T(8,128)S(1)}, u32[]{:S(2)}, u32[]{:S(2)}) collective-permute-start(f32[30,8,256]{2,1,0:T(8,128)S(1)} %get-tuple-element.29), channel_id=1, source_target_pairs={{4,0},{8,4},{12,8},{5,1},{9,5},{13,9},{6,2},{10,6},{14,10},{7,3},{... | collective-permute-start | bytes 737288 | tf_op jit(solution)/shard_map/ppermute | solution.py:590
  76.5 0.0 collective-permute-done.9.refs_1_.refs_5_
  76.5 0.2 shard_map.118
  76.7 0.1 collective-permute-start.10
  76.8 2.0 %collective-permute-start.11 = (f32[32,128]{1,0:T(8,128)S(1)}, f32[32,128]{1,0:T(8,128)S(1)}, u32[]{:S(2)}, u32[]{:S(2)}) collective-permute-start(f32[32,128]{1,0:T(8,128)S(1)} %get-tuple-element.42), channel_id=1, source_target_pairs={{0,3},{1,0},{2,1},{3,2},{4,7},{5,4},{6,5},{7,6},{8,11},{9,8},{10,9... | collective-permute-start | bytes 49160 | tf_op jit(solution)/shard_map/ppermute | solution.py:590
  78.8 1.7 %collective-permute-done.10.refs_2_.refs_6_ = f32[32,128]{1,0:T(8,128)S(1)} collective-permute-done((f32[32,128]{1,0:T(8,128)S(1)}, f32[32,128]{1,0:T(8,128)S(1)}, u32[]{:S(2)}, u32[]{:S(2)}) %collective-permute-start.10) | collective-permute-done | bytes 16416 | tf_op jit(solution)/shard_map/ppermute | solution.py:590
  80.5 1.9 %collective-permute-done.11.refs_3_.refs_7_ = f32[32,128]{1,0:T(8,128)S(1)} collective-permute-done((f32[32,128]{1,0:T(8,128)S(1)}, f32[32,128]{1,0:T(8,128)S(1)}, u32[]{:S(2)}, u32[]{:S(2)}) %collective-permute-start.11) | collective-permute-done | bytes 16416 | tf_op jit(solution)/shard_map/ppermute | solution.py:590
  82.4 1.9 %collective-permute-start.12 = (f32[7,8,256]{2,1,0:T(8,128)S(1)}, f32[7,8,256]{2,1,0:T(8,128)S(1)}, u32[]{:S(2)}, u32[]{:S(2)}) collective-permute-start(f32[7,8,256]{2,1,0:T(8,128)S(1)} %get-tuple-element.43), channel_id=1, source_target_pairs={{0,4},{4,8},{8,12},{1,5},{5,9},{9,13},{2,6},{6,10},{10,14},{3,7},{... | collective-permute-start | bytes 172040 | tf_op jit(solution)/shard_map/ppermute | solution.py:590
  84.3 5.0 %collective-permute-start.13 = (f32[7,8,256]{2,1,0:T(8,128)S(1)}, f32[7,8,256]{2,1,0:T(8,128)S(1)}, u32[]{:S(2)}, u32[]{:S(2)}) collective-permute-start(f32[7,8,256]{2,1,0:T(8,128)S(1)} %get-tuple-element.44), channel_id=1, source_target_pairs={{4,0},{8,4},{12,8},{5,1},{9,5},{13,9},{6,2},{10,6},{14,10},{7,3},{... | collective-permute-start | bytes 172040 | tf_op jit(solution)/shard_map/ppermute | solution.py:590
  89.3 0.0 collective-permute-done.3.refs_8_
  89.3 0.0 collective-permute-done.4.refs_9_
  89.3 25.5 %shard_map.112 = (f32[32,32,256]{2,1,0:T(8,128)S(1)}, f32[40,384]{1,0:T(8,128)S(1)}, f32[256,320]{1,0:T(8,128)S(1)}) custom-call(s32[1]{0:T(128)} %bitcast.refs_0_, f32[1,32,32,256]{3,2,1,0:T(8,128)S(1)} %copy-done.1, f32[1,4,4,32,256]{4,3,2,1,0:T(8,128)S(1)} %copy-done.3, f32[28,32,256]{2,1,0:T(8,128)S(1)} %collective-permute-done.refs_3_.refs_2_, ...), custom_call_target="tpu_custom_call" | custom-call | bytes 4555780 | tf_op jit(solution)/shard_map/pallas_call | solution.py:152
  114.9 0.0 collective-permute-done.13.refs_9_
  114.9 1.1 shard_map.120
  (22 shorter events, 0.1 us)
Async XLA Ops:
  0.0 0.8 copy-start.8
  0.0 0.8 copy-start.13
  0.8 1.2 %copy-start = (f32[1,32,32,256]{3,2,1,0:T(8,128)S(1)}, f32[1,32,32,256]{3,2,1,0:T(8,128)}, u32[]{:S(2)}) copy-start(f32[1,32,32,256]{3,2,1,0:T(8,128)} %refs_1_.5) | copy-start | bytes 3145732
  2.0 1.0 copy-start.2
  3.1 0.8 copy-start.4
  3.8 0.8 copy-start.6
  4.6 5.6 %copy-start.3 = (f32[1,4,4,32,256]{4,3,2,1,0:T(8,128)S(1)}, f32[1,4,4,32,256]{4,3,2,1,0:T(8,128)}, u32[]{:S(2)}) copy-start(f32[1,4,4,32,256]{4,3,2,1,0:T(8,128)} %refs_3_.1) | copy-start | bytes 1572868
  4.6 5.6 %copy-start.5 = (s32[32,256]{1,0:T(8,128)S(1)}, s32[32,256]{1,0:T(8,128)}, u32[]{:S(2)}) copy-start(s32[32,256]{1,0:T(8,128)} %refs_5_.8) | copy-start | bytes 98308
  4.6 5.6 %copy-start.7 = (f32[1,32,256]{2,1,0:T(8,128)S(1)}, f32[1,32,256]{2,1,0:T(8,128)}, u32[]{:S(2)}) copy-start(f32[1,32,256]{2,1,0:T(8,128)} %refs_4_.7) | copy-start | bytes 98308
  7.6 2.5 %collective-permute-start = (f32[28,32,256]{2,1,0:T(8,128)S(1)}, f32[28,32,256]{2,1,0:T(8,128)S(1)}, u32[]{:S(2)}, u32[]{:S(2)}) collective-permute-start(f32[28,32,256]{2,1,0:T(8,128)S(1)} %get-tuple-element.25), channel_id=1, source_target_pairs={{0,16},{16,0},{1,17},{17,1},{2,18},{18,2},{3,19},{19,3},{4,20},{20... | collective-permute-start | bytes 2752520 | tf_op jit(solution)/shard_map/ppermute | solution.py:643
  10.8 3.8 %collective-permute-start.5 = (f32[32,128]{1,0:T(8,128)S(1)}, f32[32,128]{1,0:T(8,128)S(1)}, u32[]{:S(2)}, u32[]{:S(2)}) collective-permute-start(f32[32,128]{1,0:T(8,128)S(1)} %get-tuple-element.36), channel_id=1, source_target_pairs={{0,1},{1,2},{2,3},{3,0},{4,5},{5,6},{6,7},{7,4},{8,9},{9,10},{10,1... | collective-permute-start | bytes 49160 | tf_op jit(solution)/shard_map/ppermute | solution.py:590
  11.1 5.5 %collective-permute-start.6 = (f32[32,128]{1,0:T(8,128)S(1)}, f32[32,128]{1,0:T(8,128)S(1)}, u32[]{:S(2)}, u32[]{:S(2)}) collective-permute-start(f32[32,128]{1,0:T(8,128)S(1)} %get-tuple-element.37), channel_id=1, source_target_pairs={{0,3},{1,0},{2,1},{3,2},{4,7},{5,4},{6,5},{7,6},{8,11},{9,8},{10,9... | collective-permute-start | bytes 49160 | tf_op jit(solution)/shard_map/ppermute | solution.py:590
  16.6 7.0 %copy-start.12 = (s32[2048]{0:T(1024)S(1)}, s32[2048]{0:T(1024)}, u32[]{:S(2)}) copy-start(s32[2048]{0:T(1024)} %param.21) | copy-start | bytes 24580
  16.6 12.7 %copy-start.9 = (f32[1,128,128]{2,1,0:T(8,128)S(1)}, f32[1,128,128]{2,1,0:T(8,128)}, u32[]{:S(2)}) copy-start(f32[1,128,128]{2,1,0:T(8,128)} %refs_5_.9) | copy-start | bytes 196612
  16.7 12.7 %collective-permute-start.7 = (f32[12,8,256]{2,1,0:T(8,128)S(1)}, f32[12,8,256]{2,1,0:T(8,128)S(1)}, u32[]{:S(2)}, u32[]{:S(2)}) collective-permute-start(f32[12,8,256]{2,1,0:T(8,128)S(1)} %get-tuple-element.38), channel_id=1, source_target_pairs={{0,4},{4,8},{8,12},{1,5},{5,9},{9,13},{2,6},{6,10},{10,14},{3,7},{... | collective-permute-start | bytes 294920 | tf_op jit(solution)/shard_map/ppermute | solution.py:590
  20.2 9.1 %collective-permute-start.8 = (f32[12,8,256]{2,1,0:T(8,128)S(1)}, f32[12,8,256]{2,1,0:T(8,128)S(1)}, u32[]{:S(2)}, u32[]{:S(2)}) collective-permute-start(f32[12,8,256]{2,1,0:T(8,128)S(1)} %get-tuple-element.39), channel_id=1, source_target_pairs={{4,0},{8,4},{12,8},{5,1},{9,5},{13,9},{6,2},{10,6},{14,10},{7,3},{... | collective-permute-start | bytes 294920 | tf_op jit(solution)/shard_map/ppermute | solution.py:590
  23.6 0.7 copy-start.11
  23.6 0.7 copy-start.10
  58.5 1.6 %copy-start.1 = (f32[1,32,32,256]{3,2,1,0:T(8,128)S(1)}, f32[1,32,32,256]{3,2,1,0:T(8,128)}, u32[]{:S(2)}) copy-start(f32[1,32,32,256]{3,2,1,0:T(8,128)} %refs_1_.5) | copy-start | bytes 3145732
  58.8 17.7 %collective-permute-start.9 = (f32[8,32,256]{2,1,0:T(8,128)S(1)}, f32[8,32,256]{2,1,0:T(8,128)S(1)}, u32[]{:S(2)}, u32[]{:S(2)}) collective-permute-start(f32[8,32,256]{2,1,0:T(8,128)S(1)} %shard_map.117.refs_0_.refs_4_), channel_id=1, source_target_pairs={{0,16},{1,17},{2,18},{3,19},{4,20},{5,21},{6,22},{7,23},{8,24},{9,... | collective-permute-start | bytes 786440 | tf_op jit(solution)/shard_map/ppermute | solution.py:712
  60.7 4.9 %collective-permute-start.1 = (f32[32,256]{1,0:T(8,128)S(1)}, f32[32,256]{1,0:T(8,128)S(1)}, u32[]{:S(2)}, u32[]{:S(2)}) collective-permute-start(f32[32,256]{1,0:T(8,128)S(1)} %get-tuple-element.26), channel_id=1, source_target_pairs={{0,1},{1,2},{2,3},{3,0},{4,5},{5,6},{6,7},{7,4},{8,9},{9,10},{10,1... | collective-permute-start | bytes 98312 | tf_op jit(solution)/shard_map/ppermute | solution.py:590
  64.0 5.7 %collective-permute-start.2 = (f32[32,256]{1,0:T(8,128)S(1)}, f32[32,256]{1,0:T(8,128)S(1)}, u32[]{:S(2)}, u32[]{:S(2)}) collective-permute-start(f32[32,256]{1,0:T(8,128)S(1)} %get-tuple-element.27), channel_id=1, source_target_pairs={{0,3},{1,0},{2,1},{3,2},{4,7},{5,4},{6,5},{7,6},{8,11},{9,8},{10,9... | collective-permute-start | bytes 98312 | tf_op jit(solution)/shard_map/ppermute | solution.py:590
  69.8 19.6 %collective-permute-start.3 = (f32[30,8,256]{2,1,0:T(8,128)S(1)}, f32[30,8,256]{2,1,0:T(8,128)S(1)}, u32[]{:S(2)}, u32[]{:S(2)}) collective-permute-start(f32[30,8,256]{2,1,0:T(8,128)S(1)} %get-tuple-element.28), channel_id=1, source_target_pairs={{0,4},{4,8},{8,12},{1,5},{5,9},{9,13},{2,6},{6,10},{10,14},{3,7},{... | collective-permute-start | bytes 737288 | tf_op jit(solution)/shard_map/ppermute | solution.py:590
  72.2 17.1 %collective-permute-start.4 = (f32[30,8,256]{2,1,0:T(8,128)S(1)}, f32[30,8,256]{2,1,0:T(8,128)S(1)}, u32[]{:S(2)}, u32[]{:S(2)}) collective-permute-start(f32[30,8,256]{2,1,0:T(8,128)S(1)} %get-tuple-element.29), channel_id=1, source_target_pairs={{4,0},{8,4},{12,8},{5,1},{9,5},{13,9},{6,2},{10,6},{14,10},{7,3},{... | collective-permute-start | bytes 737288 | tf_op jit(solution)/shard_map/ppermute | solution.py:590
  76.7 3.8 %collective-permute-start.10 = (f32[32,128]{1,0:T(8,128)S(1)}, f32[32,128]{1,0:T(8,128)S(1)}, u32[]{:S(2)}, u32[]{:S(2)}) collective-permute-start(f32[32,128]{1,0:T(8,128)S(1)} %get-tuple-element.41), channel_id=1, source_target_pairs={{0,1},{1,2},{2,3},{3,0},{4,5},{5,6},{6,7},{7,4},{8,9},{9,10},{10,1... | collective-permute-start | bytes 49160 | tf_op jit(solution)/shard_map/ppermute | solution.py:590
  76.8 5.6 %collective-permute-start.11 = (f32[32,128]{1,0:T(8,128)S(1)}, f32[32,128]{1,0:T(8,128)S(1)}, u32[]{:S(2)}, u32[]{:S(2)}) collective-permute-start(f32[32,128]{1,0:T(8,128)S(1)} %get-tuple-element.42), channel_id=1, source_target_pairs={{0,3},{1,0},{2,1},{3,2},{4,7},{5,4},{6,5},{7,6},{8,11},{9,8},{10,9... | collective-permute-start | bytes 49160 | tf_op jit(solution)/shard_map/ppermute | solution.py:590
  82.4 32.5 %collective-permute-start.12 = (f32[7,8,256]{2,1,0:T(8,128)S(1)}, f32[7,8,256]{2,1,0:T(8,128)S(1)}, u32[]{:S(2)}, u32[]{:S(2)}) collective-permute-start(f32[7,8,256]{2,1,0:T(8,128)S(1)} %get-tuple-element.43), channel_id=1, source_target_pairs={{0,4},{4,8},{8,12},{1,5},{5,9},{9,13},{2,6},{6,10},{10,14},{3,7},{... | collective-permute-start | bytes 172040 | tf_op jit(solution)/shard_map/ppermute | solution.py:590
  84.3 30.6 %collective-permute-start.13 = (f32[7,8,256]{2,1,0:T(8,128)S(1)}, f32[7,8,256]{2,1,0:T(8,128)S(1)}, u32[]{:S(2)}, u32[]{:S(2)}) collective-permute-start(f32[7,8,256]{2,1,0:T(8,128)S(1)} %get-tuple-element.44), channel_id=1, source_target_pairs={{4,0},{8,4},{12,8},{5,1},{9,5},{13,9},{6,2},{10,6},{14,10},{7,3},{... | collective-permute-start | bytes 172040 | tf_op jit(solution)/shard_map/ppermute | solution.py:590
where the time goes:
time: 117 us; the launch traced here: 116 us
  Pallas kernels  37.9 us (32%)
  starting transfers between devices  29.3 us (25%)
  blocking collectives  27.7 us (24%)
  waiting for transfers between devices  15.5 us (13%)
  local copies, waits for them, and re-layouts  5.28 us (5%)
    pallas_call x12, Pallas kernels, call(): pl.pallas_call(kernel, out_shape=outs, in_specs=[pl.BlockSpec(memory_spac...  37.9 us
    ppermute x12, starting transfers between devices, shifted(): return lax.ppermute(x, axis, pairs)  28 us
    all_to_all x1, blocking collectives, body(): lax.all_to_all(packed.reshape(tiles, cap, -1), ('gy', 'gx'), split_axis=0...  27.7 us
    ppermute x12, waiting for transfers between devices, shifted(): return lax.ppermute(x, axis, pairs)  13 us
    unnamed x29, local copies, waits for them, and re-layouts  5.28 us
    ppermute x1, waiting for transfers between devices, body(): got = lax.ppermute(send, 'sect', [(0, 1), (1, 0)])  2.45 us
  transfers between devices with their start and end apart: 14, of which 7 were waited for; matrix products, arithmetic and copies ran while one was open for 0% of the time, Pallas kernels for 27%

commit v1 on v0

--- a/solution.py
+++ b/solution.py
@@ -11,6 +11,9 @@
 SUB = 8
 F32 = jnp.float32
 BF16 = jnp.bfloat16
+
+
+LAST = (((1,), (1,)), ((), ()))
 
 
 def full_dot(a, b, dims=(((1,), (0,)), ((), ()))):
@@ -112,24 +115,23 @@
     return jnp.concatenate([jnp.concatenate([main, bottom], axis=0), side], axis=1)
 
 
-def sides_with_rows(west_ref, east_ref, north_ref, south_ref, first, blocks, tx):
+def sides_with_rows(west_ref, east_ref, north_ref, south_ref, first, start, blocks, tx):
     west, east = [], []
     per = tx // LANES
     for block in range(blocks):
-        lanes = pl.ds((block % per) * LANES, LANES)
         out = []
         for which, ref in enumerate((west_ref, east_ref)):
             f, at = divmod(which * blocks + block, per)
             f = first + f
             cols = pl.ds(at * LANES, LANES)
             tile = edge_tile(north_ref[f // 2, :, cols], south_ref[f // 2, :, cols], f % 2)
-            out.append(jnp.concatenate([ref[:, pl.ds(block * LANES, LANES)], tile], axis=0))
+            out.append(jnp.concatenate([ref[:, pl.ds((start + block) * LANES, LANES)], tile], axis=0))
         west.append(out[0])
         east.append(out[1])
     return west, east
 
 
-def packed_reader(west_ref, east_ref, blocks, tx):
+def packed_reader(west_ref, east_ref, start, blocks, tx):
     per = tx // LANES
 
     def read(f, row_tile):
@@ -138,7 +140,7 @@
             which, block = divmod(f * per + at, blocks)
             rows = pl.ds(row_tile * SUB, SUB)
             if which < 2:
-                pieces.append((west_ref, east_ref)[which][rows, pl.ds(block * LANES, LANES)])
+                pieces.append((west_ref, east_ref)[which][rows, pl.ds((start + block) * LANES, LANES)])
             else:
                 pieces.append(jnp.zeros((SUB, LANES), F32))
         return jnp.concatenate(pieces, axis=1)
@@ -146,8 +148,8 @@
     return read, -(-2 * blocks // per)
 
 
-def call(kernel, outs, *args, smem=(), scratch=(), flops=0):
-    space = lambda i: pltpu.SMEM if i in smem else pltpu.VMEM
+def call(kernel, outs, *args, smem=(), hbm=(), scratch=(), flops=0, vmem=48):
+    space = lambda i: pltpu.SMEM if i in smem else pltpu.HBM if i in hbm else pltpu.VMEM
     nbytes = sum(math.prod(a.shape) * 4 for a in (*args, *outs))
     return pl.pallas_call(
         kernel,
@@ -155,20 +157,38 @@
         in_specs=[pl.BlockSpec(memory_space=space(i)) for i in range(len(args))],
         out_specs=[pl.BlockSpec(memory_space=pltpu.VMEM) for _ in outs],
         scratch_shapes=scratch,
-        compiler_params=pltpu.CompilerParams(vmem_limit_bytes=48 * 2**20),
+        compiler_params=pltpu.CompilerParams(vmem_limit_bytes=vmem * 2**20),
         cost_estimate=pl.CostEstimate(flops=flops, bytes_accessed=nbytes, transcendentals=0),
     )(*args)
 
 
-def tile_of(ref, g, l):
-    block = ref[:, g * SUB : (g + 1) * SUB, l * LANES : (l + 1) * LANES]
-    return block.reshape(-1, LANES)
-
-
-def project_kernel(adj_ref, mask_ref, mix_ref, ext_ref, coup_ref, hist_ref, diff_ref, keep_ref, send_ref):
-    _, nc, ty, tx = adj_ref.shape
-    _, steps, fields = hist_ref.shape[:3]
+def stacked_rows(parts):
+    high, low = halves(parts)
+    return jnp.concatenate([high, high, low], axis=1)
+
+
+def stacked_columns(parts):
+    high, low = halves(parts)
+    return jnp.concatenate([high, low, high], axis=0)
+
+
+def project_kernel(
+    adj_hbm, mask_hbm, diff_hbm, hist_hbm, mix_ref, ext_ref, coup_ref, keep_ref, send_ref, adj_ref, mask_ref, sems
+):
+    _, nc, ty, tx = adj_hbm.shape
+    _, steps, fields = hist_hbm.shape[:3]
     hf = fields // 2
+    count = (steps + 1) * hf
+    copies = [
+        pltpu.make_async_copy(mask_hbm, mask_ref, sems.at[0]),
+        pltpu.make_async_copy(adj_hbm.at[0], adj_ref, sems.at[1]),
+        pltpu.make_async_copy(diff_hbm.at[0], send_ref.at[count + 1], sems.at[2]),
+    ]
+    for k in range(steps):
+        to = send_ref.at[pl.ds(count + 2 + k * fields, fields)]
+        copies.append(pltpu.make_async_copy(hist_hbm.at[0, k], to, sems.at[3 + k]))
+    for copy in copies:
+        copy.start()
     mix = mix_ref[0]
     rows = ext_ref[...]
     lows, highs = [], []
@@ -177,27 +197,25 @@
         lows.append(big[: hf * SUB])
         highs.append(big[hf * SUB :])
         if m < steps:
-            force = grown(full_dot(rows, coup_ref[0]))
+            force = grown(full_dot(rows, coup_ref[0], LAST))
             height, width = hf * SUB, force.shape[1]
             for ref, at in ((keep_ref, 0), (send_ref, height)):
                 per = ty // height
                 r0, c0 = (m % per) * height, (m // per) * LANES
-                ref[(steps + 1) * hf, r0 : r0 + height, c0 : c0 + width] = force[at : at + height]
-            rows = rows + full_dot(rows, mix, (((1,), (1,)), ((), ())))
+                ref[count, r0 : r0 + height, c0 : c0 + width] = force[at : at + height]
+            rows = rows + full_dot(rows, mix, LAST)
     big = halves(jnp.concatenate(lows + highs, axis=0))
-    count = (steps + 1) * hf
+    copies[0].wait()
+    copies[1].wait()
     for g in range(ty // SUB):
-        for l in range(tx // LANES):
-            rs, cs = slice(g * SUB, (g + 1) * SUB), slice(l * LANES, (l + 1) * LANES)
-            wet = mask_ref[rs, cs].astype(F32)
-            u = (adj_ref[0, :, rs, cs] * wet[None]).reshape(nc * SUB, LANES)
-            t = dot3(big, halves(u)).reshape(2 * count, SUB, LANES)
-            keep_ref[:count, rs, cs] = t[:count]
-            send_ref[:count, rs, cs] = t[count:]
-    send_ref[count + 1] = diff_ref[0]
-    for k in range(steps):
-        for q in range(fields):
-            send_ref[count + 2 + k * fields + q] = hist_ref[0, k, q]
+        rs = slice(g * SUB, (g + 1) * SUB)
+        wet = mask_ref[rs, :].astype(F32)
+        u = (adj_ref[:, rs, :] * wet[None]).reshape(nc * SUB, tx)
+        t = dot3(big, halves(u)).reshape(2 * count, SUB, tx)
+        keep_ref[:count, rs, :] = t[:count]
+        send_ref[:count, rs, :] = t[count:]
+    for copy in copies[2:]:
+        copy.wait()
 
 
 def field_places(steps, hf):
@@ -214,7 +232,7 @@
 
 
 def force_kernel(
-    places, halo_count, flag_ref, keep_ref, got_ref, hist_ref, diff_ref, mask_ref, main_ref, east_ref, west_ref
+    places, halo_count, flag_ref, keep_ref, got_ref, adj_ref, hist_ref, diff_ref, mask_ref, main_ref, east_ref, west_ref
 ):
     _, steps, fields, ty, tx = hist_ref.shape
     hf, hw = fields // 2, steps
@@ -233,31 +251,32 @@
         r0, c0 = (m % per) * height, (m // per) * LANES
         at = (count, slice(r0, r0 + height), slice(c0, c0 + width))
         big.append(pick(keep_ref[at], got_ref[at]))
-    big = halves(jnp.concatenate(big, axis=0))
+    big = stacked_rows(jnp.concatenate(big, axis=0))
     for g in range(ty // SUB):
-        for l in range(tx // LANES):
-            rs, cs = slice(g * SUB, (g + 1) * SUB), slice(l * LANES, (l + 1) * LANES)
-            for n in range(steps):
-                k = steps - 1 - n
-                own = hist_ref[0, k, :, rs, cs]
-                far = got_ref[count + 2 + k * fields : count + 2 + (k + 1) * fields, rs, cs]
-                h = jnp.concatenate([pick(own, far), pick(far, own)], axis=0).reshape(-1, LANES)
-                top = (steps - n) * height
-                out = dot3((big[0][:top], big[1][:top]), halves(h))
-                for m in range(steps - n):
-                    for q in range(hf):
-                        at = (m * hf + q) * SUB
-                        main_ref[places["g", n, m, q], rs, cs] = out[at : at + SUB]
+        rs = slice(g * SUB, (g + 1) * SUB)
+        for n in range(steps):
+            k = steps - 1 - n
+            own = hist_ref[0, k, :, rs, :]
+            far = got_ref[count + 2 + k * fields : count + 2 + (k + 1) * fields, rs, :]
+            h = jnp.concatenate([pick(own, far), pick(far, own)], axis=0).reshape(-1, tx)
+            out = bf_dot(big[: (steps - n) * height], stacked_columns(h))
+            for m in range(steps - n):
+                for q in range(hf):
+                    at = (m * hf + q) * SUB
+                    main_ref[places["g", n, m, q], rs, :] = out[at : at + SUB]
     read = lambda f, l: main_ref[f, :, l * LANES : (l + 1) * LANES]
     east, west = pack_columns(read, halo_count, ty, tx, hw)
-    for block, (e, w) in enumerate(zip(east, west)):
+    state, total = state_reader(adj_ref, hist_ref, got_ref, count + 2, diff_ref, own_wet(flag_ref, mask_ref))
+    read = lambda f, l: state(f, slice(0, ty), slice(l * LANES, (l + 1) * LANES))
+    more = pack_columns(read, total, ty, tx, hw)
+    for block, (e, w) in enumerate(zip(east + more[0], west + more[1])):
         east_ref[:, block * LANES : (block + 1) * LANES] = e
         west_ref[:, block * LANES : (block + 1) * LANES] = w
 
 
 def rows_kernel(halo_count, blocks, main_ref, west_ref, east_ref, north_ref, south_ref):
     _, ty, tx = main_ref.shape
-    packed, more = packed_reader(west_ref, east_ref, blocks, tx)
+    packed, more = packed_reader(west_ref, east_ref, 0, blocks, tx)
 
     def read(f, t):
         return main_ref[f, t * SUB : (t + 1) * SUB, :] if f < halo_count else packed(f - halo_count, t)
@@ -265,38 +284,47 @@
     send_rows(read, halo_count + more, ty, north_ref, south_ref)
 
 
-def index_kernel(cap, slots, nb, pos_ref, dest_ref, src_ref, dst_ref, sel_ref, acc_ref):
+def block_place(slots, nb):
+    return lambda b: (b % nb) * (slots // nb) + b // nb
+
+
+def onehot(size, values):
+    ids = lax.broadcasted_iota(jnp.int32, (size, values.shape[1]), 0)
+    return (ids == values).astype(F32).astype(BF16)
+
+
+def earlier(entries):
+    row = lax.broadcasted_iota(jnp.int32, (entries, entries), 0)
+    return row < lax.broadcasted_iota(jnp.int32, (entries, entries), 1)
+
+
+def select_kernel(cap, slots, nb, pos_ref, dest_ref, src_ref, sel_ref):
     tiles, entries = dest_ref.shape
     tile = pos_ref[0]
-    count = tiles * cap
-    per_row = slots // nb
-    place = lambda b: (b % nb) * per_row + b // nb
-    row = lax.broadcasted_iota(jnp.int32, (entries, entries), 0)
-    col = lax.broadcasted_iota(jnp.int32, (entries, entries), 1)
     dest = dest_ref[pl.ds(tile, 1), :]
     across = jnp.broadcast_to(dest.astype(F32), (entries, entries))
-    same = (across == across.T) & (row < col)
+    same = (across == across.T) & earlier(entries)
     rank = jnp.sum(same.astype(F32), axis=0, keepdims=True).astype(jnp.int32)
-    slot = dest * cap + rank
-    last = (((1,), (1,)), ((), ()))
-
-    def onehot(size, values):
-        ids = lax.broadcasted_iota(jnp.int32, (size, entries), 0)
-        return (ids == values).astype(F32).astype(BF16)
-
-    sel_ref[...] = bf_dot(onehot(count, slot), onehot(slots, place(src_ref[pl.ds(tile, 1), :])), last)
+    source = block_place(slots, nb)(src_ref[pl.ds(tile, 1), :])
+    sel_ref[...] = bf_dot(onehot(tiles * cap, dest * cap + rank), onehot(slots, source), LAST)
+
+
+def arrival_kernel(cap, slots, nb, pos_ref, dest_ref, dst_ref, acc_ref):
+    tiles, entries = dest_ref.shape
+    tile = pos_ref[0]
     acc_ref[...] = jnp.zeros_like(acc_ref)
-    before = (row < col).astype(F32).astype(BF16)
+    before = earlier(entries).astype(F32).astype(BF16)
 
     def source(i, carry):
         mine = dest_ref[pl.ds(i, 1), :] == tile
         mine_f = jnp.broadcast_to(mine.astype(F32), (SUB, entries)).astype(BF16)
         ranks = bf_dot(mine_f, before)[:1].astype(jnp.int32)
         spot = jnp.where(mine, i * cap + ranks, -1)
-        acc_ref[...] += bf_dot(onehot(slots, place(dst_ref[pl.ds(i, 1), :])), onehot(count, spot), last)
+        place = block_place(slots, nb)(dst_ref[pl.ds(i, 1), :])
+        acc_ref[...] += bf_dot(onehot(slots, place), onehot(tiles * cap, spot), LAST)
         return carry
 
-    lax.fori_loop(0, tiles, source, 0)
+    lax.fori_loop(0, tiles, source, 0, unroll=4)
 
 
 def surface_kernel(
@@ -306,7 +334,7 @@
     hw = steps
     per = LANES // hw
     blocks = -(-halo_count // per)
-    wests, easts = sides_with_rows(west_ref, east_ref, north_ref, south_ref, halo_count, blocks, tx)
+    wests, easts = sides_with_rows(west_ref, east_ref, north_ref, south_ref, halo_count, 0, blocks, tx)
 
     def ext(key):
         f = places[key]
@@ -371,23 +399,12 @@
     return lambda rows, cols: jnp.where(ocean, mask_ref[rows, cols].astype(F32), 1.0)
 
 
-def state_columns_kernel(far_at, flag_ref, adj_ref, hist_ref, far_ref, diff_ref, mask_ref, east_ref, west_ref):
-    ty, tx = mask_ref.shape
-    hw = hist_ref.shape[1]
-    read, total = state_reader(adj_ref, hist_ref, far_ref, far_at, diff_ref, own_wet(flag_ref, mask_ref))
-    at = lambda f, l: read(f, slice(0, ty), slice(l * LANES, (l + 1) * LANES))
-    east, west = pack_columns(at, total, ty, tx, hw)
-    for block, (e, w) in enumerate(zip(east, west)):
-        east_ref[:, block * LANES : (block + 1) * LANES] = e
-        west_ref[:, block * LANES : (block + 1) * LANES] = w
-
-
 def state_rows_kernel(
-    far_at, blocks, flag_ref, adj_ref, hist_ref, far_ref, diff_ref, mask_ref, west_ref, east_ref, north_ref, south_ref
+    far_at, start, blocks, flag_ref, adj_ref, hist_ref, far_ref, diff_ref, mask_ref, west_ref, east_ref, north_ref, south_ref
 ):
     ty, tx = mask_ref.shape
     read, total = state_reader(adj_ref, hist_ref, far_ref, far_at, diff_ref, own_wet(flag_ref, mask_ref))
-    packed, more = packed_reader(west_ref, east_ref, blocks, tx)
+    packed, more = packed_reader(west_ref, east_ref, start, blocks, tx)
 
     def at(f, t):
         rows = slice(t * SUB, (t + 1) * SUB)
@@ -398,6 +415,7 @@
 
 def state_kernel(
     far_at,
+    start,
     blocks,
     flag_ref,
     adj_ref,
@@ -425,7 +443,7 @@
     per = LANES // hw
     ocean = flag_ref[0] == 0
     read, total = state_reader(adj_ref, hist_ref, far_ref, far_at, diff_ref, own_wet(flag_ref, mask_ref))
-    wests, easts = sides_with_rows(west_ref, east_ref, north_ref, south_ref, total, blocks, tx)
+    wests, easts = sides_with_rows(west_ref, east_ref, north_ref, south_ref, total, start, blocks, tx)
 
     def ext(f):
         main = read(f, slice(0, ty), slice(0, tx))
@@ -445,7 +463,7 @@
     ring_ref[...] = diff
     ident = lax.broadcasted_iota(jnp.int32, (nc, nc), 0) == lax.broadcasted_iota(jnp.int32, (nc, nc), 1)
     step_m = mix_ref[0].T + ident.astype(F32)
-    coup = coup_ref[0]
+    coup = coup_ref[0].T
     late = coup[:, fields:]
     powers = []
     for i in range(steps):
@@ -461,7 +479,13 @@
         at += fields * SUB
     first = lax.broadcasted_iota(jnp.int32, coup.shape, 1) < fields
     coup = jnp.where(jnp.logical_or(first, ocean), coup, 0.0)
-    mix8, coup8 = halves(grown(step_m)), halves(grown(coup))
+    mix8, coup8 = halves(grown(step_m)), stacked_rows(grown(coup))
+    groups = ty // SUB
+    main = [((g, 0, tx),) for g in range(groups)]
+    halo = [((groups, 0, tx),)] + [
+        tuple((g, tx, LANES) for g in range(at, min(at + tx // LANES, groups + 1)))
+        for at in range(0, groups + 1, tx // LANES)
+    ]
 
     for n in range(steps):
         k = steps - 1 - n
@@ -473,18 +497,20 @@
             spread[c] = ring_lap(diff * u)
             return carry
 
-        lax.fori_loop(0, nc, one, 0)
-        for g in range(ty // SUB + (not small)):
-            for l in range(tx // LANES + (not small)):
-                rs, cs = slice(g * SUB, (g + 1) * SUB), slice(l * LANES, (l + 1) * LANES)
-                u = state[:, rs, cs].reshape(nc * SUB, LANES)
-                h = force[k, :, rs, cs].reshape(2 * fields * SUB, LANES)
-                new = dot3(mix8, halves(u)) + dot3(coup8, halves(h))
-                new = new.reshape(nc, SUB, LANES) + spread[:, rs, cs]
+        lax.fori_loop(0, nc, one, 0, unroll=8)
+        for places in main if small else main + halo:
+            spots = [(slice(g * SUB, (g + 1) * SUB), slice(c, c + w)) for g, c, w in places]
+            u = jnp.concatenate([state[:, rs, cs].reshape(nc * SUB, -1) for rs, cs in spots], axis=1)
+            h = jnp.concatenate([force[k, :, rs, cs].reshape(2 * fields * SUB, -1) for rs, cs in spots], axis=1)
+            new = dot3(mix8, halves(u)) + bf_dot(coup8, stacked_columns(h))
+            at = 0
+            for (rs, cs), (_, _, w) in zip(spots, places):
+                value = new[:, at : at + w].reshape(nc, SUB, w) + spread[:, rs, cs]
+                at += w
                 if small:
-                    out_ref[:, rs, cs] = new
+                    out_ref[:, rs, cs] = value
                 else:
-                    state[:, rs, cs] = new
+                    state[:, rs, cs] = value
 
 
 def late_fields(steps, fields):
@@ -518,7 +544,7 @@
     count, ty, tx = own_ref.shape
     hf = count // steps
     todo = late_fields(steps, 2 * hf)
-    packed, more = packed_reader(west_ref, east_ref, blocks, tx)
+    packed, more = packed_reader(west_ref, east_ref, 0, blocks, tx)
 
     def read(f, t):
         if f >= len(todo):
@@ -561,7 +587,7 @@
     @pl.when(flag_ref[0] != 0)
     def _():
         diff = ring_ref[...]
-        wests, easts = sides_with_rows(west_ref, east_ref, north_ref, south_ref, len(todo), blocks, tx)
+        wests, easts = sides_with_rows(west_ref, east_ref, north_ref, south_ref, len(todo), 0, blocks, tx)
         at = 0
         for n in range(steps):
             k = steps - 1 - n
@@ -635,18 +661,30 @@
         return shifted(x_after, axis, 1, wrap, only), shifted(x_before, axis, -1, wrap, only)
 
     count = (steps + 1) * hf
+    coupling = jnp.swapaxes(coupling, 1, 2)
     keep, send = call(
         project_kernel,
         [struct(count + 1, ty, tx), struct(count + 2 + steps * fields, ty, tx)],
-        adjoint_init, land_mask, mixing, extract, coupling, history, diffusivity,
+        adjoint_init, land_mask, diffusivity, history, mixing, extract, coupling,
+        hbm=(0, 1, 2, 3),
+        vmem=60,
+        scratch=[
+            pltpu.VMEM((nc, ty, tx), F32),
+            pltpu.VMEM((ty, tx), jnp.int32),
+            pltpu.SemaphoreType.DMA((3 + steps,)),
+        ],
     )
     got = lax.ppermute(send, "sect", [(0, 1), (1, 0)])
     places, halo_count = field_places(steps, hf)
     blocks = -(-halo_count // per)
+    far_at = count + 2
+    total = nc + 2 * (steps - 1) * fields + 2
+    state_blocks = -(-total // per)
+    side = struct(ty, (blocks + state_blocks) * LANES)
     main, east, west = call(
         partial(force_kernel, places, halo_count),
-        [struct(len(places), ty, tx), struct(ty, blocks * LANES), struct(ty, blocks * LANES)],
-        flag, keep, got, history, diffusivity, land_mask,
+        [struct(len(places), ty, tx), side, side],
+        flag, keep, got, adjoint_init, history, diffusivity, land_mask,
         smem=(0,),
     )
     from_west, from_east = exchange(east, west, "gx", True)
@@ -657,13 +695,11 @@
         main, from_west, from_east,
     )
     from_north, from_south = exchange(south, north, "gy", False)
-    sel, acc = call(
-        partial(index_kernel, cap, slots, nb),
-        [struct(tiles * cap, slots), struct(slots, tiles * cap)],
-        tile.reshape(1),
-        atmos_tile_index.reshape(tiles, entries),
-        ocean_block_index.reshape(tiles, entries),
-        atmos_block_index.reshape(tiles, entries),
+    dest = atmos_tile_index.reshape(tiles, entries)
+    [sel] = call(
+        partial(select_kernel, cap, slots, nb),
+        [struct(tiles * cap, slots)],
+        tile.reshape(1), dest, ocean_block_index.reshape(tiles, entries),
         smem=(0,),
     )
     [packed] = call(
@@ -671,23 +707,14 @@
         [struct(tiles * cap, steps * hf * LANES)],
         main, from_west, from_east, from_north, from_south, regrid, sel,
     )
+    packed, adjoint_init, dest = lax.optimization_barrier((packed, adjoint_init, dest))
     arrived = lax.all_to_all(
         packed.reshape(tiles, cap, -1), ("gy", "gx"), split_axis=0, concat_axis=0, tiled=True
     ).reshape(tiles * cap, -1)
 
-    far_at = count + 2
-    total = nc + 2 * (steps - 1) * fields + 2
-    blocks = -(-total // per)
-    east, west = call(
-        partial(state_columns_kernel, far_at),
-        [struct(ty, blocks * LANES)] * 2,
-        flag, adjoint_init, history, got, diffusivity, land_mask,
-        smem=(0,),
-    )
-    from_west, from_east = exchange(east, west, "gx", True)
-    pairs = -(-(total + -(-2 * blocks * LANES // tx)) // 2)
+    pairs = -(-(total + -(-2 * state_blocks * LANES // tx)) // 2)
     north, south = call(
-        partial(state_rows_kernel, far_at, blocks),
+        partial(state_rows_kernel, far_at, blocks, state_blocks),
         [struct(pairs, SUB, tx)] * 2,
         flag, adjoint_init, history, got, diffusivity, land_mask, from_west, from_east,
         smem=(0,),
@@ -696,7 +723,7 @@
     terms = fields * steps * (steps + 1) // 2
     ext = (ty + SUB, tx + LANES)
     base, ring, late = call(
-        partial(state_kernel, far_at, blocks),
+        partial(state_kernel, far_at, blocks, state_blocks),
         [struct(nc, ty, tx), struct(*ext), struct(nc * SUB, terms * SUB)],
         flag, adjoint_init, history, got, diffusivity, land_mask,
         from_west, from_east, from_north, from_south, mixing, coupling,
@@ -708,17 +735,24 @@
         ],
     )
 
+    [acc] = call(
+        partial(arrival_kernel, cap, slots, nb),
+        [struct(slots, tiles * cap)],
+        tile.reshape(1), dest, atmos_block_index.reshape(tiles, entries),
+        smem=(0,),
+    )
+    arrived, base, acc = lax.optimization_barrier((arrived, base, acc))
     [own] = call(gather_kernel, [struct(steps * hf, ty, tx)], acc, arrived)
     far = lax.ppermute(own, "sect", [(0, 1)])
     halo_count = (steps - 1) * fields
     blocks = -(-halo_count // per)
     east, west = call(partial(late_columns_kernel, steps), [struct(ty, blocks * LANES)] * 2, own, far)
-    from_west, from_east = exchange(east, west, "gx", True, 1) if False else exchange(east, west, "gx", True)
+    from_west, from_east = exchange(east, west, "gx", True, 1)
     pairs = -(-(halo_count + -(-2 * blocks * LANES // tx)) // 2)
     north, south = call(
         partial(late_rows_kernel, steps, blocks), [struct(pairs, SUB, tx)] * 2, own, far, from_west, from_east
     )
-    from_north, from_south = exchange(south, north, "gy", False)
+    from_north, from_south = exchange(south, north, "gy", False, 1)
     [out] = call(
         partial(late_kernel, steps, blocks),
         [struct(1, nc, ty, tx)],

time: 117 us -> 103 us (0.88)
  the two profiles are of different devices: /device:TPU:28 before, /device:TPU:1 now
where the time goes in v1:
time: 103 us; the launch traced here: 102 us
  starting transfers between devices  33.6 us (33%)
  waiting for transfers between devices  28.7 us (28%)
  Pallas kernels  27.7 us (27%)
  local copies, waits for them, and re-layouts  12 us (12%)
    pallas_call x12, Pallas kernels, call(): pl.pallas_call(kernel, out_shape=outs, in_specs=[pl.BlockSpec(memory_spac...  27.7 us
    ppermute x6, waiting for transfers between devices, shifted(): return lax.ppermute(x, axis, pairs)  17.6 us
    ppermute x6, starting transfers between devices, shifted(): return lax.ppermute(x, axis, pairs)  14.5 us
    ppermute x4, starting transfers between devices, shifted(): lax.ppermute(x, ('sect', axis), [(base + i, base + j) for i, j in pairs])  12.2 us
    unnamed x64, local copies, waits for them, and re-layouts  12 us
    ppermute x4, waiting for transfers between devices, shifted(): lax.ppermute(x, ('sect', axis), [(base + i, base + j) for i, j in pairs])  5.58 us
    all_to_all x1, starting transfers between devices, body(): lax.all_to_all(packed.reshape(tiles, cap, -1), ('gy', 'gx'), split_axis=0...  5.54 us
    ppermute x1, waiting for transfers between devices, body(): far = lax.ppermute(own, 'sect', [(0, 1)])  2.85 us
  transfers between devices with their start and end apart: 13, of which 8 were waited for; matrix products, arithmetic and copies ran while one was open for 0% of the time, Pallas kernels for 15%

profile of v1, /device:TPU:1, one launch (start us, length us, event | category | flops | bytes accessed | tf_op | source)
XLA Modules:
  0.0 102.4 jit_solution(12316483315191378660)
XLA Ops:
  0.0 5.0 %shard_map.109 = (f32[11,32,256]{2,1,0:T(8,128)}, f32[28,32,256]{2,1,0:T(8,128)}) custom-call(f32[1,32,32,256]{3,2,1,0:T(8,128)} %refs_1_.1, s32[32,256]{1,0:T(8,128)} %refs_5_.7, f32[1,32,256]{2,1,0:T(8,128)} %refs_4_.5, f32[1,4,4,32,256]{4,3,2,1,0:T(8,128)} %refs_2_.3, f32[1,32,32]{2,1,0:T(8,128)} %refs_10_.1, f32[4,32]{1,0:T(4,128)} %ext_ref.1, ...), custom_call_target="tpu_custom_call" | custom-call | bytes 2921984 | tf_op jit(solution)/shard_map/pallas_call | solution.py:154
  5.0 0.1 collective-permute-start
  5.1 2.6 %collective-permute-done.refs_2_.refs_3_ = f32[28,32,256]{2,1,0:T(8,128)S(1)} collective-permute-done((f32[28,32,256]{2,1,0:T(8,128)}, f32[28,32,256]{2,1,0:T(8,128)S(1)}, u32[]{:S(2)}, u32[]{:S(2)}) %collective-permute-start) | collective-permute-done | bytes 917536 | tf_op jit(solution)/shard_map/ppermute | solution.py:677
  7.7 0.8 copy-done.13
  8.5 0.8 copy-done.16
  9.3 1.0 copy-done.21
  10.2 0.8 shard_map.110
  11.1 2.5 %collective-permute-start.1 = (f32[32,384]{1,0:T(8,128)S(1)}, f32[32,384]{1,0:T(8,128)S(1)}, u32[]{:S(2)}, u32[]{:S(2)}) collective-permute-start(f32[32,384]{1,0:T(8,128)S(1)} %get-tuple-element.30), channel_id=1, source_target_pairs={{0,1},{1,2},{2,3},{3,0},{4,5},{5,6},{6,7},{7,4},{8,9},{9,10},{10,1... | collective-permute-start | bytes 147464 | tf_op jit(solution)/shard_map/ppermute | solution.py:616
  13.5 2.1 %collective-permute-start.2 = (f32[32,384]{1,0:T(8,128)S(1)}, f32[32,384]{1,0:T(8,128)S(1)}, u32[]{:S(2)}, u32[]{:S(2)}) collective-permute-start(f32[32,384]{1,0:T(8,128)S(1)} %get-tuple-element.31), channel_id=1, source_target_pairs={{0,3},{1,0},{2,1},{3,2},{4,7},{5,4},{6,5},{7,6},{8,11},{9,8},{10,9... | collective-permute-start | bytes 147464 | tf_op jit(solution)/shard_map/ppermute | solution.py:616
  15.6 1.4 %collective-permute-done.1.refs_1_.refs_6_ = f32[32,384]{1,0:T(8,128)S(1)} collective-permute-done((f32[32,384]{1,0:T(8,128)S(1)}, f32[32,384]{1,0:T(8,128)S(1)}, u32[]{:S(2)}, u32[]{:S(2)}) %collective-permute-start.1) | collective-permute-done | bytes 49184 | tf_op jit(solution)/shard_map/ppermute | solution.py:616
  17.1 0.7 shard_map.111
  17.7 3.8 %collective-permute-start.3 = (f32[12,8,256]{2,1,0:T(8,128)}, f32[12,8,256]{2,1,0:T(8,128)}, u32[]{:S(2)}, u32[]{:S(2)}) collective-permute-start(f32[12,8,256]{2,1,0:T(8,128)} %get-tuple-element.32), channel_id=1, source_target_pairs={{0,4},{4,8},{8,12},{1,5},{5,9},{9,13},{2,6},{6,10},{10,14},{3,7},{... | collective-permute-start | bytes 294920 | tf_op jit(solution)/shard_map/ppermute | solution.py:616
  21.5 1.3 %collective-permute-start.4 = (f32[12,8,256]{2,1,0:T(8,128)}, f32[12,8,256]{2,1,0:T(8,128)}, u32[]{:S(2)}, u32[]{:S(2)}) collective-permute-start(f32[12,8,256]{2,1,0:T(8,128)} %get-tuple-element.33), channel_id=1, source_target_pairs={{4,0},{8,4},{12,8},{5,1},{9,5},{13,9},{6,2},{10,6},{14,10},{7,3},{... | collective-permute-start | bytes 294920 | tf_op jit(solution)/shard_map/ppermute | solution.py:616
  22.8 0.7 copy-done.30
  23.5 0.0 copy-done.28
  23.5 0.2 shard_map.112.refs_6_
  23.8 3.9 %collective-permute-done.4.refs_4_ = f32[12,8,256]{2,1,0:T(8,128)} collective-permute-done((f32[12,8,256]{2,1,0:T(8,128)}, f32[12,8,256]{2,1,0:T(8,128)}, u32[]{:S(2)}, u32[]{:S(2)}) %collective-permute-start.4) | collective-permute-done | bytes 98336 | tf_op jit(solution)/shard_map/ppermute | solution.py:616
  27.6 0.8 copy-done.25
  28.5 2.4 %shard_map.113 = f32[256,1024]{1,0:T(8,128)S(1)} custom-call(f32[32,32,256]{2,1,0:T(8,128)S(1)} %get-tuple-element.29.refs_0_, f32[32,384]{1,0:T(8,128)S(1)} %copy-done.6, f32[32,384]{1,0:T(8,128)S(1)} %copy-done.10, f32[12,8,256]{2,1,0:T(8,128)} %collective-permute-done.3.refs_3_, f32[12,8,256]{2,1,0:T(8,128)} %collective-permute-done.4.refs_4_, ...), custom_call_target="tpu_custom_call" | custom-call | bytes 2523136 | tf_op jit(solution)/shard_map/pallas_call | solution.py:154
  30.9 1.0 copy-done.2
  31.9 5.5 %all-to-all-start = ((f32[16,16,1024]{2,1,0:T(8,128)}), f32[16,16,1024]{2,1,0:T(8,128)S(1)}, u32[]{:S(2)}, u32[]{:S(2)}) async-start(f32[16,16,1024]{2,1,0:T(8,128)} %bitcast.9), calls=%async_computation | async-start | bytes 2097152 | tf_op jit(solution)/shard_map/all_to_all | solution.py:711
  37.5 0.8 copy-done.7
  38.2 0.8 copy-done.11
  39.0 0.8 copy-done.14
  39.8 0.8 copy-done.17
  40.6 0.1 shard_map.114
  40.6 3.4 %collective-permute-start.5 = (f32[30,8,256]{2,1,0:T(8,128)S(1)}, f32[30,8,256]{2,1,0:T(8,128)S(1)}, u32[]{:S(2)}, u32[]{:S(2)}) collective-permute-start(f32[30,8,256]{2,1,0:T(8,128)S(1)} %get-tuple-element.36), channel_id=1, source_target_pairs={{0,4},{4,8},{8,12},{1,5},{5,9},{9,13},{2,6},{6,10},{10,14},{3,7},{... | collective-permute-start | bytes 737288 | tf_op jit(solution)/shard_map/ppermute | solution.py:616
  44.1 1.5 %collective-permute-start.6 = (f32[30,8,256]{2,1,0:T(8,128)S(1)}, f32[30,8,256]{2,1,0:T(8,128)S(1)}, u32[]{:S(2)}, u32[]{:S(2)}) collective-permute-start(f32[30,8,256]{2,1,0:T(8,128)S(1)} %get-tuple-element.37), channel_id=1, source_target_pairs={{4,0},{8,4},{12,8},{5,1},{9,5},{13,9},{6,2},{10,6},{14,10},{7,3},{... | collective-permute-start | bytes 737288 | tf_op jit(solution)/shard_map/ppermute | solution.py:616
  45.6 2.2 %shard_map.116.acc_ref = f32[64,256]{1,0:T(8,128)S(1)} custom-call(s32[1]{0:T(128)} %bitcast.2.refs_0_, s32[16,128]{1,0:T(8,128)S(1)} %bitcast.11, s32[16,128]{1,0:T(8,128)S(1)} %bitcast.15), custom_call_target="tpu_custom_call" | custom-call | bytes 81924 | tf_op jit(solution)/shard_map/pallas_call | solution.py:154
  47.8 0.6 copy-done.22
  48.4 2.6 %collective-permute-done.5.refs_8_ = f32[30,8,256]{2,1,0:T(8,128)S(1)} collective-permute-done((f32[30,8,256]{2,1,0:T(8,128)S(1)}, f32[30,8,256]{2,1,0:T(8,128)S(1)}, u32[]{:S(2)}, u32[]{:S(2)}) %collective-permute-start.5) | collective-permute-done | bytes 245792 | tf_op jit(solution)/shard_map/ppermute | solution.py:616
  51.0 9.7 %collective-permute-done.6.refs_9_ = f32[30,8,256]{2,1,0:T(8,128)S(1)} collective-permute-done((f32[30,8,256]{2,1,0:T(8,128)S(1)}, f32[30,8,256]{2,1,0:T(8,128)S(1)}, u32[]{:S(2)}, u32[]{:S(2)}) %collective-permute-start.6) | collective-permute-done | bytes 245792 | tf_op jit(solution)/shard_map/ppermute | solution.py:616
  60.8 13.1 %shard_map.115 = (f32[32,32,256]{2,1,0:T(8,128)S(1)}, f32[40,384]{1,0:T(8,128)S(1)}, f32[256,320]{1,0:T(8,128)S(1)}) custom-call(s32[1]{0:T(128)} %bitcast.refs_0_, f32[1,32,32,256]{3,2,1,0:T(8,128)S(1)} %copy-done, f32[1,4,4,32,256]{4,3,2,1,0:T(8,128)S(1)} %copy-done.1, f32[28,32,256]{2,1,0:T(8,128)S(1)} %collective-permute-done.refs_2_.refs_3_, ...), custom_call_target="tpu_custom_call" | custom-call | bytes 4588548 | tf_op jit(solution)/shard_map/pallas_call | solution.py:154
  73.9 1.0 copy-done.3
  74.8 0.8 copy-done.19
  75.6 0.6 copy-done.26
  76.2 0.8 copy-done.23
  77.0 0.3 shard_map.117.refs_0_.refs_4_
  77.3 1.3 %collective-permute-start.7 = (f32[8,32,256]{2,1,0:T(8,128)S(1)}, f32[8,32,256]{2,1,0:T(8,128)S(1)}, u32[]{:S(2)}, u32[]{:S(2)}) collective-permute-start(f32[8,32,256]{2,1,0:T(8,128)S(1)} %shard_map.117.refs_0_.refs_4_), channel_id=1, source_target_pairs={{0,16},{1,17},{2,18},{3,19},{4,20},{5,21},{6,22},{7,23},{8,24},{9,... | collective-permute-start | bytes 786440 | tf_op jit(solution)/shard_map/ppermute | solution.py:746
  78.6 2.9 %collective-permute-done.7.refs_1_.refs_5_ = f32[8,32,256]{2,1,0:T(8,128)S(1)} collective-permute-done((f32[8,32,256]{2,1,0:T(8,128)S(1)}, f32[8,32,256]{2,1,0:T(8,128)S(1)}, u32[]{:S(2)}, u32[]{:S(2)}) %collective-permute-start.7) | collective-permute-done | bytes 262176 | tf_op jit(solution)/shard_map/ppermute | solution.py:746
  81.5 0.2 shard_map.118
  81.7 5.2 %collective-permute-start.8 = (f32[32,128]{1,0:T(8,128)S(1)}, f32[32,128]{1,0:T(8,128)S(1)}, u32[]{:S(2)}, u32[]{:S(2)}) collective-permute-start(f32[32,128]{1,0:T(8,128)S(1)} %get-tuple-element.45), channel_id=1, source_target_pairs={{16,17},{17,18},{18,19},{19,16},{20,21},{21,22},{22,23},{23,20},{2... | collective-permute-start | bytes 49160 | tf_op jit(solution)/shard_map/ppermute | solution.py:618
  86.9 2.6 %collective-permute-start.9 = (f32[32,128]{1,0:T(8,128)S(1)}, f32[32,128]{1,0:T(8,128)S(1)}, u32[]{:S(2)}, u32[]{:S(2)}) collective-permute-start(f32[32,128]{1,0:T(8,128)S(1)} %get-tuple-element.46), channel_id=1, source_target_pairs={{16,19},{17,16},{18,17},{19,18},{20,23},{21,20},{22,21},{23,22},{2... | collective-permute-start | bytes 49160 | tf_op jit(solution)/shard_map/ppermute | solution.py:618
  89.6 2.0 %collective-permute-done.9.refs_3_.refs_7_ = f32[32,128]{1,0:T(8,128)S(1)} collective-permute-done((f32[32,128]{1,0:T(8,128)S(1)}, f32[32,128]{1,0:T(8,128)S(1)}, u32[]{:S(2)}, u32[]{:S(2)}) %collective-permute-start.9) | collective-permute-done | bytes 16416 | tf_op jit(solution)/shard_map/ppermute | solution.py:618
  91.5 3.0 %collective-permute-start.10 = (f32[7,8,256]{2,1,0:T(8,128)S(1)}, f32[7,8,256]{2,1,0:T(8,128)S(1)}, u32[]{:S(2)}, u32[]{:S(2)}) collective-permute-start(f32[7,8,256]{2,1,0:T(8,128)S(1)} %get-tuple-element.47), channel_id=1, source_target_pairs={{16,20},{20,24},{24,28},{17,21},{21,25},{25,29},{18,22},{22,26},{2... | collective-permute-start | bytes 172040 | tf_op jit(solution)/shard_map/ppermute | solution.py:618
  94.6 1.3 %collective-permute-start.11 = (f32[7,8,256]{2,1,0:T(8,128)S(1)}, f32[7,8,256]{2,1,0:T(8,128)S(1)}, u32[]{:S(2)}, u32[]{:S(2)}) collective-permute-start(f32[7,8,256]{2,1,0:T(8,128)S(1)} %get-tuple-element.48), channel_id=1, source_target_pairs={{20,16},{24,20},{28,24},{21,17},{25,21},{29,25},{22,18},{26,22},{3... | collective-permute-start | bytes 172040 | tf_op jit(solution)/shard_map/ppermute | solution.py:618
  95.9 3.6 %collective-permute-done.11.refs_9_ = f32[7,8,256]{2,1,0:T(8,128)S(1)} collective-permute-done((f32[7,8,256]{2,1,0:T(8,128)S(1)}, f32[7,8,256]{2,1,0:T(8,128)S(1)}, u32[]{:S(2)}, u32[]{:S(2)}) %collective-permute-start.11) | collective-permute-done | bytes 57376 | tf_op jit(solution)/shard_map/ppermute | solution.py:618
  99.5 2.9 %shard_map.120 = f32[1,32,32,256]{3,2,1,0:T(8,128)} custom-call(s32[1]{0:T(128)} %bitcast.refs_0_, f32[32,32,256]{2,1,0:T(8,128)S(1)} %copy-done.4, f32[40,384]{1,0:T(8,128)S(1)} %copy-done.27, f32[256,320]{1,0:T(8,128)S(1)} %copy-done.20, f32[8,32,256]{2,1,0:T(8,128)S(1)} %shard_map.117.refs_0_.refs_4_, ...), custom_call_target="tpu_custom_call" | custom-call | bytes 3158020 | tf_op jit(solution)/shard_map/pallas_call | solution.py:154
  (54 shorter events, 0.1 us)
Async XLA Ops:
  0.0 7.7 %copy-start = (f32[1,32,32,256]{3,2,1,0:T(8,128)S(1)}, f32[1,32,32,256]{3,2,1,0:T(8,128)}, u32[]{:S(2)}) copy-start(f32[1,32,32,256]{3,2,1,0:T(8,128)} %refs_1_.1) | copy-start | bytes 3145732
  0.0 7.7 %copy-start.1 = (f32[1,4,4,32,256]{4,3,2,1,0:T(8,128)S(1)}, f32[1,4,4,32,256]{4,3,2,1,0:T(8,128)}, u32[]{:S(2)}) copy-start(f32[1,4,4,32,256]{4,3,2,1,0:T(8,128)} %refs_2_.3) | copy-start | bytes 1572868
  5.0 2.7 %collective-permute-start = (f32[28,32,256]{2,1,0:T(8,128)}, f32[28,32,256]{2,1,0:T(8,128)S(1)}, u32[]{:S(2)}, u32[]{:S(2)}) collective-permute-start(f32[28,32,256]{2,1,0:T(8,128)} %get-tuple-element.28), channel_id=1, source_target_pairs={{0,16},{16,0},{1,17},{17,1},{2,18},{18,2},{3,19},{19,3},{4,20},{20... | collective-permute-start | bytes 2752520 | tf_op jit(solution)/shard_map/ppermute | solution.py:677
  7.7 0.8 copy-start.13
  8.5 0.8 copy-start.16
  9.3 1.0 copy-start.21
  11.1 6.0 %collective-permute-start.1 = (f32[32,384]{1,0:T(8,128)S(1)}, f32[32,384]{1,0:T(8,128)S(1)}, u32[]{:S(2)}, u32[]{:S(2)}) collective-permute-start(f32[32,384]{1,0:T(8,128)S(1)} %get-tuple-element.30), channel_id=1, source_target_pairs={{0,1},{1,2},{2,3},{3,0},{4,5},{5,6},{6,7},{7,4},{8,9},{9,10},{10,1... | collective-permute-start | bytes 147464 | tf_op jit(solution)/shard_map/ppermute | solution.py:616
  13.5 3.5 %collective-permute-start.2 = (f32[32,384]{1,0:T(8,128)S(1)}, f32[32,384]{1,0:T(8,128)S(1)}, u32[]{:S(2)}, u32[]{:S(2)}) collective-permute-start(f32[32,384]{1,0:T(8,128)S(1)} %get-tuple-element.31), channel_id=1, source_target_pairs={{0,3},{1,0},{2,1},{3,2},{4,7},{5,4},{6,5},{7,6},{8,11},{9,8},{10,9... | collective-permute-start | bytes 147464 | tf_op jit(solution)/shard_map/ppermute | solution.py:616
  17.0 0.7 copy-start.5
  17.0 0.7 copy-start.9
  17.7 6.0 %collective-permute-start.3 = (f32[12,8,256]{2,1,0:T(8,128)}, f32[12,8,256]{2,1,0:T(8,128)}, u32[]{:S(2)}, u32[]{:S(2)}) collective-permute-start(f32[12,8,256]{2,1,0:T(8,128)} %get-tuple-element.32), channel_id=1, source_target_pairs={{0,4},{4,8},{8,12},{1,5},{5,9},{9,13},{2,6},{6,10},{10,14},{3,7},{... | collective-permute-start | bytes 294920 | tf_op jit(solution)/shard_map/ppermute | solution.py:616
  21.5 6.1 %collective-permute-start.4 = (f32[12,8,256]{2,1,0:T(8,128)}, f32[12,8,256]{2,1,0:T(8,128)}, u32[]{:S(2)}, u32[]{:S(2)}) collective-permute-start(f32[12,8,256]{2,1,0:T(8,128)} %get-tuple-element.33), channel_id=1, source_target_pairs={{4,0},{8,4},{12,8},{5,1},{9,5},{13,9},{6,2},{10,6},{14,10},{7,3},{... | collective-permute-start | bytes 294920 | tf_op jit(solution)/shard_map/ppermute | solution.py:616
  22.8 0.7 copy-start.30
  22.8 0.7 copy-start.28
  23.5 4.1 %copy-start.6 = (f32[32,384]{1,0:T(8,128)S(1)}, f32[32,384]{1,0:T(8,128)}, u32[]{:S(2)}) copy-start(f32[32,384]{1,0:T(8,128)} %copy-done.5) | copy-start | bytes 147460
  23.5 4.1 %copy-start.10 = (f32[32,384]{1,0:T(8,128)S(1)}, f32[32,384]{1,0:T(8,128)}, u32[]{:S(2)}) copy-start(f32[32,384]{1,0:T(8,128)} %copy-done.9) | copy-start | bytes 147460
  27.6 0.8 copy-start.25
  30.9 1.0 copy-start.2
  31.9 44.3 %all-to-all-start = ((f32[16,16,1024]{2,1,0:T(8,128)}), f32[16,16,1024]{2,1,0:T(8,128)S(1)}, u32[]{:S(2)}, u32[]{:S(2)}) async-start(f32[16,16,1024]{2,1,0:T(8,128)} %bitcast.9), calls=%async_computation | async-start | bytes 2097152 | tf_op jit(solution)/shard_map/all_to_all | solution.py:711
  37.4 0.8 copy-start.7
  38.2 0.8 copy-start.11
  39.0 0.8 copy-start.14
  39.8 0.8 copy-start.17
  40.6 5.0 %copy-start.31 = (s32[2048]{0:T(1024)S(1)}, s32[2048]{0:T(1024)}, u32[]{:S(2)}) copy-start(s32[2048]{0:T(1024)} %param.21) | copy-start | bytes 24580
  40.6 20.2 %copy-start.12 = (f32[32,384]{1,0:T(8,128)S(1)}, f32[32,384]{1,0:T(8,128)}, u32[]{:S(2)}) copy-start(f32[32,384]{1,0:T(8,128)} %copy-done.9) | copy-start | bytes 147460
  40.6 20.2 %copy-start.18 = (f32[1,32,256]{2,1,0:T(8,128)S(1)}, f32[1,32,256]{2,1,0:T(8,128)}, u32[]{:S(2)}) copy-start(f32[1,32,256]{2,1,0:T(8,128)} %refs_4_.5) | copy-start | bytes 98308
  40.6 20.2 %copy-start.24 = (f32[1,32,32]{2,1,0:T(8,128)S(1)}, f32[1,32,32]{2,1,0:T(8,128)}, u32[]{:S(2)}) copy-start(f32[1,32,32]{2,1,0:T(8,128)} %refs_10_.1) | copy-start | bytes 12292
  40.6 20.1 %copy-start.8 = (f32[32,384]{1,0:T(8,128)S(1)}, f32[32,384]{1,0:T(8,128)}, u32[]{:S(2)}) copy-start(f32[32,384]{1,0:T(8,128)} %copy-done.5) | copy-start | bytes 147460
  40.6 10.4 %collective-permute-start.5 = (f32[30,8,256]{2,1,0:T(8,128)S(1)}, f32[30,8,256]{2,1,0:T(8,128)S(1)}, u32[]{:S(2)}, u32[]{:S(2)}) collective-permute-start(f32[30,8,256]{2,1,0:T(8,128)S(1)} %get-tuple-element.36), channel_id=1, source_target_pairs={{0,4},{4,8},{8,12},{1,5},{5,9},{9,13},{2,6},{6,10},{10,14},{3,7},{... | collective-permute-start | bytes 737288 | tf_op jit(solution)/shard_map/ppermute | solution.py:616
  44.1 16.7 %collective-permute-start.6 = (f32[30,8,256]{2,1,0:T(8,128)S(1)}, f32[30,8,256]{2,1,0:T(8,128)S(1)}, u32[]{:S(2)}, u32[]{:S(2)}) collective-permute-start(f32[30,8,256]{2,1,0:T(8,128)S(1)} %get-tuple-element.37), channel_id=1, source_target_pairs={{4,0},{8,4},{12,8},{5,1},{9,5},{13,9},{6,2},{10,6},{14,10},{7,3},{... | collective-permute-start | bytes 737288 | tf_op jit(solution)/shard_map/ppermute | solution.py:616
  45.6 15.2 %copy-start.15 = (s32[32,256]{1,0:T(8,128)S(1)}, s32[32,256]{1,0:T(8,128)}, u32[]{:S(2)}) copy-start(s32[32,256]{1,0:T(8,128)} %refs_5_.7) | copy-start | bytes 98308
  45.6 15.2 %copy-start.29 = (f32[1,32,8]{1,2,0:T(8,128)S(1)}, f32[1,32,8]{1,2,0:T(8,128)}, u32[]{:S(2)}) copy-start(f32[1,32,8]{1,2,0:T(8,128)} %param.14) | copy-start | bytes 3076
  47.8 0.6 copy-start.22
  73.8 1.0 copy-start.3
  74.8 0.8 copy-start.19
  75.6 0.6 copy-start.26
  76.2 0.8 copy-start.23
  77.0 22.4 %copy-start.4 = (f32[32,32,256]{2,1,0:T(8,128)S(1)}, f32[32,32,256]{2,1,0:T(8,128)}, u32[]{:S(2)}) copy-start(f32[32,32,256]{2,1,0:T(8,128)} %copy-done.3) | copy-start | bytes 3145732
  77.3 4.2 %collective-permute-start.7 = (f32[8,32,256]{2,1,0:T(8,128)S(1)}, f32[8,32,256]{2,1,0:T(8,128)S(1)}, u32[]{:S(2)}, u32[]{:S(2)}) collective-permute-start(f32[8,32,256]{2,1,0:T(8,128)S(1)} %shard_map.117.refs_0_.refs_4_), channel_id=1, source_target_pairs={{0,16},{1,17},{2,18},{3,19},{4,20},{5,21},{6,22},{7,23},{8,24},{9,... | collective-permute-start | bytes 786440 | tf_op jit(solution)/shard_map/ppermute | solution.py:746
  81.7 17.8 %copy-start.20 = (f32[256,320]{1,0:T(8,128)S(1)}, f32[256,320]{1,0:T(8,128)}, u32[]{:S(2)}) copy-start(f32[256,320]{1,0:T(8,128)} %copy-done.19) | copy-start | bytes 983044
  81.7 7.9 %collective-permute-start.8 = (f32[32,128]{1,0:T(8,128)S(1)}, f32[32,128]{1,0:T(8,128)S(1)}, u32[]{:S(2)}, u32[]{:S(2)}) collective-permute-start(f32[32,128]{1,0:T(8,128)S(1)} %get-tuple-element.45), channel_id=1, source_target_pairs={{16,17},{17,18},{18,19},{19,16},{20,21},{21,22},{22,23},{23,20},{2... | collective-permute-start | bytes 49160 | tf_op jit(solution)/shard_map/ppermute | solution.py:618
  86.9 12.6 %copy-start.27 = (f32[40,384]{1,0:T(8,128)S(1)}, f32[40,384]{1,0:T(8,128)}, u32[]{:S(2)}) copy-start(f32[40,384]{1,0:T(8,128)} %copy-done.26) | copy-start | bytes 184324
  86.9 4.6 %collective-permute-start.9 = (f32[32,128]{1,0:T(8,128)S(1)}, f32[32,128]{1,0:T(8,128)S(1)}, u32[]{:S(2)}, u32[]{:S(2)}) collective-permute-start(f32[32,128]{1,0:T(8,128)S(1)} %get-tuple-element.46), channel_id=1, source_target_pairs={{16,19},{17,16},{18,17},{19,18},{20,23},{21,20},{22,21},{23,22},{2... | collective-permute-start | bytes 49160 | tf_op jit(solution)/shard_map/ppermute | solution.py:618
  91.5 4.3 %collective-permute-start.10 = (f32[7,8,256]{2,1,0:T(8,128)S(1)}, f32[7,8,256]{2,1,0:T(8,128)S(1)}, u32[]{:S(2)}, u32[]{:S(2)}) collective-permute-start(f32[7,8,256]{2,1,0:T(8,128)S(1)} %get-tuple-element.47), channel_id=1, source_target_pairs={{16,20},{20,24},{24,28},{17,21},{21,25},{25,29},{18,22},{22,26},{2... | collective-permute-start | bytes 172040 | tf_op jit(solution)/shard_map/ppermute | solution.py:618
  94.6 4.9 %collective-permute-start.11 = (f32[7,8,256]{2,1,0:T(8,128)S(1)}, f32[7,8,256]{2,1,0:T(8,128)S(1)}, u32[]{:S(2)}, u32[]{:S(2)}) collective-permute-start(f32[7,8,256]{2,1,0:T(8,128)S(1)} %get-tuple-element.48), channel_id=1, source_target_pairs={{20,16},{24,20},{28,24},{21,17},{25,21},{29,25},{22,18},{26,22},{3... | collective-permute-start | bytes 172040 | tf_op jit(solution)/shard_map/ppermute | solution.py:618

commit v2 on v1

--- a/solution.py
+++ b/solution.py
@@ -71,6 +71,13 @@
     return east, west
 
 
+def store_columns(read, count, tx, hw, east_ref, west_ref, start):
+    east, west = pack_columns(read, count, east_ref.shape[0], tx, hw)
+    for block, (e, w) in enumerate(zip(east, west)):
+        east_ref[:, (start + block) * LANES : (start + block + 1) * LANES] = e
+        west_ref[:, (start + block) * LANES : (start + block + 1) * LANES] = w
+
+
 def side_block(from_west, from_east, f, hw):
     place = f % (LANES // hw)
     ids = lane_ids(from_west.shape[0])
@@ -80,26 +87,47 @@
     return jnp.where(ids < hw, e, jnp.where(ids >= LANES - hw, w, 0.0))
 
 
-def pair_rows(a, b, first):
-    low = lax.broadcasted_iota(jnp.int32, a.shape, 0) < SUB // 2
-    turned = pltpu.roll(b, SUB // 2, 0)
-    return jnp.where(low, a, turned) if first else jnp.where(low, turned, a)
-
-
-def edge_tile(from_north, from_south, odd):
-    if odd:
-        from_north = pltpu.roll(from_north, SUB // 2, 0)
-        from_south = pltpu.roll(from_south, SUB // 2, 0)
-    low = lax.broadcasted_iota(jnp.int32, from_north.shape, 0) < SUB // 2
-    return jnp.where(low, from_south, from_north)
-
-
-def send_rows(read, count, ty, north_ref, south_ref):
-    for pair in range(-(-count // 2)):
-        a, b = 2 * pair, min(2 * pair + 1, count - 1)
-        last = ty // SUB - 1
-        north_ref[pair] = pair_rows(read(a, 0), read(b, 0), True)
-        south_ref[pair] = pair_rows(read(a, last), read(b, last), False)
+def strip_places(widths):
+    used, spots = [], [None] * len(widths)
+    for f in sorted(range(len(widths)), key=lambda f: -widths[f]):
+        t = next((t for t, rows in enumerate(used) if rows + widths[f] <= SUB), len(used))
+        if t == len(used):
+            used.append(0)
+        spots[f] = (t, used[t])
+        used[t] += widths[f]
+    return spots, len(used)
+
+
+def turn(x, by):
+    return pltpu.roll(x, by % SUB, 0) if by % SUB else x
+
+
+def edge_reader(north_ref, south_ref, widths):
+    spots, _ = strip_places(widths)
+
+    def edge(f, cols=slice(None)):
+        (t, first), w = spots[f], widths[f]
+        south = turn(south_ref[t, :, cols], -first)
+        north = turn(north_ref[t, :, cols], -w - first)
+        sub = lax.broadcasted_iota(jnp.int32, south.shape, 0)
+        return jnp.where(sub < w, south, jnp.where(sub >= SUB - w, north, 0.0))
+
+    return edge
+
+
+def send_rows(read, widths, ty, north_ref, south_ref):
+    spots, tiles = strip_places(widths)
+    last = ty // SUB - 1
+    sub = lax.broadcasted_iota(jnp.int32, north_ref.shape[1:], 0)
+    for t in range(tiles):
+        north = south = jnp.zeros(north_ref.shape[1:], F32)
+        for f, (at, first) in enumerate(spots):
+            if at == t:
+                here = (sub >= first) & (sub < first + widths[f])
+                north = jnp.where(here, turn(read(f, 0), first), north)
+                south = jnp.where(here, turn(read(f, last), first + widths[f]), south)
+        north_ref[t] = north
+        south_ref[t] = south
 
 
 def ring_lap(p):
@@ -109,22 +137,20 @@
     return around - 4.0 * p
 
 
-def with_ring(main, packed_west, packed_east, f, north_ref, south_ref, hw):
-    bottom = edge_tile(north_ref[f // 2], south_ref[f // 2], f % 2)
+def with_ring(main, packed_west, packed_east, f, edge, hw):
+    bottom = edge(f)
     side = side_block(packed_west, packed_east, f, hw)
     return jnp.concatenate([jnp.concatenate([main, bottom], axis=0), side], axis=1)
 
 
-def sides_with_rows(west_ref, east_ref, north_ref, south_ref, first, start, blocks, tx):
+def sides_with_rows(west_ref, east_ref, edge, first, start, blocks, tx):
     west, east = [], []
     per = tx // LANES
     for block in range(blocks):
         out = []
         for which, ref in enumerate((west_ref, east_ref)):
             f, at = divmod(which * blocks + block, per)
-            f = first + f
-            cols = pl.ds(at * LANES, LANES)
-            tile = edge_tile(north_ref[f // 2, :, cols], south_ref[f // 2, :, cols], f % 2)
+            tile = edge(first + f, slice(at * LANES, (at + 1) * LANES))
             out.append(jnp.concatenate([ref[:, pl.ds((start + block) * LANES, LANES)], tile], axis=0))
         west.append(out[0])
         east.append(out[1])
@@ -148,16 +174,37 @@
     return read, -(-2 * blocks // per)
 
 
-def call(kernel, outs, *args, smem=(), hbm=(), scratch=(), flops=0, vmem=48):
+def with_packed(widths, blocks, tx, hw):
+    return widths + [hw] * -(-2 * blocks * LANES // tx)
+
+
+def projected_widths(places, halo_count, steps):
+    widths = [0] * halo_count
+    for key, f in places.items():
+        if f < halo_count:
+            widths[f] = steps if key == "d" else steps - 1 if key == "w" else steps - key[1] if key[0] == "t" else steps - 1 - key[1] - key[2]
+    return widths
+
+
+def state_widths(steps, fields, nc):
+    return [k for _ in range(2) for k in range(1, steps) for _ in range(fields)] + [steps] * (2 + nc)
+
+
+def late_widths(steps, fields):
+    return [steps - 1 - n for n, _ in late_fields(steps, fields)]
+
+
+def call(kernel, outs, *args, smem=(), hbm=(), hbm_out=False, scratch=(), flops=0):
     space = lambda i: pltpu.SMEM if i in smem else pltpu.HBM if i in hbm else pltpu.VMEM
+    args = [pltpu.with_memory_space_constraint(a, pltpu.HBM) if i in hbm else a for i, a in enumerate(args)]
     nbytes = sum(math.prod(a.shape) * 4 for a in (*args, *outs))
     return pl.pallas_call(
         kernel,
-        out_shape=outs,
+        out_shape=[pltpu.HBM(o.shape, o.dtype) for o in outs] if hbm_out else outs,
         in_specs=[pl.BlockSpec(memory_space=space(i)) for i in range(len(args))],
-        out_specs=[pl.BlockSpec(memory_space=pltpu.VMEM) for _ in outs],
+        out_specs=[pl.BlockSpec(memory_space=pltpu.HBM if hbm_out else pltpu.VMEM) for _ in outs],
         scratch_shapes=scratch,
-        compiler_params=pltpu.CompilerParams(vmem_limit_bytes=vmem * 2**20),
+        compiler_params=pltpu.CompilerParams(vmem_limit_bytes=48 * 2**20),
         cost_estimate=pl.CostEstimate(flops=flops, bytes_accessed=nbytes, transcendentals=0),
     )(*args)
 
@@ -173,7 +220,8 @@
 
 
 def project_kernel(
-    adj_hbm, mask_hbm, diff_hbm, hist_hbm, mix_ref, ext_ref, coup_ref, keep_ref, send_ref, adj_ref, mask_ref, sems
+    adj_hbm, mask_hbm, diff_hbm, hist_hbm, mix_hbm, ext_hbm, coup_hbm,
+    keep_ref, send_ref, east_ref, west_ref, adj_ref, mask_ref, mix_ref, ext_ref, coup_ref, chain_ref, sems,
 ):
     _, nc, ty, tx = adj_hbm.shape
     _, steps, fields = hist_hbm.shape[:3]
@@ -187,33 +235,45 @@
     for k in range(steps):
         to = send_ref.at[pl.ds(count + 2 + k * fields, fields)]
         copies.append(pltpu.make_async_copy(hist_hbm.at[0, k], to, sems.at[3 + k]))
-    for copy in copies:
+    small = [
+        pltpu.make_async_copy(a, b, sems.at[3 + steps + i])
+        for i, (a, b) in enumerate(((mix_hbm, mix_ref), (ext_hbm, ext_ref), (coup_hbm, coup_ref)))
+    ]
+    for copy in small + copies:
         copy.start()
+    for copy in small:
+        copy.wait()
     mix = mix_ref[0]
     rows = ext_ref[...]
-    lows, highs = [], []
+    chain_ref[...] = jnp.zeros_like(chain_ref)
     for m in range(steps + 1):
-        big = grown(rows)
-        lows.append(big[: hf * SUB])
-        highs.append(big[hf * SUB :])
-        if m < steps:
-            force = grown(full_dot(rows, coup_ref[0], LAST))
-            height, width = hf * SUB, force.shape[1]
-            for ref, at in ((keep_ref, 0), (send_ref, height)):
-                per = ty // height
-                r0, c0 = (m % per) * height, (m // per) * LANES
-                ref[count, r0 : r0 + height, c0 : c0 + width] = force[at : at + height]
-            rows = rows + full_dot(rows, mix, LAST)
-    big = halves(jnp.concatenate(lows + highs, axis=0))
+        chain_ref[m * fields : (m + 1) * fields, :] = rows
+        rows = rows + full_dot(rows, mix, LAST)
+    chain = chain_ref[...]
+    big = grown(chain)
+    half = lambda x, h: jnp.concatenate(
+        [x[(m * fields + h * hf) * SUB : (m * fields + (h + 1) * hf) * SUB] for m in range(steps + 1)], axis=0
+    )
+    force = grown(full_dot(chain, coup_ref[0], LAST))
+    height, width = hf * SUB, force.shape[1]
+    for m in range(steps):
+        for h, ref in enumerate((keep_ref, send_ref)):
+            per = ty // height
+            r0, c0 = (m % per) * height, (m // per) * LANES
+            at = (m * fields + h * hf) * SUB
+            ref[count, r0 : r0 + height, c0 : c0 + width] = force[at : at + height]
+    big = halves(jnp.concatenate([half(big, 0), half(big, 1)], axis=0))
     copies[0].wait()
     copies[1].wait()
+    wet = mask_ref[...].astype(F32)
+    keep_ref[count + 1] = wet
     for g in range(ty // SUB):
         rs = slice(g * SUB, (g + 1) * SUB)
-        wet = mask_ref[rs, :].astype(F32)
-        u = (adj_ref[:, rs, :] * wet[None]).reshape(nc * SUB, tx)
+        u = (adj_ref[:, rs, :] * wet[rs][None]).reshape(nc * SUB, tx)
         t = dot3(big, halves(u)).reshape(2 * count, SUB, tx)
         keep_ref[:count, rs, :] = t[:count]
         send_ref[:count, rs, :] = t[count:]
+    store_columns(lambda f, l: adj_ref[f, :, l * LANES : (l + 1) * LANES], nc, tx, steps, east_ref, west_ref, 0)
     for copy in copies[2:]:
         copy.wait()
 
@@ -232,9 +292,10 @@
 
 
 def force_kernel(
-    places, halo_count, flag_ref, keep_ref, got_ref, adj_ref, hist_ref, diff_ref, mask_ref, main_ref, east_ref, west_ref
+    places, halo_count, steps, fields, flag_ref, keep_ref, send_ref, got_ref, adj_east_ref, adj_west_ref,
+    main_ref, east_ref, west_ref,
 ):
-    _, steps, fields, ty, tx = hist_ref.shape
+    _, ty, tx = main_ref.shape
     hf, hw = fields // 2, steps
     count = (steps + 1) * hf
     ocean = flag_ref[0] == 0
@@ -242,8 +303,8 @@
     for m in range(steps + 1):
         for q in range(hf):
             main_ref[places["t", m, q]] = pick(keep_ref[m * hf + q], got_ref[m * hf + q])
-    main_ref[places["d"]] = pick(diff_ref[0], got_ref[count + 1])
-    main_ref[places["w"]] = mask_ref[...].astype(F32)
+    main_ref[places["d"]] = pick(send_ref[count + 1], got_ref[count + 1])
+    main_ref[places["w"]] = keep_ref[count + 1]
     height, width = hf * SUB, 2 * fields * SUB
     per = ty // height
     big = []
@@ -256,8 +317,8 @@
         rs = slice(g * SUB, (g + 1) * SUB)
         for n in range(steps):
             k = steps - 1 - n
-            own = hist_ref[0, k, :, rs, :]
-            far = got_ref[count + 2 + k * fields : count + 2 + (k + 1) * fields, rs, :]
+            at = (slice(count + 2 + k * fields, count + 2 + (k + 1) * fields), rs)
+            own, far = send_ref[at], got_ref[at]
             h = jnp.concatenate([pick(own, far), pick(far, own)], axis=0).reshape(-1, tx)
             out = bf_dot(big[: (steps - n) * height], stacked_columns(h))
             for m in range(steps - n):
@@ -265,23 +326,25 @@
                     at = (m * hf + q) * SUB
                     main_ref[places["g", n, m, q], rs, :] = out[at : at + SUB]
     read = lambda f, l: main_ref[f, :, l * LANES : (l + 1) * LANES]
-    east, west = pack_columns(read, halo_count, ty, tx, hw)
-    state, total = state_reader(adj_ref, hist_ref, got_ref, count + 2, diff_ref, own_wet(flag_ref, mask_ref))
+    store_columns(read, halo_count, tx, hw, east_ref, west_ref, 0)
+    start = -(-halo_count // (LANES // hw))
+    state, total = forced_reader(steps, fields, flag_ref, send_ref, got_ref, keep_ref)
     read = lambda f, l: state(f, slice(0, ty), slice(l * LANES, (l + 1) * LANES))
-    more = pack_columns(read, total, ty, tx, hw)
-    for block, (e, w) in enumerate(zip(east + more[0], west + more[1])):
-        east_ref[:, block * LANES : (block + 1) * LANES] = e
-        west_ref[:, block * LANES : (block + 1) * LANES] = w
-
-
-def rows_kernel(halo_count, blocks, main_ref, west_ref, east_ref, north_ref, south_ref):
+    store_columns(read, total, tx, hw, east_ref, west_ref, start)
+    start += -(-total // (LANES // hw))
+    east_ref[:, start * LANES :] = adj_east_ref[...]
+    west_ref[:, start * LANES :] = adj_west_ref[...]
+
+
+def rows_kernel(widths, blocks, main_ref, west_ref, east_ref, north_ref, south_ref):
     _, ty, tx = main_ref.shape
     packed, more = packed_reader(west_ref, east_ref, 0, blocks, tx)
+    count = len(widths) - more
 
     def read(f, t):
-        return main_ref[f, t * SUB : (t + 1) * SUB, :] if f < halo_count else packed(f - halo_count, t)
-
-    send_rows(read, halo_count + more, ty, north_ref, south_ref)
+        return main_ref[f, t * SUB : (t + 1) * SUB, :] if f < count else packed(f - count, t)
+
+    send_rows(read, widths, ty, north_ref, south_ref)
 
 
 def block_place(slots, nb):
@@ -298,7 +361,7 @@
     return row < lax.broadcasted_iota(jnp.int32, (entries, entries), 1)
 
 
-def select_kernel(cap, slots, nb, pos_ref, dest_ref, src_ref, sel_ref):
+def select_kernel(cap, slots, nb, pos_ref, dest_ref, src_ref, regrid_ref, sel_ref, weights_ref):
     tiles, entries = dest_ref.shape
     tile = pos_ref[0]
     dest = dest_ref[pl.ds(tile, 1), :]
@@ -306,6 +369,7 @@
     same = (across == across.T) & earlier(entries)
     rank = jnp.sum(same.astype(F32), axis=0, keepdims=True).astype(jnp.int32)
     source = block_place(slots, nb)(src_ref[pl.ds(tile, 1), :])
+    weights_ref[...] = regrid_ref[0]
     sel_ref[...] = bf_dot(onehot(tiles * cap, dest * cap + rank), onehot(slots, source), LAST)
 
 
@@ -328,40 +392,43 @@
 
 
 def surface_kernel(
-    places, halo_count, steps, hf, main_ref, west_ref, east_ref, north_ref, south_ref, regrid_ref, sel_ref, out_ref
+    places, halo_count, widths, steps, hf, main_ref, west_ref, east_ref, north_ref, south_ref, weights_ref, sel_ref,
+    out_hbm, out_ref, sems,
 ):
     _, ty, tx = main_ref.shape
     hw = steps
     per = LANES // hw
     blocks = -(-halo_count // per)
-    wests, easts = sides_with_rows(west_ref, east_ref, north_ref, south_ref, halo_count, 0, blocks, tx)
+    edge = edge_reader(north_ref, south_ref, widths)
+    wests, easts = sides_with_rows(west_ref, east_ref, edge, halo_count, 0, blocks, tx)
 
     def ext(key):
         f = places[key]
         if f < halo_count:
-            return with_ring(main_ref[f], wests[f // per], easts[f // per], f, north_ref, south_ref, hw)
+            return with_ring(main_ref[f], wests[f // per], easts[f // per], f, edge, hw)
         main = jnp.concatenate([main_ref[f], jnp.zeros((SUB, tx), F32)], axis=0)
         return jnp.concatenate([main, jnp.zeros((ty + SUB, LANES), F32)], axis=1)
 
     diff, wet = ext("d"), ext("w")
-    weights = halves(regrid_ref[0])
+    weights = halves(weights_ref[...])
     sel = sel_ref[...].astype(BF16)
-    surfaces = {}
+    copies = []
     for q in range(hf):
         t = [ext(("t", m, q)) for m in range(steps + 1)]
         for n in range(steps):
             t = [wet * (t[m + 1] + ring_lap(diff * t[m]) + ext(("g", n, m, q))) for m in range(steps - n)]
-            surfaces[n, q] = t[0]
-    for n in range(steps):
-        for q in range(hf):
-            s = surfaces[n, q]
-            s = jnp.concatenate([s[:ty, l * LANES : (l + 1) * LANES] for l in range(tx // LANES)], axis=0)
+            s = jnp.concatenate([t[0][:ty, l * LANES : (l + 1) * LANES] for l in range(tx // LANES)], axis=0)
             s = halves(dot3(halves(s), weights))
             at = (n * hf + q) * LANES
             out_ref[:, at : at + LANES] = bf_dot(sel, s[0]) + bf_dot(sel, s[1])
-
-
-def gather_kernel(acc_ref, in_ref, out_ref):
+            to = out_hbm.at[:, pl.ds(at, LANES)]
+            copies.append(pltpu.make_async_copy(out_ref.at[:, pl.ds(at, LANES)], to, sems.at[n * hf + q]))
+            copies[-1].start()
+    for copy in copies:
+        copy.wait()
+
+
+def gather_kernel(acc_ref, in_ref, after_ref, out_ref):
     count, ty, tx = out_ref.shape
     acc = acc_ref[...].astype(BF16)
     for i in range(count):
@@ -371,96 +438,49 @@
             out_ref[i, :, l * LANES : (l + 1) * LANES] = total[l * ty : (l + 1) * ty]
 
 
-def state_reader(adj_ref, hist_ref, far_ref, far_at, diff_ref, wet):
-    _, steps, fields = hist_ref.shape[:3]
-    nc = adj_ref.shape[1]
+def forced_reader(steps, fields, flag_ref, send_ref, got_ref, keep_ref):
+    count = (steps + 1) * (fields // 2)
     forced = (steps - 1) * fields
-    total = nc + 2 * forced + 2
 
     def read(f, rows, cols):
-        if f < nc:
-            return adj_ref[0, f, rows, cols]
-        f -= nc
         if f < 2 * forced:
             part, f = divmod(f, forced)
-            k, q = divmod(f, fields)
-            if part == 0:
-                return hist_ref[0, k + 1, q, rows, cols]
-            return far_ref[far_at + (k + 1) * fields + q, rows, cols]
+            return (send_ref, got_ref)[part][count + 2 + fields + f, rows, cols]
         if f == 2 * forced:
-            return diff_ref[0, rows, cols]
-        return wet(rows, cols)
-
-    return read, total
-
-
-def own_wet(flag_ref, mask_ref):
-    ocean = flag_ref[0] == 0
-    return lambda rows, cols: jnp.where(ocean, mask_ref[rows, cols].astype(F32), 1.0)
+            return send_ref[count + 1, rows, cols]
+        return jnp.where(flag_ref[0] == 0, keep_ref[count + 1, rows, cols], 1.0)
+
+    return read, 2 * forced + 2
 
 
 def state_rows_kernel(
-    far_at, start, blocks, flag_ref, adj_ref, hist_ref, far_ref, diff_ref, mask_ref, west_ref, east_ref, north_ref, south_ref
+    steps, fields, start, blocks, flag_ref, adj_hbm, send_ref, got_ref, keep_ref, west_ref, east_ref,
+    north_ref, south_ref, edges, sems,
 ):
-    ty, tx = mask_ref.shape
-    read, total = state_reader(adj_ref, hist_ref, far_ref, far_at, diff_ref, own_wet(flag_ref, mask_ref))
-    packed, more = packed_reader(west_ref, east_ref, start, blocks, tx)
-
-    def at(f, t):
-        rows = slice(t * SUB, (t + 1) * SUB)
-        return read(f, rows, slice(0, tx)) if f < total else packed(f - total, t)
-
-    send_rows(at, total + more, ty, north_ref, south_ref)
-
-
-def state_kernel(
-    far_at,
-    start,
-    blocks,
-    flag_ref,
-    adj_ref,
-    hist_ref,
-    far_ref,
-    diff_ref,
-    mask_ref,
-    west_ref,
-    east_ref,
-    north_ref,
-    south_ref,
-    mix_ref,
-    coup_ref,
-    out_ref,
-    ring_ref,
-    late_ref,
-    state,
-    force,
-    spread,
-):
-    ty, tx = mask_ref.shape
-    nc = adj_ref.shape[1]
-    _, steps, fields = hist_ref.shape[:3]
-    hw = steps
-    per = LANES // hw
-    ocean = flag_ref[0] == 0
-    read, total = state_reader(adj_ref, hist_ref, far_ref, far_at, diff_ref, own_wet(flag_ref, mask_ref))
-    wests, easts = sides_with_rows(west_ref, east_ref, north_ref, south_ref, total, start, blocks, tx)
-
-    def ext(f):
-        main = read(f, slice(0, ty), slice(0, tx))
-        return with_ring(main, wests[f // per], easts[f // per], f, north_ref, south_ref, hw)
-
-    for c in range(nc):
-        state[c] = ext(c)
-    forced = (steps - 1) * fields
-    for k in range(1, steps):
-        for q in range(fields):
-            force[k, q] = ext(nc + (k - 1) * fields + q)
-            force[k, fields + q] = ext(nc + forced + (k - 1) * fields + q)
-    for q in range(fields):
-        force[0, q, :ty, :tx] = hist_ref[0, 0, q]
-        force[0, fields + q, :ty, :tx] = far_ref[far_at + q]
-    diff, wet = ext(nc + 2 * forced), ext(nc + 2 * forced + 1)
-    ring_ref[...] = diff
+    _, nc, ty, tx = adj_hbm.shape
+    copies = [
+        pltpu.make_async_copy(adj_hbm.at[0, :, pl.ds(t, SUB), :], edges.at[i], sems.at[i])
+        for i, t in enumerate((0, ty - SUB))
+    ]
+    for copy in copies:
+        copy.start()
+    forced, total = forced_reader(steps, fields, flag_ref, send_ref, got_ref, keep_ref)
+    packed, _ = packed_reader(west_ref, east_ref, start, blocks, tx)
+    for copy in copies:
+        copy.wait()
+
+    def read(f, t):
+        if f < total:
+            return forced(f, slice(t * SUB, (t + 1) * SUB), slice(0, tx))
+        f -= total
+        return edges[min(t, 1), f] if f < nc else packed(f - nc, t)
+
+    widths = with_packed(state_widths(steps, fields, nc), blocks, tx, steps)
+    send_rows(read, widths, ty, north_ref, south_ref)
+
+
+def matrices_kernel(steps, fields, flag_ref, mix_ref, coup_ref, mix8_ref, coup8_ref, late_ref):
+    nc = mix_ref.shape[1]
     ident = lax.broadcasted_iota(jnp.int32, (nc, nc), 0) == lax.broadcasted_iota(jnp.int32, (nc, nc), 1)
     step_m = mix_ref[0].T + ident.astype(F32)
     coup = coup_ref[0].T
@@ -469,23 +489,58 @@
     for i in range(steps):
         powers.append(late)
         late = full_dot(step_m, late)
-    columns = []
+    at = 0
     for k in range(steps - 1, -1, -1):
         for j in range(k + 1):
-            columns.append(math.comb(k, j) * powers[k - j])
-    at = 0
-    for column in columns:
-        late_ref[:, at : at + fields * SUB] = grown(column)
-        at += fields * SUB
+            late_ref[:, at : at + fields * SUB] = grown(math.comb(k, j) * powers[k - j])
+            at += fields * SUB
     first = lax.broadcasted_iota(jnp.int32, coup.shape, 1) < fields
-    coup = jnp.where(jnp.logical_or(first, ocean), coup, 0.0)
-    mix8, coup8 = halves(grown(step_m)), stacked_rows(grown(coup))
+    mix8_ref[...] = grown(step_m)
+    coup8_ref[...] = grown(jnp.where(jnp.logical_or(first, flag_ref[0] == 0), coup, 0.0))
+
+
+def state_kernel(
+    steps, fields, start, blocks, flag_ref, adj_hbm, send_ref, got_ref, keep_ref, west_ref, east_ref, north_ref,
+    south_ref, mix8_ref, coup8_ref, out_ref, ring_ref, state, force, spread, sem,
+):
+    _, nc, ty, tx = adj_hbm.shape
+    copy = pltpu.make_async_copy(adj_hbm.at[0], out_ref, sem)
+    copy.start()
+    hw = steps
+    per = LANES // hw
+    read, total = forced_reader(steps, fields, flag_ref, send_ref, got_ref, keep_ref)
+    edge = edge_reader(north_ref, south_ref, with_packed(state_widths(steps, fields, nc), blocks, tx, hw))
+    wests, easts = sides_with_rows(west_ref, east_ref, edge, total + nc, start, blocks, tx)
+
+    def ext(f):
+        main = read(f, slice(0, ty), slice(0, tx))
+        return with_ring(main, wests[f // per], easts[f // per], f, edge, hw)
+
+    forced = (steps - 1) * fields
+    for k in range(1, steps):
+        for q in range(fields):
+            force[k, q] = ext((k - 1) * fields + q)
+            force[k, fields + q] = ext(forced + (k - 1) * fields + q)
+    at = (steps + 1) * (fields // 2) + 2
+    for q in range(fields):
+        force[0, q, :ty, :tx] = send_ref[at + q]
+        force[0, fields + q, :ty, :tx] = got_ref[at + q]
+    diff, wet = ext(2 * forced), ext(2 * forced + 1)
+    ring_ref[...] = diff
+    mix8, coup8 = halves(mix8_ref[...]), stacked_rows(coup8_ref[...])
     groups = ty // SUB
     main = [((g, 0, tx),) for g in range(groups)]
     halo = [((groups, 0, tx),)] + [
         tuple((g, tx, LANES) for g in range(at, min(at + tx // LANES, groups + 1)))
         for at in range(0, groups + 1, tx // LANES)
     ]
+    copy.wait()
+    block = -(-total // per)
+    for c in range(nc):
+        west, east = wests[block + c // per], easts[block + c // per]
+        state[c, :ty, :tx] = out_ref[c]
+        state[c, ty:, :tx] = edge(total + c)
+        state[c, :, tx:] = side_block(west, east, c, hw)
 
     for n in range(steps):
         k = steps - 1 - n
@@ -544,7 +599,7 @@
     count, ty, tx = own_ref.shape
     hf = count // steps
     todo = late_fields(steps, 2 * hf)
-    packed, more = packed_reader(west_ref, east_ref, 0, blocks, tx)
+    packed, _ = packed_reader(west_ref, east_ref, 0, blocks, tx)
 
     def read(f, t):
         if f >= len(todo):
@@ -553,7 +608,7 @@
         ref, i = (far_ref, n * hf + q) if q < hf else (own_ref, n * hf + q - hf)
         return ref[i, t * SUB : (t + 1) * SUB, :]
 
-    send_rows(read, len(todo) + more, ty, north_ref, south_ref)
+    send_rows(read, with_packed(late_widths(steps, 2 * hf), blocks, tx, steps), ty, north_ref, south_ref)
 
 
 def late_kernel(
@@ -587,7 +642,8 @@
     @pl.when(flag_ref[0] != 0)
     def _():
         diff = ring_ref[...]
-        wests, easts = sides_with_rows(west_ref, east_ref, north_ref, south_ref, len(todo), 0, blocks, tx)
+        edge = edge_reader(north_ref, south_ref, with_packed(late_widths(steps, fields), blocks, tx, steps))
+        wests, easts = sides_with_rows(west_ref, east_ref, edge, len(todo), 0, blocks, tx)
         at = 0
         for n in range(steps):
             k = steps - 1 - n
@@ -595,7 +651,7 @@
                 r = read(n, q)
                 if k:
                     f = todo.index((n, q))
-                    r = with_ring(r, wests[f // per], easts[f // per], f, north_ref, south_ref, steps)
+                    r = with_ring(r, wests[f // per], easts[f // per], f, edge, steps)
                 for j in range(k + 1):
                     stack[at + j * fields + q] = r[:ty, :tx]
                     if j < k:
@@ -662,76 +718,91 @@
 
     count = (steps + 1) * hf
     coupling = jnp.swapaxes(coupling, 1, 2)
-    keep, send = call(
+    columns = struct(ty, -(-nc // per) * LANES)
+    keep, send, east, west = call(
         project_kernel,
-        [struct(count + 1, ty, tx), struct(count + 2 + steps * fields, ty, tx)],
+        [struct(count + 2, ty, tx), struct(count + 2 + steps * fields, ty, tx), columns, columns],
         adjoint_init, land_mask, diffusivity, history, mixing, extract, coupling,
-        hbm=(0, 1, 2, 3),
-        vmem=60,
+        hbm=tuple(range(7)),
         scratch=[
             pltpu.VMEM((nc, ty, tx), F32),
             pltpu.VMEM((ty, tx), jnp.int32),
-            pltpu.SemaphoreType.DMA((3 + steps,)),
+            pltpu.VMEM(mixing.shape, F32),
+            pltpu.VMEM(extract.shape, F32),
+            pltpu.VMEM(coupling.shape, F32),
+            pltpu.VMEM((-(-(steps + 1) * fields // SUB) * SUB, nc), F32),
+            pltpu.SemaphoreType.DMA((6 + steps,)),
         ],
     )
     got = lax.ppermute(send, "sect", [(0, 1), (1, 0)])
     places, halo_count = field_places(steps, hf)
     blocks = -(-halo_count // per)
-    far_at = count + 2
-    total = nc + 2 * (steps - 1) * fields + 2
-    state_blocks = -(-total // per)
+    total = 2 * (steps - 1) * fields + 2
+    state_blocks = -(-total // per) + -(-nc // per)
     side = struct(ty, (blocks + state_blocks) * LANES)
     main, east, west = call(
-        partial(force_kernel, places, halo_count),
+        partial(force_kernel, places, halo_count, steps, fields),
         [struct(len(places), ty, tx), side, side],
-        flag, keep, got, adjoint_init, history, diffusivity, land_mask,
+        flag, keep, send, got, east, west,
         smem=(0,),
     )
     from_west, from_east = exchange(east, west, "gx", True)
-    pairs = -(-(halo_count + -(-2 * blocks * LANES // tx)) // 2)
+    widths = with_packed(projected_widths(places, halo_count, steps), blocks, tx, hw)
     north, south = call(
-        partial(rows_kernel, halo_count, blocks),
-        [struct(pairs, SUB, tx)] * 2,
+        partial(rows_kernel, widths, blocks),
+        [struct(strip_places(widths)[1], SUB, tx)] * 2,
         main, from_west, from_east,
     )
     from_north, from_south = exchange(south, north, "gy", False)
     dest = atmos_tile_index.reshape(tiles, entries)
-    [sel] = call(
+    sel, weights = call(
         partial(select_kernel, cap, slots, nb),
-        [struct(tiles * cap, slots)],
-        tile.reshape(1), dest, ocean_block_index.reshape(tiles, entries),
+        [struct(tiles * cap, slots), struct(cells, cells)],
+        tile.reshape(1), dest, ocean_block_index.reshape(tiles, entries), regrid,
         smem=(0,),
     )
     [packed] = call(
-        partial(surface_kernel, places, halo_count, steps, hf),
+        partial(surface_kernel, places, halo_count, widths, steps, hf),
         [struct(tiles * cap, steps * hf * LANES)],
-        main, from_west, from_east, from_north, from_south, regrid, sel,
-    )
-    packed, adjoint_init, dest = lax.optimization_barrier((packed, adjoint_init, dest))
+        main, from_west, from_east, from_north, from_south, weights, sel,
+        hbm_out=True,
+        scratch=[pltpu.VMEM((tiles * cap, steps * hf * LANES), F32), pltpu.SemaphoreType.DMA((steps * hf,))],
+    )
+    widths = with_packed(state_widths(steps, fields, nc), state_blocks, tx, hw)
+    sizes = (steps, fields, blocks, state_blocks)
+    north, south = call(
+        partial(state_rows_kernel, *sizes),
+        [struct(strip_places(widths)[1], SUB, tx)] * 2,
+        flag, adjoint_init, send, got, keep, from_west, from_east,
+        smem=(0,),
+        hbm=(1,),
+        scratch=[pltpu.VMEM((2, nc, SUB, tx), F32), pltpu.SemaphoreType.DMA((2,))],
+    )
+    packed, dest, mixing, north, south = lax.optimization_barrier((packed, dest, mixing, north, south))
     arrived = lax.all_to_all(
         packed.reshape(tiles, cap, -1), ("gy", "gx"), split_axis=0, concat_axis=0, tiled=True
     ).reshape(tiles * cap, -1)
 
-    pairs = -(-(total + -(-2 * state_blocks * LANES // tx)) // 2)
-    north, south = call(
-        partial(state_rows_kernel, far_at, blocks, state_blocks),
-        [struct(pairs, SUB, tx)] * 2,
-        flag, adjoint_init, history, got, diffusivity, land_mask, from_west, from_east,
-        smem=(0,),
-    )
     from_north, from_south = exchange(south, north, "gy", False)
     terms = fields * steps * (steps + 1) // 2
     ext = (ty + SUB, tx + LANES)
-    base, ring, late = call(
-        partial(state_kernel, far_at, blocks, state_blocks),
-        [struct(nc, ty, tx), struct(*ext), struct(nc * SUB, terms * SUB)],
-        flag, adjoint_init, history, got, diffusivity, land_mask,
-        from_west, from_east, from_north, from_south, mixing, coupling,
+    mix8, coup8, late = call(
+        partial(matrices_kernel, steps, fields),
+        [struct(nc * SUB, nc * SUB), struct(nc * SUB, 2 * fields * SUB), struct(nc * SUB, terms * SUB)],
+        flag, mixing, coupling,
         smem=(0,),
+    )
+    base, ring = call(
+        partial(state_kernel, *sizes),
+        [struct(nc, ty, tx), struct(*ext)],
+        flag, adjoint_init, send, got, keep, from_west, from_east, from_north, from_south, mix8, coup8,
+        smem=(0,),
+        hbm=(1,),
         scratch=[
             pltpu.VMEM((nc, *ext), F32),
             pltpu.VMEM((steps, 2 * fields, *ext), F32),
             pltpu.VMEM((nc, *ext), F32),
+            pltpu.SemaphoreType.DMA,
         ],
     )
 
@@ -741,16 +812,15 @@
         tile.reshape(1), dest, atmos_block_index.reshape(tiles, entries),
         smem=(0,),
     )
-    arrived, base, acc = lax.optimization_barrier((arrived, base, acc))
-    [own] = call(gather_kernel, [struct(steps * hf, ty, tx)], acc, arrived)
+    [own] = call(gather_kernel, [struct(steps * hf, ty, tx)], acc, arrived, ring)
     far = lax.ppermute(own, "sect", [(0, 1)])
     halo_count = (steps - 1) * fields
     blocks = -(-halo_count // per)
     east, west = call(partial(late_columns_kernel, steps), [struct(ty, blocks * LANES)] * 2, own, far)
     from_west, from_east = exchange(east, west, "gx", True, 1)
-    pairs = -(-(halo_count + -(-2 * blocks * LANES // tx)) // 2)
+    widths = with_packed(late_widths(steps, fields), blocks, tx, hw)
     north, south = call(
-        partial(late_rows_kernel, steps, blocks), [struct(pairs, SUB, tx)] * 2, own, far, from_west, from_east
+        partial(late_rows_kernel, steps, blocks), [struct(strip_places(widths)[1], SUB, tx)] * 2, own, far, from_west, from_east
     )
     from_north, from_south = exchange(south, north, "gy", False, 1)
     [out] = call(

time: 103 us -> 88.3 us (0.86)
  local copies, waits for them, and re-layouts: 12 us -> 3.14 us
  waiting for transfers between devices: 28.7 us -> 22.7 us
    unnamed x64 -> x26, local copies, waits for them, and re-layouts: 12 us -> 3.14 us
    ppermute x6, waiting for transfers between devices: 17.6 us -> 12.9 us  [shifted(): return lax.ppermute(x, axis, pairs)]
    ppermute x4, waiting for transfers between devices: 5.58 us -> 4.26 us  [shifted(): lax.ppermute(x, ('sect', axis), [(base + i, base + j) for i, j in pairs])]
    pallas_call x12 -> x13, Pallas kernels: 27.7 us -> 27.8 us  [call(): pl.pallas_call(kernel, out_shape=[pltpu.HBM(o.shape, o.dtype) for o in ou...]
  transfers between devices with their start and end apart: 13 -> 13, of which waited for: 8 -> 8; matrix products, arithmetic and copies ran while one was open for 0% -> 0% of each run, Pallas kernels for 15% -> 21%
where the time goes in v2:
time: 88.3 us; the launch traced here: 87.7 us
  starting transfers between devices  33.7 us (38%)
  Pallas kernels  27.8 us (31%)
  waiting for transfers between devices  22.7 us (26%)
  local copies, waits for them, and re-layouts  3.14 us (4%)
    pallas_call x13, Pallas kernels, call(): pl.pallas_call(kernel, out_shape=[pltpu.HBM(o.shape, o.dtype) for o in ou...  27.8 us
    ppermute x6, starting transfers between devices, shifted(): return lax.ppermute(x, axis, pairs)  13.7 us
    ppermute x6, waiting for transfers between devices, shifted(): return lax.ppermute(x, axis, pairs)  12.9 us
    ppermute x4, starting transfers between devices, shifted(): lax.ppermute(x, ('sect', axis), [(base + i, base + j) for i, j in pairs])  12.5 us
    all_to_all x1, starting transfers between devices, body(): lax.all_to_all(packed.reshape(tiles, cap, -1), ('gy', 'gx'), split_axis=0...  5.96 us
    ppermute x4, waiting for transfers between devices, shifted(): lax.ppermute(x, ('sect', axis), [(base + i, base + j) for i, j in pairs])  4.26 us
    unnamed x26, local copies, waits for them, and re-layouts  3.14 us
    ppermute x1, waiting for transfers between devices, body(): far = lax.ppermute(own, 'sect', [(0, 1)])  3.11 us
  transfers between devices with their start and end apart: 13, of which 8 were waited for; matrix products, arithmetic and copies ran while one was open for 0% of the time, Pallas kernels for 21%

profile of v2, /device:TPU:1, one launch (start us, length us, event | category | flops | bytes accessed | tf_op | source)
XLA Modules:
  0.0 87.7 jit_solution(16230865642196283744)
XLA Ops:
  0.0 2.9 %shard_map.109 = (f32[12,32,256]{2,1,0:T(8,128)S(1)}, f32[28,32,256]{2,1,0:T(8,128)S(1)}, f32[32,128]{1,0:T(8,128)S(1)}, f32[32,128]{1,0:T(8,128)S(1)}) custom-call(f32[1,32,32,256]{3,2,1,0:T(8,128)} %refs_1_.4, s32[32,256]{1,0:T(8,128)} %mask_hbm.1, f32[1,32,256]{2,1,0:T(8,128)} %diff_hbm.1, f32[1,4,4,32,256]{4,3,2,1,0:T(8,128)} %hist_hbm.1, ...), custom_call_target="tpu_custom_call" | custom-call | bytes 2987520 | tf_op jit(solution)/shard_map/pallas_call | solution.py:201
  2.9 0.1 collective-permute-start
  3.0 2.4 %collective-permute-done.refs_3_ = f32[28,32,256]{2,1,0:T(8,128)S(1)} collective-permute-done((f32[28,32,256]{2,1,0:T(8,128)S(1)}, f32[28,32,256]{2,1,0:T(8,128)S(1)}, u32[]{:S(2)}, u32[]{:S(2)}) %collective-permute-start) | collective-permute-done | bytes 917536 | tf_op jit(solution)/shard_map/ppermute | solution.py:737
  5.5 0.5 shard_map.110
  6.0 2.5 %collective-permute-start.1 = (f32[32,384]{1,0:T(8,128)S(1)}, f32[32,384]{1,0:T(8,128)S(1)}, u32[]{:S(2)}, u32[]{:S(2)}) collective-permute-start(f32[32,384]{1,0:T(8,128)S(1)} %get-tuple-element.36), channel_id=1, source_target_pairs={{0,1},{1,2},{2,3},{3,0},{4,5},{5,6},{6,7},{7,4},{8,9},{9,10},{10,1... | collective-permute-start | bytes 147464 | tf_op jit(solution)/shard_map/ppermute | solution.py:672
  8.5 2.1 %collective-permute-start.2 = (f32[32,384]{1,0:T(8,128)S(1)}, f32[32,384]{1,0:T(8,128)S(1)}, u32[]{:S(2)}, u32[]{:S(2)}) collective-permute-start(f32[32,384]{1,0:T(8,128)S(1)} %get-tuple-element.37), channel_id=1, source_target_pairs={{0,3},{1,0},{2,1},{3,2},{4,7},{5,4},{6,5},{7,6},{8,11},{9,8},{10,9... | collective-permute-start | bytes 147464 | tf_op jit(solution)/shard_map/ppermute | solution.py:672
  10.6 1.4 %collective-permute-done.1.refs_1_.refs_5_ = f32[32,384]{1,0:T(8,128)S(1)} collective-permute-done((f32[32,384]{1,0:T(8,128)S(1)}, f32[32,384]{1,0:T(8,128)S(1)}, u32[]{:S(2)}, u32[]{:S(2)}) %collective-permute-start.1) | collective-permute-done | bytes 49184 | tf_op jit(solution)/shard_map/ppermute | solution.py:672
  12.0 0.0 collective-permute-done.2.refs_2_.refs_6_
  12.0 0.7 shard_map.111
  12.7 3.1 %collective-permute-start.3 = (f32[7,8,256]{2,1,0:T(8,128)}, f32[7,8,256]{2,1,0:T(8,128)S(1)}, u32[]{:S(2)}, u32[]{:S(2)}) collective-permute-start(f32[7,8,256]{2,1,0:T(8,128)} %get-tuple-element.39), channel_id=1, source_target_pairs={{0,4},{4,8},{8,12},{1,5},{5,9},{9,13},{2,6},{6,10},{10,14},{3,7},{... | collective-permute-start | bytes 172040 | tf_op jit(solution)/shard_map/ppermute | solution.py:672
  15.8 1.3 %collective-permute-start.4 = (f32[7,8,256]{2,1,0:T(8,128)}, f32[7,8,256]{2,1,0:T(8,128)S(1)}, u32[]{:S(2)}, u32[]{:S(2)}) collective-permute-start(f32[7,8,256]{2,1,0:T(8,128)} %get-tuple-element.40), channel_id=1, source_target_pairs={{4,0},{8,4},{12,8},{5,1},{9,5},{13,9},{6,2},{10,6},{14,10},{7,3},{... | collective-permute-start | bytes 172040 | tf_op jit(solution)/shard_map/ppermute | solution.py:672
  17.1 0.0 copy-start.6
  17.1 0.7 copy-done.6
  17.8 0.7 copy-done.9
  18.5 0.2 shard_map.112
  18.7 1.1 %shard_map.114 = (f32[24,8,256]{2,1,0:T(8,128)S(1)}, f32[24,8,256]{2,1,0:T(8,128)S(1)}) custom-call(s32[1]{0:T(128)} %bitcast.refs_0_, f32[1,32,32,256]{3,2,1,0:T(8,128)} %refs_1_.4, f32[28,32,256]{2,1,0:T(8,128)S(1)} %get-tuple-element.32.refs_2_, f32[28,32,256]{2,1,0:T(8,128)S(1)} %collective-permute-done.refs_3_, ...), custom_call_target="tpu_custom_call" | custom-call | bytes 3768324 | tf_op jit(solution)/shard_map/pallas_call | solution.py:201
  19.9 0.0 copy-start.12
  19.9 0.0 collective-permute-done.3.refs_3_
  19.9 1.6 %collective-permute-done.4.refs_4_ = f32[7,8,256]{2,1,0:T(8,128)S(1)} collective-permute-done((f32[7,8,256]{2,1,0:T(8,128)}, f32[7,8,256]{2,1,0:T(8,128)S(1)}, u32[]{:S(2)}, u32[]{:S(2)}) %collective-permute-start.4) | collective-permute-done | bytes 57376 | tf_op jit(solution)/shard_map/ppermute | solution.py:672
  21.5 2.2 %shard_map.113 = f32[256,1024]{1,0:T(8,128)} custom-call(f32[32,32,256]{2,1,0:T(8,128)S(1)} %get-tuple-element.38.refs_0_, f32[32,384]{1,0:T(8,128)S(1)} %collective-permute-done.1.refs_1_.refs_5_, f32[32,384]{1,0:T(8,128)S(1)} %collective-permute-done.2.refs_2_.refs_6_, f32[7,8,256]{2,1,0:T(8,128)S(1)} %collective-permute-done.3.refs_3_, ...), custom_call_target="tpu_custom_call" | custom-call | bytes 2441216 | tf_op jit(solution)/shard_map/pallas_call | solution.py:201
  23.7 0.0 copy-start.4
  23.8 0.0 copy-start.8
  23.8 6.0 %all-to-all-start = ((f32[16,16,1024]{2,1,0:T(8,128)}), f32[16,16,1024]{2,1,0:T(8,128)S(1)}, u32[]{:S(2)}, u32[]{:S(2)}) async-start(f32[16,16,1024]{2,1,0:T(8,128)} %bitcast.15), calls=%async_computation | async-start | bytes 2097152 | tf_op jit(solution)/shard_map/all_to_all | solution.py:782
  29.7 0.0 copy-start.7
  29.7 0.0 copy-start.10
  29.8 3.3 %collective-permute-start.5 = (f32[24,8,256]{2,1,0:T(8,128)}, f32[24,8,256]{2,1,0:T(8,128)S(1)}, u32[]{:S(2)}, u32[]{:S(2)}) collective-permute-start(f32[24,8,256]{2,1,0:T(8,128)} %copy-done.12), channel_id=1, source_target_pairs={{0,4},{4,8},{8,12},{1,5},{5,9},{9,13},{2,6},{6,10},{10,14},{3,7},{... | collective-permute-start | bytes 589832 | tf_op jit(solution)/shard_map/ppermute | solution.py:672
  33.0 1.5 %collective-permute-start.6 = (f32[24,8,256]{2,1,0:T(8,128)}, f32[24,8,256]{2,1,0:T(8,128)S(1)}, u32[]{:S(2)}, u32[]{:S(2)}) collective-permute-start(f32[24,8,256]{2,1,0:T(8,128)} %copy-done.11), channel_id=1, source_target_pairs={{4,0},{8,4},{12,8},{5,1},{9,5},{13,9},{6,2},{10,6},{14,10},{7,3},{... | collective-permute-start | bytes 589832 | tf_op jit(solution)/shard_map/ppermute | solution.py:672
  34.5 2.8 %shard_map.115 = (f32[256,256]{1,0:T(8,128)S(1)}, f32[256,64]{1,0:T(8,128)S(1)}, f32[256,320]{1,0:T(8,128)S(1)}) custom-call(s32[1]{0:T(128)} %bitcast.refs_0_, f32[1,32,32]{2,1,0:T(8,128)S(1)} %copy-done.4, f32[1,8,32]{2,1,0:T(8,128)S(1)} %bitcast.12), custom_call_target="tpu_custom_call" | custom-call | bytes 660484 | tf_op jit(solution)/shard_map/pallas_call | solution.py:201
  37.4 0.7 copy-done.2
  38.1 2.2 %shard_map.117.acc_ref = f32[64,256]{1,0:T(8,128)S(1)} custom-call(s32[1]{0:T(128)} %bitcast.2.refs_0_, s32[16,128]{1,0:T(8,128)S(1)} %bitcast.10, s32[16,128]{1,0:T(8,128)S(1)} %bitcast.14), custom_call_target="tpu_custom_call" | custom-call | bytes 81924 | tf_op jit(solution)/shard_map/pallas_call | solution.py:201
  40.3 1.4 %collective-permute-done.5.refs_7_ = f32[24,8,256]{2,1,0:T(8,128)S(1)} collective-permute-done((f32[24,8,256]{2,1,0:T(8,128)}, f32[24,8,256]{2,1,0:T(8,128)S(1)}, u32[]{:S(2)}, u32[]{:S(2)}) %collective-permute-start.5) | collective-permute-done | bytes 196640 | tf_op jit(solution)/shard_map/ppermute | solution.py:672
  41.7 8.5 %collective-permute-done.6.refs_8_ = f32[24,8,256]{2,1,0:T(8,128)S(1)} collective-permute-done((f32[24,8,256]{2,1,0:T(8,128)}, f32[24,8,256]{2,1,0:T(8,128)S(1)}, u32[]{:S(2)}, u32[]{:S(2)}) %collective-permute-start.6) | collective-permute-done | bytes 196640 | tf_op jit(solution)/shard_map/ppermute | solution.py:672
  50.2 11.7 %shard_map.116 = (f32[32,32,256]{2,1,0:T(8,128)S(1)}, f32[40,384]{1,0:T(8,128)S(1)}) custom-call(s32[1]{0:T(128)} %bitcast.refs_0_, f32[1,32,32,256]{3,2,1,0:T(8,128)} %refs_1_.4, f32[28,32,256]{2,1,0:T(8,128)S(1)} %get-tuple-element.32.refs_2_, f32[28,32,256]{2,1,0:T(8,128)S(1)} %collective-permute-done.refs_3_, ...), custom_call_target="tpu_custom_call" | custom-call | bytes 5206020 | tf_op jit(solution)/shard_map/pallas_call | solution.py:201
  62.0 0.0 copy-start
  62.0 1.0 %copy-done = f32[32,32,256]{2,1,0:T(8,128)} copy-done((f32[32,32,256]{2,1,0:T(8,128)}, f32[32,32,256]{2,1,0:T(8,128)S(1)}, u32[]{:S(2)}) %copy-start) | copy-done | bytes 1048600
  62.9 0.0 all-to-all-done
  62.9 0.3 shard_map.118.refs_0_.refs_4_
  63.2 1.4 %collective-permute-start.7 = (f32[8,32,256]{2,1,0:T(8,128)S(1)}, f32[8,32,256]{2,1,0:T(8,128)S(1)}, u32[]{:S(2)}, u32[]{:S(2)}) collective-permute-start(f32[8,32,256]{2,1,0:T(8,128)S(1)} %shard_map.118.refs_0_.refs_4_), channel_id=1, source_target_pairs={{0,16},{1,17},{2,18},{3,19},{4,20},{5,21},{6,22},{7,23},{8,24},{9,... | collective-permute-start | bytes 786440 | tf_op jit(solution)/shard_map/ppermute | solution.py:816
  64.7 3.1 %collective-permute-done.7.refs_1_.refs_5_ = f32[8,32,256]{2,1,0:T(8,128)S(1)} collective-permute-done((f32[8,32,256]{2,1,0:T(8,128)S(1)}, f32[8,32,256]{2,1,0:T(8,128)S(1)}, u32[]{:S(2)}, u32[]{:S(2)}) %collective-permute-start.7) | collective-permute-done | bytes 262176 | tf_op jit(solution)/shard_map/ppermute | solution.py:816
  67.8 0.2 shard_map.119
  68.0 4.2 %collective-permute-start.8 = (f32[32,128]{1,0:T(8,128)S(1)}, f32[32,128]{1,0:T(8,128)S(1)}, u32[]{:S(2)}, u32[]{:S(2)}) collective-permute-start(f32[32,128]{1,0:T(8,128)S(1)} %get-tuple-element.55), channel_id=1, source_target_pairs={{16,17},{17,18},{18,19},{19,16},{20,21},{21,22},{22,23},{23,20},{2... | collective-permute-start | bytes 49160 | tf_op jit(solution)/shard_map/ppermute | solution.py:674
  72.2 3.6 %collective-permute-start.9 = (f32[32,128]{1,0:T(8,128)S(1)}, f32[32,128]{1,0:T(8,128)S(1)}, u32[]{:S(2)}, u32[]{:S(2)}) collective-permute-start(f32[32,128]{1,0:T(8,128)S(1)} %get-tuple-element.56), channel_id=1, source_target_pairs={{16,19},{17,16},{18,17},{19,18},{20,23},{21,20},{22,21},{23,22},{2... | collective-permute-start | bytes 49160 | tf_op jit(solution)/shard_map/ppermute | solution.py:674
  75.7 0.0 collective-permute-done.8.refs_2_.refs_6_
  75.7 0.9 %collective-permute-done.9.refs_3_.refs_7_ = f32[32,128]{1,0:T(8,128)S(1)} collective-permute-done((f32[32,128]{1,0:T(8,128)S(1)}, f32[32,128]{1,0:T(8,128)S(1)}, u32[]{:S(2)}, u32[]{:S(2)}) %collective-permute-start.9) | collective-permute-done | bytes 16416 | tf_op jit(solution)/shard_map/ppermute | solution.py:674
  76.7 3.5 %collective-permute-start.10 = (f32[4,8,256]{2,1,0:T(8,128)S(1)}, f32[4,8,256]{2,1,0:T(8,128)S(1)}, u32[]{:S(2)}, u32[]{:S(2)}) collective-permute-start(f32[4,8,256]{2,1,0:T(8,128)S(1)} %get-tuple-element.57), channel_id=1, source_target_pairs={{16,20},{20,24},{24,28},{17,21},{21,25},{25,29},{18,22},{22,26},{2... | collective-permute-start | bytes 98312 | tf_op jit(solution)/shard_map/ppermute | solution.py:674
  80.1 1.3 %collective-permute-start.11 = (f32[4,8,256]{2,1,0:T(8,128)S(1)}, f32[4,8,256]{2,1,0:T(8,128)S(1)}, u32[]{:S(2)}, u32[]{:S(2)}) collective-permute-start(f32[4,8,256]{2,1,0:T(8,128)S(1)} %get-tuple-element.58), channel_id=1, source_target_pairs={{20,16},{24,20},{28,24},{21,17},{25,21},{29,25},{22,18},{26,22},{3... | collective-permute-start | bytes 98312 | tf_op jit(solution)/shard_map/ppermute | solution.py:674
  81.4 3.3 %collective-permute-done.11.refs_9_ = f32[4,8,256]{2,1,0:T(8,128)S(1)} collective-permute-done((f32[4,8,256]{2,1,0:T(8,128)S(1)}, f32[4,8,256]{2,1,0:T(8,128)S(1)}, u32[]{:S(2)}, u32[]{:S(2)}) %collective-permute-start.11) | collective-permute-done | bytes 32800 | tf_op jit(solution)/shard_map/ppermute | solution.py:674
  84.8 2.9 %shard_map.121 = f32[1,32,32,256]{3,2,1,0:T(8,128)} custom-call(s32[1]{0:T(128)} %bitcast.refs_0_, f32[32,32,256]{2,1,0:T(8,128)S(1)} %copy-done.1, f32[40,384]{1,0:T(8,128)S(1)} %get-tuple-element.51.after_ref.refs_2_, f32[256,320]{1,0:T(8,128)S(1)} %copy-done.3, f32[8,32,256]{2,1,0:T(8,128)S(1)} %shard_map.118.refs_0_.refs_4_, ...), custom_call_target="tpu_custom_call" | custom-call | bytes 3108868 | tf_op jit(solution)/shard_map/pallas_call | solution.py:201
  (17 shorter events, 0.0 us)
Async XLA Ops:
  2.9 2.5 %collective-permute-start = (f32[28,32,256]{2,1,0:T(8,128)S(1)}, f32[28,32,256]{2,1,0:T(8,128)S(1)}, u32[]{:S(2)}, u32[]{:S(2)}) collective-permute-start(f32[28,32,256]{2,1,0:T(8,128)S(1)} %get-tuple-element.32.refs_2_), channel_id=1, source_target_pairs={{0,16},{16,0},{1,17},{17,1},{2,18},{18,2},{3,19},{19,3},{4,20},{20... | collective-permute-start | bytes 2752520 | tf_op jit(solution)/shard_map/ppermute | solution.py:737
  6.0 6.0 %collective-permute-start.1 = (f32[32,384]{1,0:T(8,128)S(1)}, f32[32,384]{1,0:T(8,128)S(1)}, u32[]{:S(2)}, u32[]{:S(2)}) collective-permute-start(f32[32,384]{1,0:T(8,128)S(1)} %get-tuple-element.36), channel_id=1, source_target_pairs={{0,1},{1,2},{2,3},{3,0},{4,5},{5,6},{6,7},{7,4},{8,9},{9,10},{10,1... | collective-permute-start | bytes 147464 | tf_op jit(solution)/shard_map/ppermute | solution.py:672
  8.5 3.5 %collective-permute-start.2 = (f32[32,384]{1,0:T(8,128)S(1)}, f32[32,384]{1,0:T(8,128)S(1)}, u32[]{:S(2)}, u32[]{:S(2)}) collective-permute-start(f32[32,384]{1,0:T(8,128)S(1)} %get-tuple-element.37), channel_id=1, source_target_pairs={{0,3},{1,0},{2,1},{3,2},{4,7},{5,4},{6,5},{7,6},{8,11},{9,8},{10,9... | collective-permute-start | bytes 147464 | tf_op jit(solution)/shard_map/ppermute | solution.py:672
  12.0 5.1 %copy-start.5 = (f32[1,128,128]{2,1,0:T(8,128)S(1)}, f32[1,128,128]{2,1,0:T(8,128)}, u32[]{:S(2)}) copy-start(f32[1,128,128]{2,1,0:T(8,128)} %refs_3_.1) | copy-start | bytes 196612
  12.7 7.2 %collective-permute-start.3 = (f32[7,8,256]{2,1,0:T(8,128)}, f32[7,8,256]{2,1,0:T(8,128)S(1)}, u32[]{:S(2)}, u32[]{:S(2)}) collective-permute-start(f32[7,8,256]{2,1,0:T(8,128)} %get-tuple-element.39), channel_id=1, source_target_pairs={{0,4},{4,8},{8,12},{1,5},{5,9},{9,13},{2,6},{6,10},{10,14},{3,7},{... | collective-permute-start | bytes 172040 | tf_op jit(solution)/shard_map/ppermute | solution.py:672
  15.8 5.7 %collective-permute-start.4 = (f32[7,8,256]{2,1,0:T(8,128)}, f32[7,8,256]{2,1,0:T(8,128)S(1)}, u32[]{:S(2)}, u32[]{:S(2)}) collective-permute-start(f32[7,8,256]{2,1,0:T(8,128)} %get-tuple-element.40), channel_id=1, source_target_pairs={{4,0},{8,4},{12,8},{5,1},{9,5},{13,9},{6,2},{10,6},{14,10},{7,3},{... | collective-permute-start | bytes 172040 | tf_op jit(solution)/shard_map/ppermute | solution.py:672
  17.1 0.7 copy-start.6
  17.8 0.7 copy-start.9
  19.9 3.9 %copy-start.11 = (f32[24,8,256]{2,1,0:T(8,128)}, f32[24,8,256]{2,1,0:T(8,128)S(1)}, u32[]{:S(2)}) copy-start(f32[24,8,256]{2,1,0:T(8,128)S(1)} %get-tuple-element.46) | copy-start | bytes 589828
  19.9 3.9 %copy-start.12 = (f32[24,8,256]{2,1,0:T(8,128)}, f32[24,8,256]{2,1,0:T(8,128)S(1)}, u32[]{:S(2)}) copy-start(f32[24,8,256]{2,1,0:T(8,128)S(1)} %get-tuple-element.45) | copy-start | bytes 589828
  23.7 10.8 %copy-start.4 = (f32[1,32,32]{2,1,0:T(8,128)S(1)}, f32[1,32,32]{2,1,0:T(8,128)}, u32[]{:S(2)}) copy-start(f32[1,32,32]{2,1,0:T(8,128)} %refs_1_.3) | copy-start | bytes 12292
  23.8 10.8 %copy-start.8 = (f32[1,32,8]{1,2,0:T(8,128)S(1)}, f32[1,32,8]{1,2,0:T(8,128)}, u32[]{:S(2)}) copy-start(f32[1,32,8]{1,2,0:T(8,128)} %param.14) | copy-start | bytes 3076
  23.8 39.2 %all-to-all-start = ((f32[16,16,1024]{2,1,0:T(8,128)}), f32[16,16,1024]{2,1,0:T(8,128)S(1)}, u32[]{:S(2)}, u32[]{:S(2)}) async-start(f32[16,16,1024]{2,1,0:T(8,128)} %bitcast.15), calls=%async_computation | async-start | bytes 2097152 | tf_op jit(solution)/shard_map/all_to_all | solution.py:782
  29.7 8.4 %copy-start.7 = (s32[2048,1]{0,1:T(1,128)S(1)}, s32[2048,1]{0,1:T(1,128)}, u32[]{:S(2)}) copy-start(s32[2048,1]{0,1:T(1,128)} %param.19) | copy-start | bytes 24580
  29.7 8.4 %copy-start.10 = (s32[2048]{0:T(1024)S(1)}, s32[2048]{0:T(1024)}, u32[]{:S(2)}) copy-start(s32[2048]{0:T(1024)} %param.21) | copy-start | bytes 24580
  29.8 11.9 %collective-permute-start.5 = (f32[24,8,256]{2,1,0:T(8,128)}, f32[24,8,256]{2,1,0:T(8,128)S(1)}, u32[]{:S(2)}, u32[]{:S(2)}) collective-permute-start(f32[24,8,256]{2,1,0:T(8,128)} %copy-done.12), channel_id=1, source_target_pairs={{0,4},{4,8},{8,12},{1,5},{5,9},{9,13},{2,6},{6,10},{10,14},{3,7},{... | collective-permute-start | bytes 589832 | tf_op jit(solution)/shard_map/ppermute | solution.py:672
  33.0 17.2 %collective-permute-start.6 = (f32[24,8,256]{2,1,0:T(8,128)}, f32[24,8,256]{2,1,0:T(8,128)S(1)}, u32[]{:S(2)}, u32[]{:S(2)}) collective-permute-start(f32[24,8,256]{2,1,0:T(8,128)} %copy-done.11), channel_id=1, source_target_pairs={{4,0},{8,4},{12,8},{5,1},{9,5},{13,9},{6,2},{10,6},{14,10},{7,3},{... | collective-permute-start | bytes 589832 | tf_op jit(solution)/shard_map/ppermute | solution.py:672
  37.4 0.8 copy-start.2
  62.0 1.0 %copy-start = (f32[32,32,256]{2,1,0:T(8,128)}, f32[32,32,256]{2,1,0:T(8,128)S(1)}, u32[]{:S(2)}) copy-start(f32[32,32,256]{2,1,0:T(8,128)S(1)} %get-tuple-element.50.refs_1_) | copy-start | bytes 3145732
  62.9 21.9 %copy-start.1 = (f32[32,32,256]{2,1,0:T(8,128)S(1)}, f32[32,32,256]{2,1,0:T(8,128)}, u32[]{:S(2)}) copy-start(f32[32,32,256]{2,1,0:T(8,128)} %copy-done) | copy-start | bytes 3145732
  63.2 4.5 %collective-permute-start.7 = (f32[8,32,256]{2,1,0:T(8,128)S(1)}, f32[8,32,256]{2,1,0:T(8,128)S(1)}, u32[]{:S(2)}, u32[]{:S(2)}) collective-permute-start(f32[8,32,256]{2,1,0:T(8,128)S(1)} %shard_map.118.refs_0_.refs_4_), channel_id=1, source_target_pairs={{0,16},{1,17},{2,18},{3,19},{4,20},{5,21},{6,22},{7,23},{8,24},{9,... | collective-permute-start | bytes 786440 | tf_op jit(solution)/shard_map/ppermute | solution.py:816
  68.0 16.8 %copy-start.3 = (f32[256,320]{1,0:T(8,128)S(1)}, f32[256,320]{1,0:T(8,128)}, u32[]{:S(2)}) copy-start(f32[256,320]{1,0:T(8,128)} %copy-done.2) | copy-start | bytes 983044
  68.0 7.8 %collective-permute-start.8 = (f32[32,128]{1,0:T(8,128)S(1)}, f32[32,128]{1,0:T(8,128)S(1)}, u32[]{:S(2)}, u32[]{:S(2)}) collective-permute-start(f32[32,128]{1,0:T(8,128)S(1)} %get-tuple-element.55), channel_id=1, source_target_pairs={{16,17},{17,18},{18,19},{19,16},{20,21},{21,22},{22,23},{23,20},{2... | collective-permute-start | bytes 49160 | tf_op jit(solution)/shard_map/ppermute | solution.py:674
  72.2 4.5 %collective-permute-start.9 = (f32[32,128]{1,0:T(8,128)S(1)}, f32[32,128]{1,0:T(8,128)S(1)}, u32[]{:S(2)}, u32[]{:S(2)}) collective-permute-start(f32[32,128]{1,0:T(8,128)S(1)} %get-tuple-element.56), channel_id=1, source_target_pairs={{16,19},{17,16},{18,17},{19,18},{20,23},{21,20},{22,21},{23,22},{2... | collective-permute-start | bytes 49160 | tf_op jit(solution)/shard_map/ppermute | solution.py:674
  76.7 4.8 %collective-permute-start.10 = (f32[4,8,256]{2,1,0:T(8,128)S(1)}, f32[4,8,256]{2,1,0:T(8,128)S(1)}, u32[]{:S(2)}, u32[]{:S(2)}) collective-permute-start(f32[4,8,256]{2,1,0:T(8,128)S(1)} %get-tuple-element.57), channel_id=1, source_target_pairs={{16,20},{20,24},{24,28},{17,21},{21,25},{25,29},{18,22},{22,26},{2... | collective-permute-start | bytes 98312 | tf_op jit(solution)/shard_map/ppermute | solution.py:674
  80.1 4.7 %collective-permute-start.11 = (f32[4,8,256]{2,1,0:T(8,128)S(1)}, f32[4,8,256]{2,1,0:T(8,128)S(1)}, u32[]{:S(2)}, u32[]{:S(2)}) collective-permute-start(f32[4,8,256]{2,1,0:T(8,128)S(1)} %get-tuple-element.58), channel_id=1, source_target_pairs={{20,16},{24,20},{28,24},{21,17},{25,21},{29,25},{22,18},{26,22},{3... | collective-permute-start | bytes 98312 | tf_op jit(solution)/shard_map/ppermute | solution.py:674

commit v3 on v2

--- a/solution.py
+++ b/solution.py
@@ -204,7 +204,7 @@
         in_specs=[pl.BlockSpec(memory_space=space(i)) for i in range(len(args))],
         out_specs=[pl.BlockSpec(memory_space=pltpu.HBM if hbm_out else pltpu.VMEM) for _ in outs],
         scratch_shapes=scratch,
-        compiler_params=pltpu.CompilerParams(vmem_limit_bytes=48 * 2**20),
+        compiler_params=pltpu.CompilerParams(vmem_limit_bytes=24 * 2**20),
         cost_estimate=pl.CostEstimate(flops=flops, bytes_accessed=nbytes, transcendentals=0),
     )(*args)
 
@@ -293,7 +293,7 @@
 
 def force_kernel(
     places, halo_count, steps, fields, flag_ref, keep_ref, send_ref, got_ref, adj_east_ref, adj_west_ref,
-    main_ref, east_ref, west_ref,
+    sel_ref, main_ref, east_ref, west_ref,
 ):
     _, ty, tx = main_ref.shape
     hf, hw = fields // 2, steps
@@ -361,15 +361,24 @@
     return row < lax.broadcasted_iota(jnp.int32, (entries, entries), 1)
 
 
-def select_kernel(cap, slots, nb, pos_ref, dest_ref, src_ref, regrid_ref, sel_ref, weights_ref):
+def select_kernel(
+    cap, slots, nb, pos_ref, dest_hbm, src_hbm, regrid_hbm, sel_ref, weights_ref, dest_ref, src_ref, sems
+):
     tiles, entries = dest_ref.shape
+    copies = [
+        pltpu.make_async_copy(a, b, sems.at[i])
+        for i, (a, b) in enumerate(((dest_hbm, dest_ref), (src_hbm, src_ref), (regrid_hbm.at[0], weights_ref)))
+    ]
+    for copy in copies:
+        copy.start()
+    for copy in copies:
+        copy.wait()
     tile = pos_ref[0]
     dest = dest_ref[pl.ds(tile, 1), :]
     across = jnp.broadcast_to(dest.astype(F32), (entries, entries))
     same = (across == across.T) & earlier(entries)
     rank = jnp.sum(same.astype(F32), axis=0, keepdims=True).astype(jnp.int32)
     source = block_place(slots, nb)(src_ref[pl.ds(tile, 1), :])
-    weights_ref[...] = regrid_ref[0]
     sel_ref[...] = bf_dot(onehot(tiles * cap, dest * cap + rank), onehot(slots, source), LAST)
 
 
@@ -428,14 +437,27 @@
         copy.wait()
 
 
-def gather_kernel(acc_ref, in_ref, after_ref, out_ref):
+def gather_kernel(steps, flag_ref, acc_ref, in_ref, after_ref, out_ref, east_ref, west_ref):
     count, ty, tx = out_ref.shape
+    hf = count // steps
     acc = acc_ref[...].astype(BF16)
     for i in range(count):
         high, low = halves(in_ref[:, i * LANES : (i + 1) * LANES])
         total = bf_dot(acc, high) + bf_dot(acc, low)
         for l in range(tx // LANES):
             out_ref[i, :, l * LANES : (l + 1) * LANES] = total[l * ty : (l + 1) * ty]
+    todo = late_fields(steps, 2 * hf)
+
+    def read(f, l):
+        n, q = todo[f]
+        return out_ref[n * hf + q, :, l * LANES : (l + 1) * LANES] if q < hf else jnp.zeros((ty, LANES), F32)
+
+    store_columns(read, len(todo), tx, steps, east_ref, west_ref, 0)
+
+    @pl.when(flag_ref[0] != 0)
+    def _():
+        for ref in (east_ref, west_ref):
+            ref[...] = pltpu.roll(ref[...], hf * steps, 1)
 
 
 def forced_reader(steps, fields, flag_ref, send_ref, got_ref, keep_ref):
@@ -552,7 +574,7 @@
             spread[c] = ring_lap(diff * u)
             return carry
 
-        lax.fori_loop(0, nc, one, 0, unroll=8)
+        lax.fori_loop(0, nc, one, 0, unroll=True)
         for places in main if small else main + halo:
             spots = [(slice(g * SUB, (g + 1) * SUB), slice(c, c + w)) for g, c, w in places]
             u = jnp.concatenate([state[:, rs, cs].reshape(nc * SUB, -1) for rs, cs in spots], axis=1)
@@ -579,23 +601,11 @@
     return read
 
 
-def late_columns_kernel(steps, own_ref, far_ref, east_ref, west_ref):
-    count, ty, tx = own_ref.shape
-    hf = count // steps
-    todo = late_fields(steps, 2 * hf)
-
-    def read(f, l):
-        n, q = todo[f]
-        ref, i = (far_ref, n * hf + q) if q < hf else (own_ref, n * hf + q - hf)
-        return ref[i, :, l * LANES : (l + 1) * LANES]
-
-    east, west = pack_columns(read, len(todo), ty, tx, steps)
-    for block, (e, w) in enumerate(zip(east, west)):
-        east_ref[:, block * LANES : (block + 1) * LANES] = e
-        west_ref[:, block * LANES : (block + 1) * LANES] = w
-
-
-def late_rows_kernel(steps, blocks, own_ref, far_ref, west_ref, east_ref, north_ref, south_ref):
+def late_rows_kernel(
+    steps, blocks, own_ref, far_ref, west0_ref, west1_ref, east0_ref, east1_ref, north_ref, south_ref, west_ref, east_ref
+):
+    west_ref[...] = west0_ref[...] + west1_ref[...]
+    east_ref[...] = east0_ref[...] + east1_ref[...]
     count, ty, tx = own_ref.shape
     hf = count // steps
     todo = late_fields(steps, 2 * hf)
@@ -612,20 +622,8 @@
 
 
 def late_kernel(
-    steps,
-    blocks,
-    flag_ref,
-    base_ref,
-    ring_ref,
-    late_ref,
-    own_ref,
-    far_ref,
-    west_ref,
-    east_ref,
-    north_ref,
-    south_ref,
-    out_ref,
-    stack,
+    steps, blocks, flag_ref, base_ref, ring_ref, late_ref, own_ref, far_ref, west_ref, east_ref, north_ref, south_ref,
+    out_ref, stack,
 ):
     count, ty, tx = own_ref.shape
     hf = count // steps
@@ -659,19 +657,18 @@
             at += (k + 1) * fields
         big = halves(late_ref[...])
         for g in range(ty // SUB):
-            for l in range(tx // LANES):
-                rs, cs = slice(g * SUB, (g + 1) * SUB), slice(l * LANES, (l + 1) * LANES)
-                more = dot3(big, halves(stack[:, rs, cs].reshape(-1, LANES)))
-                out_ref[0, :, rs, cs] = base_ref[:, rs, cs] + more.reshape(nc, SUB, LANES)
-
-
-def shifted(x, axis, by, wrap, sect=None):
+            rs = slice(g * SUB, (g + 1) * SUB)
+            more = dot3(big, halves(stack[:, rs, :].reshape(-1, tx)))
+            out_ref[0, :, rs, :] = base_ref[:, rs, :] + more.reshape(nc, SUB, tx)
+
+
+def shifted(x, axis, by, wrap, sects=None):
     size = lax.axis_size(axis)
     pairs = [(i, (i + by) % size) for i in range(size) if wrap or 0 <= i + by < size]
-    if sect is None:
+    if sects is None:
         return lax.ppermute(x, axis, pairs)
-    base = sect * size
-    return lax.ppermute(x, ("sect", axis), [(base + i, base + j) for i, j in pairs])
+    a, b = sects
+    return lax.ppermute(x, ("sect", axis), [(a * size + i, b * size + j) for i, j in pairs])
 
 
 def struct(*shape):
@@ -735,6 +732,15 @@
         ],
     )
     got = lax.ppermute(send, "sect", [(0, 1), (1, 0)])
+    dest = atmos_tile_index.reshape(tiles, entries)
+    sel, weights = call(
+        partial(select_kernel, cap, slots, nb),
+        [struct(tiles * cap, slots), struct(cells, cells)],
+        tile.reshape(1), dest, ocean_block_index.reshape(tiles, entries), regrid,
+        smem=(0,),
+        hbm=(1, 2, 3),
+        scratch=[pltpu.VMEM((tiles, entries), jnp.int32)] * 2 + [pltpu.SemaphoreType.DMA((3,))],
+    )
     places, halo_count = field_places(steps, hf)
     blocks = -(-halo_count // per)
     total = 2 * (steps - 1) * fields + 2
@@ -743,7 +749,7 @@
     main, east, west = call(
         partial(force_kernel, places, halo_count, steps, fields),
         [struct(len(places), ty, tx), side, side],
-        flag, keep, send, got, east, west,
+        flag, keep, send, got, east, west, sel,
         smem=(0,),
     )
     from_west, from_east = exchange(east, west, "gx", True)
@@ -754,13 +760,6 @@
         main, from_west, from_east,
     )
     from_north, from_south = exchange(south, north, "gy", False)
-    dest = atmos_tile_index.reshape(tiles, entries)
-    sel, weights = call(
-        partial(select_kernel, cap, slots, nb),
-        [struct(tiles * cap, slots), struct(cells, cells)],
-        tile.reshape(1), dest, ocean_block_index.reshape(tiles, entries), regrid,
-        smem=(0,),
-    )
     [packed] = call(
         partial(surface_kernel, places, halo_count, widths, steps, hf),
         [struct(tiles * cap, steps * hf * LANES)],
@@ -812,17 +811,21 @@
         tile.reshape(1), dest, atmos_block_index.reshape(tiles, entries),
         smem=(0,),
     )
-    [own] = call(gather_kernel, [struct(steps * hf, ty, tx)], acc, arrived, ring)
-    far = lax.ppermute(own, "sect", [(0, 1)])
     halo_count = (steps - 1) * fields
     blocks = -(-halo_count // per)
-    east, west = call(partial(late_columns_kernel, steps), [struct(ty, blocks * LANES)] * 2, own, far)
-    from_west, from_east = exchange(east, west, "gx", True, 1)
+    side = struct(ty, blocks * LANES)
+    own, east, west = call(
+        partial(gather_kernel, steps), [struct(steps * hf, ty, tx), side, side], flag, acc, arrived, ring, smem=(0,)
+    )
+    far = lax.ppermute(own, "sect", [(0, 1)])
+    west1, east1 = exchange(east, west, "gx", True, (1, 1))
+    west0, east0 = exchange(east, west, "gx", True, (0, 1))
     widths = with_packed(late_widths(steps, fields), blocks, tx, hw)
-    north, south = call(
-        partial(late_rows_kernel, steps, blocks), [struct(strip_places(widths)[1], SUB, tx)] * 2, own, far, from_west, from_east
-    )
-    from_north, from_south = exchange(south, north, "gy", False, 1)
+    rows = struct(strip_places(widths)[1], SUB, tx)
+    north, south, from_west, from_east = call(
+        partial(late_rows_kernel, steps, blocks), [rows, rows, side, side], own, far, west0, west1, east0, east1
+    )
+    from_north, from_south = exchange(south, north, "gy", False, (1, 1))
     [out] = call(
         partial(late_kernel, steps, blocks),
         [struct(1, nc, ty, tx)],

time: 88.3 us -> 84.2 us (0.954)
  Pallas kernels: 27.8 us -> 23.5 us
  local copies, waits for them, and re-layouts: 3.14 us -> 1.76 us
  starting transfers between devices: 33.7 us -> 34.8 us
    pallas_call x13 -> x12, Pallas kernels: 27.8 us -> 23.5 us  [call(): pl.pallas_call(kernel, out_shape=[pltpu.HBM(o.shape, o.dtype) for o in ou...]
    ppermute x4 -> x6, waiting for transfers between devices: 4.26 us -> 7.69 us  [shifted(): lax.ppermute(x, ('sect', axis), [(a * size + i, b * size + j) for i, j in...]
    ppermute x1, waiting for transfers between devices: 3.11 us -> 0.01 us  [body(): far = lax.ppermute(own, 'sect', [(0, 1)])]
    ppermute x6, waiting for transfers between devices: 12.9 us -> 14.4 us  [shifted(): return lax.ppermute(x, axis, pairs)]
    unnamed x26 -> x20, local copies, waits for them, and re-layouts: 3.14 us -> 1.76 us
    ppermute x1, waiting for transfers between devices: 2.42 us -> 1.26 us  [body(): got = lax.ppermute(send, 'sect', [(0, 1), (1, 0)])]
    ppermute x4 -> x6, starting transfers between devices: 12.5 us -> 13.6 us  [shifted(): lax.ppermute(x, ('sect', axis), [(a * size + i, b * size + j) for i, j in...]
  transfers between devices with their start and end apart: 13 -> 15, of which waited for: 8 -> 8; matrix products, arithmetic and copies ran while one was open for 0% -> 0% of each run, Pallas kernels for 21% -> 18%
where the time goes in v3:
time: 84.2 us; the launch traced here: 83.6 us
  starting transfers between devices  34.8 us (41%)
  Pallas kernels  23.5 us (28%)
  waiting for transfers between devices  23.3 us (28%)
  local copies, waits for them, and re-layouts  1.76 us (2%)
    pallas_call x12, Pallas kernels, call(): pl.pallas_call(kernel, out_shape=[pltpu.HBM(o.shape, o.dtype) for o in ou...  23.5 us
    ppermute x6, waiting for transfers between devices, shifted(): return lax.ppermute(x, axis, pairs)  14.4 us
    ppermute x6, starting transfers between devices, shifted(): return lax.ppermute(x, axis, pairs)  13.7 us
    ppermute x6, starting transfers between devices, shifted(): lax.ppermute(x, ('sect', axis), [(a * size + i, b * size + j) for i, j in...  13.6 us
    ppermute x6, waiting for transfers between devices, shifted(): lax.ppermute(x, ('sect', axis), [(a * size + i, b * size + j) for i, j in...  7.69 us
    all_to_all x1, starting transfers between devices, body(): lax.all_to_all(packed.reshape(tiles, cap, -1), ('gy', 'gx'), split_axis=0...  5.96 us
    unnamed x20, local copies, waits for them, and re-layouts  1.76 us
  transfers between devices with their start and end apart: 15, of which 8 were waited for; matrix products, arithmetic and copies ran while one was open for 0% of the time, Pallas kernels for 18%

profile of v3, /device:TPU:1, one launch (start us, length us, event | category | flops | bytes accessed | tf_op | source)
XLA Modules:
  0.0 83.6 jit_solution(507109927275156652)
XLA Ops:
  0.0 2.9 %shard_map.109 = (f32[12,32,256]{2,1,0:T(8,128)S(1)}, f32[28,32,256]{2,1,0:T(8,128)S(1)}, f32[32,128]{1,0:T(8,128)S(1)}, f32[32,128]{1,0:T(8,128)S(1)}) custom-call(f32[1,32,32,256]{3,2,1,0:T(8,128)} %refs_1_.4, s32[32,256]{1,0:T(8,128)} %mask_hbm.1, f32[1,32,256]{2,1,0:T(8,128)} %diff_hbm.1, f32[1,4,4,32,256]{4,3,2,1,0:T(8,128)} %hist_hbm.1, ...), custom_call_target="tpu_custom_call" | custom-call | bytes 2987520 | tf_op jit(solution)/shard_map/pallas_call | solution.py:201
  2.9 0.1 collective-permute-start
  3.0 1.2 %shard_map.110 = (f32[256,64]{1,0:T(8,128)S(1)}, f32[128,128]{1,0:T(8,128)S(1)}) custom-call(s32[1]{0:T(128)} %bitcast.2.refs_0_, s32[16,128]{1,0:T(8,128)} %bitcast.9, s32[16,128]{1,0:T(8,128)} %bitcast.15, f32[1,128,128]{2,1,0:T(8,128)} %refs_3_.1), custom_call_target="tpu_custom_call" | custom-call | bytes 212996 | tf_op jit(solution)/shard_map/pallas_call | solution.py:201
  4.2 1.3 %collective-permute-done.refs_3_ = f32[28,32,256]{2,1,0:T(8,128)S(1)} collective-permute-done((f32[28,32,256]{2,1,0:T(8,128)S(1)}, f32[28,32,256]{2,1,0:T(8,128)S(1)}, u32[]{:S(2)}, u32[]{:S(2)}) %collective-permute-start) | collective-permute-done | bytes 917536 | tf_op jit(solution)/shard_map/ppermute | solution.py:734
  5.5 0.5 shard_map.111
  6.0 2.5 %collective-permute-start.1 = (f32[32,384]{1,0:T(8,128)S(1)}, f32[32,384]{1,0:T(8,128)S(1)}, u32[]{:S(2)}, u32[]{:S(2)}) collective-permute-start(f32[32,384]{1,0:T(8,128)S(1)} %get-tuple-element.40), channel_id=1, source_target_pairs={{0,1},{1,2},{2,3},{3,0},{4,5},{5,6},{6,7},{7,4},{8,9},{9,10},{10,1... | collective-permute-start | bytes 147464 | tf_op jit(solution)/shard_map/ppermute | solution.py:669
  8.5 2.1 %collective-permute-start.2 = (f32[32,384]{1,0:T(8,128)S(1)}, f32[32,384]{1,0:T(8,128)S(1)}, u32[]{:S(2)}, u32[]{:S(2)}) collective-permute-start(f32[32,384]{1,0:T(8,128)S(1)} %get-tuple-element.41), channel_id=1, source_target_pairs={{0,3},{1,0},{2,1},{3,2},{4,7},{5,4},{6,5},{7,6},{8,11},{9,8},{10,9... | collective-permute-start | bytes 147464 | tf_op jit(solution)/shard_map/ppermute | solution.py:669
  10.6 1.4 %collective-permute-done.1.refs_1_.refs_5_ = f32[32,384]{1,0:T(8,128)S(1)} collective-permute-done((f32[32,384]{1,0:T(8,128)S(1)}, f32[32,384]{1,0:T(8,128)S(1)}, u32[]{:S(2)}, u32[]{:S(2)}) %collective-permute-start.1) | collective-permute-done | bytes 49184 | tf_op jit(solution)/shard_map/ppermute | solution.py:669
  12.0 0.0 collective-permute-done.2.refs_2_.refs_6_
  12.0 3.1 %collective-permute-start.3 = (f32[7,8,256]{2,1,0:T(8,128)S(1)}, f32[7,8,256]{2,1,0:T(8,128)S(1)}, u32[]{:S(2)}, u32[]{:S(2)}) collective-permute-start(f32[7,8,256]{2,1,0:T(8,128)S(1)} %get-tuple-element.43), channel_id=1, source_target_pairs={{0,4},{4,8},{8,12},{1,5},{5,9},{9,13},{2,6},{6,10},{10,14},{3,7},{... | collective-permute-start | bytes 172040 | tf_op jit(solution)/shard_map/ppermute | solution.py:669
  15.2 1.3 %collective-permute-start.4 = (f32[7,8,256]{2,1,0:T(8,128)S(1)}, f32[7,8,256]{2,1,0:T(8,128)S(1)}, u32[]{:S(2)}, u32[]{:S(2)}) collective-permute-start(f32[7,8,256]{2,1,0:T(8,128)S(1)} %get-tuple-element.44), channel_id=1, source_target_pairs={{4,0},{8,4},{12,8},{5,1},{9,5},{13,9},{6,2},{10,6},{14,10},{7,3},{... | collective-permute-start | bytes 172040 | tf_op jit(solution)/shard_map/ppermute | solution.py:669
  16.5 1.1 %shard_map.114 = (f32[24,8,256]{2,1,0:T(8,128)S(1)}, f32[24,8,256]{2,1,0:T(8,128)S(1)}) custom-call(s32[1]{0:T(128)} %bitcast.refs_0_, f32[1,32,32,256]{3,2,1,0:T(8,128)} %refs_1_.4, f32[28,32,256]{2,1,0:T(8,128)S(1)} %get-tuple-element.35.refs_2_, f32[28,32,256]{2,1,0:T(8,128)S(1)} %collective-permute-done.refs_3_, ...), custom_call_target="tpu_custom_call" | custom-call | bytes 3768324 | tf_op jit(solution)/shard_map/pallas_call | solution.py:201
  17.6 0.0 copy-start.9
  17.6 0.0 collective-permute-done.3.refs_3_
  17.6 3.0 %collective-permute-done.4.refs_4_ = f32[7,8,256]{2,1,0:T(8,128)S(1)} collective-permute-done((f32[7,8,256]{2,1,0:T(8,128)S(1)}, f32[7,8,256]{2,1,0:T(8,128)S(1)}, u32[]{:S(2)}, u32[]{:S(2)}) %collective-permute-start.4) | collective-permute-done | bytes 57376 | tf_op jit(solution)/shard_map/ppermute | solution.py:669
  20.6 2.2 %shard_map.113 = f32[256,1024]{1,0:T(8,128)} custom-call(f32[32,32,256]{2,1,0:T(8,128)S(1)} %get-tuple-element.42.refs_0_, f32[32,384]{1,0:T(8,128)S(1)} %collective-permute-done.1.refs_1_.refs_5_, f32[32,384]{1,0:T(8,128)S(1)} %collective-permute-done.2.refs_2_.refs_6_, f32[7,8,256]{2,1,0:T(8,128)S(1)} %collective-permute-done.3.refs_3_, ...), custom_call_target="tpu_custom_call" | custom-call | bytes 2441216 | tf_op jit(solution)/shard_map/pallas_call | solution.py:201
  22.9 0.0 copy-start.4
  22.9 0.0 copy-start.6
  22.9 6.0 %all-to-all-start = ((f32[16,16,1024]{2,1,0:T(8,128)}), f32[16,16,1024]{2,1,0:T(8,128)S(1)}, u32[]{:S(2)}, u32[]{:S(2)}) async-start(f32[16,16,1024]{2,1,0:T(8,128)} %bitcast.14), calls=%async_computation | async-start | bytes 2097152 | tf_op jit(solution)/shard_map/all_to_all | solution.py:781
  28.9 0.0 copy-start.5
  28.9 0.0 copy-start.7
  28.9 3.3 %collective-permute-start.5 = (f32[24,8,256]{2,1,0:T(8,128)}, f32[24,8,256]{2,1,0:T(8,128)S(1)}, u32[]{:S(2)}, u32[]{:S(2)}) collective-permute-start(f32[24,8,256]{2,1,0:T(8,128)} %copy-done.9), channel_id=1, source_target_pairs={{0,4},{4,8},{8,12},{1,5},{5,9},{9,13},{2,6},{6,10},{10,14},{3,7},{... | collective-permute-start | bytes 589832 | tf_op jit(solution)/shard_map/ppermute | solution.py:669
  32.2 1.5 %collective-permute-start.6 = (f32[24,8,256]{2,1,0:T(8,128)}, f32[24,8,256]{2,1,0:T(8,128)S(1)}, u32[]{:S(2)}, u32[]{:S(2)}) collective-permute-start(f32[24,8,256]{2,1,0:T(8,128)} %copy-done.8), channel_id=1, source_target_pairs={{4,0},{8,4},{12,8},{5,1},{9,5},{13,9},{6,2},{10,6},{14,10},{7,3},{... | collective-permute-start | bytes 589832 | tf_op jit(solution)/shard_map/ppermute | solution.py:669
  33.7 2.8 %shard_map.115 = (f32[256,256]{1,0:T(8,128)S(1)}, f32[256,64]{1,0:T(8,128)S(1)}, f32[256,320]{1,0:T(8,128)S(1)}) custom-call(s32[1]{0:T(128)} %bitcast.refs_0_, f32[1,32,32]{2,1,0:T(8,128)S(1)} %copy-done.4, f32[1,8,32]{2,1,0:T(8,128)S(1)} %bitcast.12), custom_call_target="tpu_custom_call" | custom-call | bytes 660484 | tf_op jit(solution)/shard_map/pallas_call | solution.py:201
  36.6 0.8 copy-done.2
  37.3 2.2 %shard_map.117.refs_1_ = f32[64,256]{1,0:T(8,128)S(1)} custom-call(s32[1]{0:T(128)} %bitcast.2.refs_0_, s32[16,128]{1,0:T(8,128)S(1)} %bitcast.10, s32[16,128]{1,0:T(8,128)S(1)} %bitcast.13), custom_call_target="tpu_custom_call" | custom-call | bytes 81924 | tf_op jit(solution)/shard_map/pallas_call | solution.py:201
  39.5 1.3 %collective-permute-done.5.refs_7_ = f32[24,8,256]{2,1,0:T(8,128)S(1)} collective-permute-done((f32[24,8,256]{2,1,0:T(8,128)}, f32[24,8,256]{2,1,0:T(8,128)S(1)}, u32[]{:S(2)}, u32[]{:S(2)}) %collective-permute-start.5) | collective-permute-done | bytes 196640 | tf_op jit(solution)/shard_map/ppermute | solution.py:669
  40.8 8.5 %collective-permute-done.6.refs_8_ = f32[24,8,256]{2,1,0:T(8,128)S(1)} collective-permute-done((f32[24,8,256]{2,1,0:T(8,128)}, f32[24,8,256]{2,1,0:T(8,128)S(1)}, u32[]{:S(2)}, u32[]{:S(2)}) %collective-permute-start.6) | collective-permute-done | bytes 196640 | tf_op jit(solution)/shard_map/ppermute | solution.py:669
  49.4 7.4 %shard_map.116 = (f32[32,32,256]{2,1,0:T(8,128)S(1)}, f32[40,384]{1,0:T(8,128)S(1)}) custom-call(s32[1]{0:T(128)} %bitcast.refs_0_, f32[1,32,32,256]{3,2,1,0:T(8,128)} %refs_1_.4, f32[28,32,256]{2,1,0:T(8,128)S(1)} %get-tuple-element.35.refs_2_, f32[28,32,256]{2,1,0:T(8,128)S(1)} %collective-permute-done.refs_3_, ...), custom_call_target="tpu_custom_call" | custom-call | bytes 5206020 | tf_op jit(solution)/shard_map/pallas_call | solution.py:201
  56.8 0.0 copy-start
  56.8 1.0 %copy-done = f32[32,32,256]{2,1,0:T(8,128)} copy-done((f32[32,32,256]{2,1,0:T(8,128)}, f32[32,32,256]{2,1,0:T(8,128)S(1)}, u32[]{:S(2)}) %copy-start) | copy-done | bytes 1048600
  57.8 0.0 all-to-all-done
  57.8 0.4 shard_map.118
  58.2 1.4 %collective-permute-start.7 = (f32[8,32,256]{2,1,0:T(8,128)S(1)}, f32[8,32,256]{2,1,0:T(8,128)S(1)}, u32[]{:S(2)}, u32[]{:S(2)}) collective-permute-start(f32[8,32,256]{2,1,0:T(8,128)S(1)} %get-tuple-element.58.refs_0_.refs_4_), channel_id=1, source_target_pairs={{0,16},{1,17},{2,18},{3,19},{4,20},{5,21},{6,22},{7,23},{8,24},{9,... | collective-permute-start | bytes 786440 | tf_op jit(solution)/shard_map/ppermute | solution.py:820
  59.6 1.3 %collective-permute-start.10 = (f32[32,128]{1,0:T(8,128)S(1)}, f32[32,128]{1,0:T(8,128)S(1)}, u32[]{:S(2)}, u32[]{:S(2)}) collective-permute-start(f32[32,128]{1,0:T(8,128)S(1)} %get-tuple-element.60), channel_id=1, source_target_pairs={{0,19},{1,16},{2,17},{3,18},{4,23},{5,20},{6,21},{7,22},{8,27},{9,... | collective-permute-start | bytes 49160 | tf_op jit(solution)/shard_map/ppermute | solution.py:671
  60.9 5.0 %collective-permute-start.11 = (f32[32,128]{1,0:T(8,128)S(1)}, f32[32,128]{1,0:T(8,128)S(1)}, u32[]{:S(2)}, u32[]{:S(2)}) collective-permute-start(f32[32,128]{1,0:T(8,128)S(1)} %get-tuple-element.60), channel_id=1, source_target_pairs={{16,19},{17,16},{18,17},{19,18},{20,23},{21,20},{22,21},{23,22},{2... | collective-permute-start | bytes 49160 | tf_op jit(solution)/shard_map/ppermute | solution.py:671
  65.9 1.3 %collective-permute-start.8 = (f32[32,128]{1,0:T(8,128)S(1)}, f32[32,128]{1,0:T(8,128)S(1)}, u32[]{:S(2)}, u32[]{:S(2)}) collective-permute-start(f32[32,128]{1,0:T(8,128)S(1)} %get-tuple-element.59), channel_id=1, source_target_pairs={{0,17},{1,18},{2,19},{3,16},{4,21},{5,22},{6,23},{7,20},{8,25},{9,... | collective-permute-start | bytes 49160 | tf_op jit(solution)/shard_map/ppermute | solution.py:671
  67.2 1.9 %collective-permute-start.9 = (f32[32,128]{1,0:T(8,128)S(1)}, f32[32,128]{1,0:T(8,128)S(1)}, u32[]{:S(2)}, u32[]{:S(2)}) collective-permute-start(f32[32,128]{1,0:T(8,128)S(1)} %get-tuple-element.59), channel_id=1, source_target_pairs={{16,17},{17,18},{18,19},{19,16},{20,21},{21,22},{22,23},{23,20},{2... | collective-permute-start | bytes 49160 | tf_op jit(solution)/shard_map/ppermute | solution.py:671
  69.2 0.0 collective-permute-done.10.refs_4_
  69.2 0.0 collective-permute-done.11.refs_5_
  69.2 3.6 %collective-permute-done.8.refs_2_ = f32[32,128]{1,0:T(8,128)S(1)} collective-permute-done((f32[32,128]{1,0:T(8,128)S(1)}, f32[32,128]{1,0:T(8,128)S(1)}, u32[]{:S(2)}, u32[]{:S(2)}) %collective-permute-start.8) | collective-permute-done | bytes 16416 | tf_op jit(solution)/shard_map/ppermute | solution.py:671
  72.8 0.7 collective-permute-done.9.refs_3_
  73.5 0.0 collective-permute-done.7.refs_1_.refs_5_
  73.5 2.8 %collective-permute-start.12 = (f32[4,8,256]{2,1,0:T(8,128)S(1)}, f32[4,8,256]{2,1,0:T(8,128)S(1)}, u32[]{:S(2)}, u32[]{:S(2)}) collective-permute-start(f32[4,8,256]{2,1,0:T(8,128)S(1)} %get-tuple-element.63), channel_id=1, source_target_pairs={{16,20},{20,24},{24,28},{17,21},{21,25},{25,29},{18,22},{22,26},{2... | collective-permute-start | bytes 98312 | tf_op jit(solution)/shard_map/ppermute | solution.py:671
  76.3 1.3 %collective-permute-start.13 = (f32[4,8,256]{2,1,0:T(8,128)S(1)}, f32[4,8,256]{2,1,0:T(8,128)S(1)}, u32[]{:S(2)}, u32[]{:S(2)}) collective-permute-start(f32[4,8,256]{2,1,0:T(8,128)S(1)} %get-tuple-element.64), channel_id=1, source_target_pairs={{20,16},{24,20},{28,24},{21,17},{25,21},{29,25},{22,18},{26,22},{3... | collective-permute-start | bytes 98312 | tf_op jit(solution)/shard_map/ppermute | solution.py:671
  77.6 0.0 collective-permute-done.12.refs_8_
  77.6 3.3 %collective-permute-done.13.refs_9_ = f32[4,8,256]{2,1,0:T(8,128)S(1)} collective-permute-done((f32[4,8,256]{2,1,0:T(8,128)S(1)}, f32[4,8,256]{2,1,0:T(8,128)S(1)}, u32[]{:S(2)}, u32[]{:S(2)}) %collective-permute-start.13) | collective-permute-done | bytes 32800 | tf_op jit(solution)/shard_map/ppermute | solution.py:671
  81.0 2.6 %shard_map.120 = f32[1,32,32,256]{3,2,1,0:T(8,128)} custom-call(s32[1]{0:T(128)} %bitcast.refs_0_, f32[32,32,256]{2,1,0:T(8,128)S(1)} %copy-done.1, f32[40,384]{1,0:T(8,128)S(1)} %get-tuple-element.54.refs_3_.refs_2_, f32[256,320]{1,0:T(8,128)S(1)} %copy-done.3, f32[8,32,256]{2,1,0:T(8,128)S(1)} %get-tuple-element.58.refs_0_.refs_4_, ...), custom_call_target="tpu_custom_call" | custom-call | bytes 3108868 | tf_op jit(solution)/shard_map/pallas_call | solution.py:201
  (14 shorter events, 0.1 us)
Async XLA Ops:
  2.9 2.5 %collective-permute-start = (f32[28,32,256]{2,1,0:T(8,128)S(1)}, f32[28,32,256]{2,1,0:T(8,128)S(1)}, u32[]{:S(2)}, u32[]{:S(2)}) collective-permute-start(f32[28,32,256]{2,1,0:T(8,128)S(1)} %get-tuple-element.35.refs_2_), channel_id=1, source_target_pairs={{0,16},{16,0},{1,17},{17,1},{2,18},{18,2},{3,19},{19,3},{4,20},{20... | collective-permute-start | bytes 2752520 | tf_op jit(solution)/shard_map/ppermute | solution.py:734
  6.0 6.0 %collective-permute-start.1 = (f32[32,384]{1,0:T(8,128)S(1)}, f32[32,384]{1,0:T(8,128)S(1)}, u32[]{:S(2)}, u32[]{:S(2)}) collective-permute-start(f32[32,384]{1,0:T(8,128)S(1)} %get-tuple-element.40), channel_id=1, source_target_pairs={{0,1},{1,2},{2,3},{3,0},{4,5},{5,6},{6,7},{7,4},{8,9},{9,10},{10,1... | collective-permute-start | bytes 147464 | tf_op jit(solution)/shard_map/ppermute | solution.py:669
  8.5 3.5 %collective-permute-start.2 = (f32[32,384]{1,0:T(8,128)S(1)}, f32[32,384]{1,0:T(8,128)S(1)}, u32[]{:S(2)}, u32[]{:S(2)}) collective-permute-start(f32[32,384]{1,0:T(8,128)S(1)} %get-tuple-element.41), channel_id=1, source_target_pairs={{0,3},{1,0},{2,1},{3,2},{4,7},{5,4},{6,5},{7,6},{8,11},{9,8},{10,9... | collective-permute-start | bytes 147464 | tf_op jit(solution)/shard_map/ppermute | solution.py:669
  12.0 5.6 %collective-permute-start.3 = (f32[7,8,256]{2,1,0:T(8,128)S(1)}, f32[7,8,256]{2,1,0:T(8,128)S(1)}, u32[]{:S(2)}, u32[]{:S(2)}) collective-permute-start(f32[7,8,256]{2,1,0:T(8,128)S(1)} %get-tuple-element.43), channel_id=1, source_target_pairs={{0,4},{4,8},{8,12},{1,5},{5,9},{9,13},{2,6},{6,10},{10,14},{3,7},{... | collective-permute-start | bytes 172040 | tf_op jit(solution)/shard_map/ppermute | solution.py:669
  15.2 5.5 %collective-permute-start.4 = (f32[7,8,256]{2,1,0:T(8,128)S(1)}, f32[7,8,256]{2,1,0:T(8,128)S(1)}, u32[]{:S(2)}, u32[]{:S(2)}) collective-permute-start(f32[7,8,256]{2,1,0:T(8,128)S(1)} %get-tuple-element.44), channel_id=1, source_target_pairs={{4,0},{8,4},{12,8},{5,1},{9,5},{13,9},{6,2},{10,6},{14,10},{7,3},{... | collective-permute-start | bytes 172040 | tf_op jit(solution)/shard_map/ppermute | solution.py:669
  17.6 5.3 %copy-start.8 = (f32[24,8,256]{2,1,0:T(8,128)}, f32[24,8,256]{2,1,0:T(8,128)S(1)}, u32[]{:S(2)}) copy-start(f32[24,8,256]{2,1,0:T(8,128)S(1)} %get-tuple-element.49) | copy-start | bytes 589828
  17.6 5.3 %copy-start.9 = (f32[24,8,256]{2,1,0:T(8,128)}, f32[24,8,256]{2,1,0:T(8,128)S(1)}, u32[]{:S(2)}) copy-start(f32[24,8,256]{2,1,0:T(8,128)S(1)} %get-tuple-element.48) | copy-start | bytes 589828
  22.9 10.8 %copy-start.4 = (f32[1,32,32]{2,1,0:T(8,128)S(1)}, f32[1,32,32]{2,1,0:T(8,128)}, u32[]{:S(2)}) copy-start(f32[1,32,32]{2,1,0:T(8,128)} %refs_1_.3) | copy-start | bytes 12292
  22.9 10.8 %copy-start.6 = (f32[1,32,8]{1,2,0:T(8,128)S(1)}, f32[1,32,8]{1,2,0:T(8,128)}, u32[]{:S(2)}) copy-start(f32[1,32,8]{1,2,0:T(8,128)} %param.14) | copy-start | bytes 3076
  22.9 34.8 %all-to-all-start = ((f32[16,16,1024]{2,1,0:T(8,128)}), f32[16,16,1024]{2,1,0:T(8,128)S(1)}, u32[]{:S(2)}, u32[]{:S(2)}) async-start(f32[16,16,1024]{2,1,0:T(8,128)} %bitcast.14), calls=%async_computation | async-start | bytes 2097152 | tf_op jit(solution)/shard_map/all_to_all | solution.py:781
  28.9 8.4 %copy-start.5 = (s32[2048,1]{0,1:T(1,128)S(1)}, s32[2048,1]{0,1:T(1,128)}, u32[]{:S(2)}) copy-start(s32[2048,1]{0,1:T(1,128)} %param.19) | copy-start | bytes 24580
  28.9 8.4 %copy-start.7 = (s32[2048]{0:T(1024)S(1)}, s32[2048]{0:T(1024)}, u32[]{:S(2)}) copy-start(s32[2048]{0:T(1024)} %param.21) | copy-start | bytes 24580
  28.9 11.9 %collective-permute-start.5 = (f32[24,8,256]{2,1,0:T(8,128)}, f32[24,8,256]{2,1,0:T(8,128)S(1)}, u32[]{:S(2)}, u32[]{:S(2)}) collective-permute-start(f32[24,8,256]{2,1,0:T(8,128)} %copy-done.9), channel_id=1, source_target_pairs={{0,4},{4,8},{8,12},{1,5},{5,9},{9,13},{2,6},{6,10},{10,14},{3,7},{... | collective-permute-start | bytes 589832 | tf_op jit(solution)/shard_map/ppermute | solution.py:669
  32.2 17.2 %collective-permute-start.6 = (f32[24,8,256]{2,1,0:T(8,128)}, f32[24,8,256]{2,1,0:T(8,128)S(1)}, u32[]{:S(2)}, u32[]{:S(2)}) collective-permute-start(f32[24,8,256]{2,1,0:T(8,128)} %copy-done.8), channel_id=1, source_target_pairs={{4,0},{8,4},{12,8},{5,1},{9,5},{13,9},{6,2},{10,6},{14,10},{7,3},{... | collective-permute-start | bytes 589832 | tf_op jit(solution)/shard_map/ppermute | solution.py:669
  36.5 0.8 copy-start.2
  56.8 1.0 %copy-start = (f32[32,32,256]{2,1,0:T(8,128)}, f32[32,32,256]{2,1,0:T(8,128)S(1)}, u32[]{:S(2)}) copy-start(f32[32,32,256]{2,1,0:T(8,128)S(1)} %get-tuple-element.53.refs_1_) | copy-start | bytes 3145732
  57.8 23.2 %copy-start.1 = (f32[32,32,256]{2,1,0:T(8,128)S(1)}, f32[32,32,256]{2,1,0:T(8,128)}, u32[]{:S(2)}) copy-start(f32[32,32,256]{2,1,0:T(8,128)} %copy-done) | copy-start | bytes 3145732
  58.2 22.8 %copy-start.3 = (f32[256,320]{1,0:T(8,128)S(1)}, f32[256,320]{1,0:T(8,128)}, u32[]{:S(2)}) copy-start(f32[256,320]{1,0:T(8,128)} %copy-done.2) | copy-start | bytes 983044
  58.2 15.3 %collective-permute-start.7 = (f32[8,32,256]{2,1,0:T(8,128)S(1)}, f32[8,32,256]{2,1,0:T(8,128)S(1)}, u32[]{:S(2)}, u32[]{:S(2)}) collective-permute-start(f32[8,32,256]{2,1,0:T(8,128)S(1)} %get-tuple-element.58.refs_0_.refs_4_), channel_id=1, source_target_pairs={{0,16},{1,17},{2,18},{3,19},{4,20},{5,21},{6,22},{7,23},{8,24},{9,... | collective-permute-start | bytes 786440 | tf_op jit(solution)/shard_map/ppermute | solution.py:820
  59.6 9.5 %collective-permute-start.10 = (f32[32,128]{1,0:T(8,128)S(1)}, f32[32,128]{1,0:T(8,128)S(1)}, u32[]{:S(2)}, u32[]{:S(2)}) collective-permute-start(f32[32,128]{1,0:T(8,128)S(1)} %get-tuple-element.60), channel_id=1, source_target_pairs={{0,19},{1,16},{2,17},{3,18},{4,23},{5,20},{6,21},{7,22},{8,27},{9,... | collective-permute-start | bytes 49160 | tf_op jit(solution)/shard_map/ppermute | solution.py:671
  60.9 8.3 %collective-permute-start.11 = (f32[32,128]{1,0:T(8,128)S(1)}, f32[32,128]{1,0:T(8,128)S(1)}, u32[]{:S(2)}, u32[]{:S(2)}) collective-permute-start(f32[32,128]{1,0:T(8,128)S(1)} %get-tuple-element.60), channel_id=1, source_target_pairs={{16,19},{17,16},{18,17},{19,18},{20,23},{21,20},{22,21},{23,22},{2... | collective-permute-start | bytes 49160 | tf_op jit(solution)/shard_map/ppermute | solution.py:671
  65.9 6.9 %collective-permute-start.8 = (f32[32,128]{1,0:T(8,128)S(1)}, f32[32,128]{1,0:T(8,128)S(1)}, u32[]{:S(2)}, u32[]{:S(2)}) collective-permute-start(f32[32,128]{1,0:T(8,128)S(1)} %get-tuple-element.59), channel_id=1, source_target_pairs={{0,17},{1,18},{2,19},{3,16},{4,21},{5,22},{6,23},{7,20},{8,25},{9,... | collective-permute-start | bytes 49160 | tf_op jit(solution)/shard_map/ppermute | solution.py:671
  67.2 6.3 %collective-permute-start.9 = (f32[32,128]{1,0:T(8,128)S(1)}, f32[32,128]{1,0:T(8,128)S(1)}, u32[]{:S(2)}, u32[]{:S(2)}) collective-permute-start(f32[32,128]{1,0:T(8,128)S(1)} %get-tuple-element.59), channel_id=1, source_target_pairs={{16,17},{17,18},{18,19},{19,16},{20,21},{21,22},{22,23},{23,20},{2... | collective-permute-start | bytes 49160 | tf_op jit(solution)/shard_map/ppermute | solution.py:671
  73.5 4.1 %collective-permute-start.12 = (f32[4,8,256]{2,1,0:T(8,128)S(1)}, f32[4,8,256]{2,1,0:T(8,128)S(1)}, u32[]{:S(2)}, u32[]{:S(2)}) collective-permute-start(f32[4,8,256]{2,1,0:T(8,128)S(1)} %get-tuple-element.63), channel_id=1, source_target_pairs={{16,20},{20,24},{24,28},{17,21},{21,25},{25,29},{18,22},{22,26},{2... | collective-permute-start | bytes 98312 | tf_op jit(solution)/shard_map/ppermute | solution.py:671
  76.3 4.7 %collective-permute-start.13 = (f32[4,8,256]{2,1,0:T(8,128)S(1)}, f32[4,8,256]{2,1,0:T(8,128)S(1)}, u32[]{:S(2)}, u32[]{:S(2)}) collective-permute-start(f32[4,8,256]{2,1,0:T(8,128)S(1)} %get-tuple-element.64), channel_id=1, source_target_pairs={{20,16},{24,20},{28,24},{21,17},{25,21},{29,25},{22,18},{26,22},{3... | collective-permute-start | bytes 98312 | tf_op jit(solution)/shard_map/ppermute | solution.py:671

commit v4 on v3

--- a/solution.py
+++ b/solution.py
@@ -194,15 +194,15 @@
     return [steps - 1 - n for n, _ in late_fields(steps, fields)]
 
 
-def call(kernel, outs, *args, smem=(), hbm=(), hbm_out=False, scratch=(), flops=0):
+def call(kernel, outs, *args, smem=(), hbm=(), hbm_out=(), scratch=(), flops=0):
     space = lambda i: pltpu.SMEM if i in smem else pltpu.HBM if i in hbm else pltpu.VMEM
     args = [pltpu.with_memory_space_constraint(a, pltpu.HBM) if i in hbm else a for i, a in enumerate(args)]
     nbytes = sum(math.prod(a.shape) * 4 for a in (*args, *outs))
     return pl.pallas_call(
         kernel,
-        out_shape=[pltpu.HBM(o.shape, o.dtype) for o in outs] if hbm_out else outs,
+        out_shape=[pltpu.HBM(o.shape, o.dtype) if i in hbm_out else o for i, o in enumerate(outs)],
         in_specs=[pl.BlockSpec(memory_space=space(i)) for i in range(len(args))],
-        out_specs=[pl.BlockSpec(memory_space=pltpu.HBM if hbm_out else pltpu.VMEM) for _ in outs],
+        out_specs=[pl.BlockSpec(memory_space=pltpu.HBM if i in hbm_out else pltpu.VMEM) for i in range(len(outs))],
         scratch_shapes=scratch,
         compiler_params=pltpu.CompilerParams(vmem_limit_bytes=24 * 2**20),
         cost_estimate=pl.CostEstimate(flops=flops, bytes_accessed=nbytes, transcendentals=0),
@@ -521,13 +521,74 @@
     coup8_ref[...] = grown(jnp.where(jnp.logical_or(first, flag_ref[0] == 0), coup, 0.0))
 
 
+def mixed(state, force, spread, mix8, coup8, k, places):
+    nc = state.shape[0]
+    spots = [(slice(g * SUB, (g + 1) * SUB), slice(c, c + w)) for g, c, w in places]
+    u = jnp.concatenate([state[:, rs, cs].reshape(nc * SUB, -1) for rs, cs in spots], axis=1)
+    h = jnp.concatenate([force[k, :, rs, cs].reshape(coup8.shape[1] // 3, -1) for rs, cs in spots], axis=1)
+    new = dot3(mix8, halves(u)) + bf_dot(coup8, stacked_columns(h))
+    out, at = [], 0
+    for (rs, cs), (_, _, w) in zip(spots, places):
+        out.append((rs, cs, new[:, at : at + w].reshape(nc, SUB, w) + spread[:, rs, cs]))
+        at += w
+    return out
+
+
+def side_places(groups, tx):
+    per = tx // LANES
+    return [tuple((g, tx, LANES) for g in range(at, min(at + per, groups))) for at in range(0, groups, per)]
+
+
+def state_first_kernel(
+    steps, fields, start, flag_ref, adj_hbm, send_ref, got_ref, keep_ref, west_ref, east_ref, mix8_ref, coup8_ref,
+    new_ref, force_ref, ends_ref, adj_ref, state, spread, sem,
+):
+    nc, ty, tx = adj_ref.shape
+    copy = pltpu.make_async_copy(adj_hbm.at[0], adj_ref, sem)
+    copy.start()
+    hw = steps
+    per = LANES // hw
+    read, total = forced_reader(steps, fields, flag_ref, send_ref, got_ref, keep_ref)
+
+    def side(f, block):
+        at = slice((start + block + f // per) * LANES, (start + block + f // per + 1) * LANES)
+        return side_block(west_ref[:, at], east_ref[:, at], f, hw)
+
+    def ext(f):
+        return jnp.concatenate([read(f, slice(0, ty), slice(0, tx)), side(f, 0)], axis=1)
+
+    forced = (steps - 1) * fields
+    for k in range(1, steps):
+        for q in range(fields):
+            force_ref[k, q] = ext((k - 1) * fields + q)
+            force_ref[k, fields + q] = ext(forced + (k - 1) * fields + q)
+    at = (steps + 1) * (fields // 2) + 2
+    for q in range(fields):
+        force_ref[0, q, :, :tx] = send_ref[at + q]
+        force_ref[0, fields + q, :, :tx] = got_ref[at + q]
+    diff, wet = ext(2 * forced), ext(2 * forced + 1)
+    mix8, coup8 = halves(mix8_ref[...]), stacked_rows(coup8_ref[...])
+    block = -(-total // per)
+    empty = jnp.zeros((SUB, tx + LANES), F32)
+    copy.wait()
+    for c in range(nc):
+        u = wet * jnp.concatenate([adj_ref[c], side(c, block)], axis=1)
+        state[c] = u
+        p = diff * u
+        spread[c] = ring_lap(jnp.concatenate([p, empty], axis=0))[:ty]
+        ends_ref[c, :SUB] = p[:SUB]
+        ends_ref[c, SUB:] = p[ty - SUB :]
+    groups = ty // SUB
+    for places in [((g, 0, tx),) for g in range(groups)] + side_places(groups, tx):
+        for rs, cs, value in mixed(state, force_ref, spread, mix8, coup8, steps - 1, places):
+            new_ref[:, rs, cs] = value
+
+
 def state_kernel(
-    steps, fields, start, blocks, flag_ref, adj_hbm, send_ref, got_ref, keep_ref, west_ref, east_ref, north_ref,
-    south_ref, mix8_ref, coup8_ref, out_ref, ring_ref, state, force, spread, sem,
+    steps, fields, start, blocks, flag_ref, new_ref, most_ref, ends_ref, send_ref, got_ref, keep_ref, west_ref,
+    east_ref, north_ref, south_ref, mix8_ref, coup8_ref, out_hbm, ring_ref, out_ref, state, force, spread, sems,
 ):
-    _, nc, ty, tx = adj_hbm.shape
-    copy = pltpu.make_async_copy(adj_hbm.at[0], out_ref, sem)
-    copy.start()
+    nc, ty, tx = new_ref.shape[0], new_ref.shape[1], new_ref.shape[2] - LANES
     hw = steps
     per = LANES // hw
     read, total = forced_reader(steps, fields, flag_ref, send_ref, got_ref, keep_ref)
@@ -538,33 +599,41 @@
         main = read(f, slice(0, ty), slice(0, tx))
         return with_ring(main, wests[f // per], easts[f // per], f, edge, hw)
 
+    def bottom(f, place, block):
+        west, east = wests[block + place // per], easts[block + place // per]
+        return jnp.concatenate([edge(f), side_block(west[ty:], east[ty:], place, hw)], axis=1)
+
     forced = (steps - 1) * fields
+    for k in range(steps):
+        force[k, :, :ty, :] = most_ref[k]
     for k in range(1, steps):
         for q in range(fields):
-            force[k, q] = ext((k - 1) * fields + q)
-            force[k, fields + q] = ext(forced + (k - 1) * fields + q)
-    at = (steps + 1) * (fields // 2) + 2
-    for q in range(fields):
-        force[0, q, :ty, :tx] = send_ref[at + q]
-        force[0, fields + q, :ty, :tx] = got_ref[at + q]
+            for f, to in (((k - 1) * fields + q, q), (forced + (k - 1) * fields + q, fields + q)):
+                force[k, to, ty:, :] = bottom(f, f, 0)
     diff, wet = ext(2 * forced), ext(2 * forced + 1)
     ring_ref[...] = diff
     mix8, coup8 = halves(mix8_ref[...]), stacked_rows(coup8_ref[...])
+    block = -(-total // per)
     groups = ty // SUB
     main = [((g, 0, tx),) for g in range(groups)]
-    halo = [((groups, 0, tx),)] + [
-        tuple((g, tx, LANES) for g in range(at, min(at + tx // LANES, groups + 1)))
-        for at in range(0, groups + 1, tx // LANES)
-    ]
-    copy.wait()
-    block = -(-total // per)
+    below = [((groups, 0, tx),), ((groups, tx, LANES),)]
+
+    sub = lax.broadcasted_iota(jnp.int32, (SUB, tx + LANES), 0)
     for c in range(nc):
-        west, east = wests[block + c // per], easts[block + c // per]
-        state[c, :ty, :tx] = out_ref[c]
-        state[c, ty:, :tx] = edge(total + c)
-        state[c, :, tx:] = side_block(west, east, c, hw)
-
-    for n in range(steps):
+        u = wet[ty:] * bottom(total + c, c, block)
+        p = diff[ty:] * u
+        stack = jnp.concatenate([ends_ref[c, SUB:], p, ends_ref[c, :SUB]], axis=0)
+        spread[c, ty:, :] = ring_lap(stack)[SUB : 2 * SUB]
+        state[c, ty:, :] = u
+        state[c, :SUB, :] = new_ref[c, :SUB] + jnp.where(sub == 0, turn(p, 1), 0.0)
+        state[c, SUB : ty - SUB, :] = new_ref[c, SUB : ty - SUB]
+        state[c, ty - SUB : ty, :] = new_ref[c, ty - SUB :] + jnp.where(sub == SUB - 1, turn(p, -1), 0.0)
+    for places in below:
+        for rs, cs, value in mixed(state, force, spread, mix8, coup8, steps - 1, places):
+            state[:, rs, cs] = value
+
+    leaving = []
+    for n in range(1, steps):
         k = steps - 1 - n
         small = n == steps - 1
 
@@ -575,19 +644,17 @@
             return carry
 
         lax.fori_loop(0, nc, one, 0, unroll=True)
-        for places in main if small else main + halo:
-            spots = [(slice(g * SUB, (g + 1) * SUB), slice(c, c + w)) for g, c, w in places]
-            u = jnp.concatenate([state[:, rs, cs].reshape(nc * SUB, -1) for rs, cs in spots], axis=1)
-            h = jnp.concatenate([force[k, :, rs, cs].reshape(2 * fields * SUB, -1) for rs, cs in spots], axis=1)
-            new = dot3(mix8, halves(u)) + bf_dot(coup8, stacked_columns(h))
-            at = 0
-            for (rs, cs), (_, _, w) in zip(spots, places):
-                value = new[:, at : at + w].reshape(nc, SUB, w) + spread[:, rs, cs]
-                at += w
+        for places in main if small else main + below[:1] + side_places(groups + 1, tx):
+            for rs, cs, value in mixed(state, force, spread, mix8, coup8, k, places):
                 if small:
                     out_ref[:, rs, cs] = value
                 else:
                     state[:, rs, cs] = value
+            if small:
+                leaving.append(pltpu.make_async_copy(out_ref.at[:, rs, :], out_hbm.at[:, rs, :], sems.at[len(leaving)]))
+                leaving[-1].start()
+    for copy in leaving:
+        copy.wait()
 
 
 def late_fields(steps, fields):
@@ -623,7 +690,7 @@
 
 def late_kernel(
     steps, blocks, flag_ref, base_ref, ring_ref, late_ref, own_ref, far_ref, west_ref, east_ref, north_ref, south_ref,
-    out_ref, stack,
+    out_hbm, stack, out_ref, sems,
 ):
     count, ty, tx = own_ref.shape
     hf = count // steps
@@ -635,7 +702,9 @@
 
     @pl.when(flag_ref[0] == 0)
     def _():
-        out_ref[0] = base_ref[...]
+        copy = pltpu.make_async_copy(base_ref, out_hbm.at[0], sems.at[0])
+        copy.start()
+        copy.wait()
 
     @pl.when(flag_ref[0] != 0)
     def _():
@@ -656,10 +725,15 @@
                         r = ring_lap(diff * r)
             at += (k + 1) * fields
         big = halves(late_ref[...])
+        copies = []
         for g in range(ty // SUB):
             rs = slice(g * SUB, (g + 1) * SUB)
             more = dot3(big, halves(stack[:, rs, :].reshape(-1, tx)))
-            out_ref[0, :, rs, :] = base_ref[:, rs, :] + more.reshape(nc, SUB, tx)
+            out_ref[:, rs, :] = base_ref[:, rs, :] + more.reshape(nc, SUB, tx)
+            copies.append(pltpu.make_async_copy(out_ref.at[:, rs, :], out_hbm.at[0, :, rs, :], sems.at[g]))
+            copies[-1].start()
+        for copy in copies:
+            copy.wait()
 
 
 def shifted(x, axis, by, wrap, sects=None):
@@ -764,7 +838,7 @@
         partial(surface_kernel, places, halo_count, widths, steps, hf),
         [struct(tiles * cap, steps * hf * LANES)],
         main, from_west, from_east, from_north, from_south, weights, sel,
-        hbm_out=True,
+        hbm_out=(0,),
         scratch=[pltpu.VMEM((tiles * cap, steps * hf * LANES), F32), pltpu.SemaphoreType.DMA((steps * hf,))],
     )
     widths = with_packed(state_widths(steps, fields, nc), state_blocks, tx, hw)
@@ -791,17 +865,31 @@
         flag, mixing, coupling,
         smem=(0,),
     )
+    new, most, ends = call(
+        partial(state_first_kernel, steps, fields, blocks),
+        [struct(nc, ty, ext[1]), struct(steps, 2 * fields, ty, ext[1]), struct(nc, 2 * SUB, ext[1])],
+        flag, adjoint_init, send, got, keep, from_west, from_east, mix8, coup8,
+        smem=(0,),
+        hbm=(1,),
+        scratch=[
+            pltpu.VMEM((nc, ty, tx), F32),
+            pltpu.VMEM((nc, ty, ext[1]), F32),
+            pltpu.VMEM((nc, ty, ext[1]), F32),
+            pltpu.SemaphoreType.DMA,
+        ],
+    )
     base, ring = call(
         partial(state_kernel, *sizes),
         [struct(nc, ty, tx), struct(*ext)],
-        flag, adjoint_init, send, got, keep, from_west, from_east, from_north, from_south, mix8, coup8,
+        flag, new, most, ends, send, got, keep, from_west, from_east, from_north, from_south, mix8, coup8,
         smem=(0,),
-        hbm=(1,),
+        hbm_out=(0,),
         scratch=[
+            pltpu.VMEM((nc, ty, tx), F32),
             pltpu.VMEM((nc, *ext), F32),
             pltpu.VMEM((steps, 2 * fields, *ext), F32),
             pltpu.VMEM((nc, *ext), F32),
-            pltpu.SemaphoreType.DMA,
+            pltpu.SemaphoreType.DMA((ty // SUB,)),
         ],
     )
 
@@ -831,7 +919,12 @@
         [struct(1, nc, ty, tx)],
         flag, base, ring, late, own, far, from_west, from_east, from_north, from_south,
         smem=(0,),
-        scratch=[pltpu.VMEM((terms, ty, tx), F32)],
+        hbm_out=(0,),
+        scratch=[
+            pltpu.VMEM((terms, ty, tx), F32),
+            pltpu.VMEM((nc, ty, tx), F32),
+            pltpu.SemaphoreType.DMA((ty // SUB,)),
+        ],
     )
     return out
 

time: 84.2 us -> 81.4 us (0.967)
  waiting for transfers between devices: 23.3 us -> 20.1 us
  Pallas kernels: 23.5 us -> 25.3 us
  local copies, waits for them, and re-layouts: 1.76 us -> 0.8 us
    ppermute x6, waiting for transfers between devices: 14.4 us -> 10.6 us  [shifted(): return lax.ppermute(x, axis, pairs)]
    pallas_call x12 -> x13, Pallas kernels: 23.5 us -> 25.3 us  [call(): pl.pallas_call(kernel, out_shape=[pltpu.HBM(o.shape, o.dtype) if i in hbm...]
    unnamed x20 -> x18, local copies, waits for them, and re-layouts: 1.76 us -> 0.8 us
  transfers between devices with their start and end apart: 15 -> 15, of which waited for: 8 -> 8; matrix products, arithmetic and copies ran while one was open for 0% -> 0% of each run, Pallas kernels for 18% -> 21%
where the time goes in v4:
time: 81.4 us; the launch traced here: 80.8 us
  starting transfers between devices  34.1 us (42%)
  Pallas kernels  25.3 us (31%)
  waiting for transfers between devices  20.1 us (25%)
    pallas_call x13, Pallas kernels, call(): pl.pallas_call(kernel, out_shape=[pltpu.HBM(o.shape, o.dtype) if i in hbm...  25.3 us
    ppermute x6, starting transfers between devices, shifted(): return lax.ppermute(x, axis, pairs)  13.7 us
    ppermute x6, starting transfers between devices, shifted(): lax.ppermute(x, ('sect', axis), [(a * size + i, b * size + j) for i, j in...  13 us
    ppermute x6, waiting for transfers between devices, shifted(): return lax.ppermute(x, axis, pairs)  10.6 us
    ppermute x6, waiting for transfers between devices, shifted(): lax.ppermute(x, ('sect', axis), [(a * size + i, b * size + j) for i, j in...  7.69 us
    all_to_all x1, starting transfers between devices, body(): lax.all_to_all(packed.reshape(tiles, cap, -1), ('gy', 'gx'), split_axis=0...  5.96 us
  transfers between devices with their start and end apart: 15, of which 8 were waited for; matrix products, arithmetic and copies ran while one was open for 0% of the time, Pallas kernels for 21%

profile of v4, /device:TPU:1, one launch (start us, length us, event | category | flops | bytes accessed | tf_op | source)
XLA Modules:
  0.0 80.8 jit_solution(13448501192821192847)
XLA Ops:
  0.0 2.9 %shard_map.109 = (f32[12,32,256]{2,1,0:T(8,128)S(1)}, f32[28,32,256]{2,1,0:T(8,128)S(1)}, f32[32,128]{1,0:T(8,128)S(1)}, f32[32,128]{1,0:T(8,128)S(1)}) custom-call(f32[1,32,32,256]{3,2,1,0:T(8,128)} %refs_1_.4, s32[32,256]{1,0:T(8,128)} %mask_hbm.1, f32[1,32,256]{2,1,0:T(8,128)} %diff_hbm.1, f32[1,4,4,32,256]{4,3,2,1,0:T(8,128)} %hist_hbm.1, ...), custom_call_target="tpu_custom_call" | custom-call | bytes 2987520 | tf_op jit(solution)/shard_map/pallas_call | solution.py:201
  2.9 0.1 collective-permute-start
  3.0 1.2 %shard_map.110 = (f32[256,64]{1,0:T(8,128)S(1)}, f32[128,128]{1,0:T(8,128)S(1)}) custom-call(s32[1]{0:T(128)} %bitcast.2.refs_0_, s32[16,128]{1,0:T(8,128)} %bitcast.9, s32[16,128]{1,0:T(8,128)} %bitcast.15, f32[1,128,128]{2,1,0:T(8,128)} %refs_3_.1), custom_call_target="tpu_custom_call" | custom-call | bytes 212996 | tf_op jit(solution)/shard_map/pallas_call | solution.py:201
  4.2 1.3 %collective-permute-done.refs_3_.refs_5_ = f32[28,32,256]{2,1,0:T(8,128)S(1)} collective-permute-done((f32[28,32,256]{2,1,0:T(8,128)S(1)}, f32[28,32,256]{2,1,0:T(8,128)S(1)}, u32[]{:S(2)}, u32[]{:S(2)}) %collective-permute-start) | collective-permute-done | bytes 917536 | tf_op jit(solution)/shard_map/ppermute | solution.py:808
  5.5 0.5 shard_map.111
  6.0 2.5 %collective-permute-start.1 = (f32[32,384]{1,0:T(8,128)S(1)}, f32[32,384]{1,0:T(8,128)S(1)}, u32[]{:S(2)}, u32[]{:S(2)}) collective-permute-start(f32[32,384]{1,0:T(8,128)S(1)} %get-tuple-element.43), channel_id=1, source_target_pairs={{0,1},{1,2},{2,3},{3,0},{4,5},{5,6},{6,7},{7,4},{8,9},{9,10},{10,1... | collective-permute-start | bytes 147464 | tf_op jit(solution)/shard_map/ppermute | solution.py:743
  8.5 2.1 %collective-permute-start.2 = (f32[32,384]{1,0:T(8,128)S(1)}, f32[32,384]{1,0:T(8,128)S(1)}, u32[]{:S(2)}, u32[]{:S(2)}) collective-permute-start(f32[32,384]{1,0:T(8,128)S(1)} %get-tuple-element.44), channel_id=1, source_target_pairs={{0,3},{1,0},{2,1},{3,2},{4,7},{5,4},{6,5},{7,6},{8,11},{9,8},{10,9... | collective-permute-start | bytes 147464 | tf_op jit(solution)/shard_map/ppermute | solution.py:743
  10.6 1.4 %collective-permute-done.1.refs_1_.refs_5_.refs_7_ = f32[32,384]{1,0:T(8,128)S(1)} collective-permute-done((f32[32,384]{1,0:T(8,128)S(1)}, f32[32,384]{1,0:T(8,128)S(1)}, u32[]{:S(2)}, u32[]{:S(2)}) %collective-permute-start.1) | collective-permute-done | bytes 49184 | tf_op jit(solution)/shard_map/ppermute | solution.py:743
  12.0 0.0 collective-permute-done.2.refs_2_.refs_6_.refs_8_
  12.0 3.1 %collective-permute-start.3 = (f32[7,8,256]{2,1,0:T(8,128)S(1)}, f32[7,8,256]{2,1,0:T(8,128)S(1)}, u32[]{:S(2)}, u32[]{:S(2)}) collective-permute-start(f32[7,8,256]{2,1,0:T(8,128)S(1)} %get-tuple-element.46), channel_id=1, source_target_pairs={{0,4},{4,8},{8,12},{1,5},{5,9},{9,13},{2,6},{6,10},{10,14},{3,7},{... | collective-permute-start | bytes 172040 | tf_op jit(solution)/shard_map/ppermute | solution.py:743
  15.2 1.3 %collective-permute-start.4 = (f32[7,8,256]{2,1,0:T(8,128)S(1)}, f32[7,8,256]{2,1,0:T(8,128)S(1)}, u32[]{:S(2)}, u32[]{:S(2)}) collective-permute-start(f32[7,8,256]{2,1,0:T(8,128)S(1)} %get-tuple-element.47), channel_id=1, source_target_pairs={{4,0},{8,4},{12,8},{5,1},{9,5},{13,9},{6,2},{10,6},{14,10},{7,3},{... | collective-permute-start | bytes 172040 | tf_op jit(solution)/shard_map/ppermute | solution.py:743
  16.5 1.1 %shard_map.114 = (f32[24,8,256]{2,1,0:T(8,128)S(1)}, f32[24,8,256]{2,1,0:T(8,128)S(1)}) custom-call(s32[1]{0:T(128)} %bitcast.refs_0_, f32[1,32,32,256]{3,2,1,0:T(8,128)} %refs_1_.4, f32[28,32,256]{2,1,0:T(8,128)S(1)} %get-tuple-element.38.refs_2_.refs_4_, f32[28,32,256]{2,1,0:T(8,128)S(1)} %collective-permute-done.refs_3_.refs_5_, ...), custom_call_target="tpu_custom_call" | custom-call | bytes 3768324 | tf_op jit(solution)/shard_map/pallas_call | solution.py:201
  17.6 0.0 copy-start.8
  17.6 0.0 collective-permute-done.3.refs_3_
  17.6 3.0 %collective-permute-done.4.refs_4_ = f32[7,8,256]{2,1,0:T(8,128)S(1)} collective-permute-done((f32[7,8,256]{2,1,0:T(8,128)S(1)}, f32[7,8,256]{2,1,0:T(8,128)S(1)}, u32[]{:S(2)}, u32[]{:S(2)}) %collective-permute-start.4) | collective-permute-done | bytes 57376 | tf_op jit(solution)/shard_map/ppermute | solution.py:743
  20.6 2.2 %shard_map.113 = f32[256,1024]{1,0:T(8,128)} custom-call(f32[32,32,256]{2,1,0:T(8,128)S(1)} %get-tuple-element.45.refs_0_, f32[32,384]{1,0:T(8,128)S(1)} %collective-permute-done.1.refs_1_.refs_5_.refs_7_, f32[32,384]{1,0:T(8,128)S(1)} %collective-permute-done.2.refs_2_.refs_6_.refs_8_, f32[7,8,256]{2,1,0:T(8,128)S(1)} %collective-permute-done.3.refs_3_, ...), custom_call_target="tpu_custom_call" | custom-call | bytes 2441216 | tf_op jit(solution)/shard_map/pallas_call | solution.py:201
  22.9 0.0 copy-start.3
  22.9 0.0 copy-start.5
  22.9 0.0 copy-start.4
  22.9 0.0 copy-start.6
  23.0 6.0 %all-to-all-start = ((f32[16,16,1024]{2,1,0:T(8,128)}), f32[16,16,1024]{2,1,0:T(8,128)S(1)}, u32[]{:S(2)}, u32[]{:S(2)}) async-start(f32[16,16,1024]{2,1,0:T(8,128)} %bitcast.14), calls=%async_computation | async-start | bytes 2097152 | tf_op jit(solution)/shard_map/all_to_all | solution.py:855
  28.9 3.3 %collective-permute-start.5 = (f32[24,8,256]{2,1,0:T(8,128)}, f32[24,8,256]{2,1,0:T(8,128)S(1)}, u32[]{:S(2)}, u32[]{:S(2)}) collective-permute-start(f32[24,8,256]{2,1,0:T(8,128)} %copy-done.8), channel_id=1, source_target_pairs={{0,4},{4,8},{8,12},{1,5},{5,9},{9,13},{2,6},{6,10},{10,14},{3,7},{... | collective-permute-start | bytes 589832 | tf_op jit(solution)/shard_map/ppermute | solution.py:743
  32.2 1.5 %collective-permute-start.6 = (f32[24,8,256]{2,1,0:T(8,128)}, f32[24,8,256]{2,1,0:T(8,128)S(1)}, u32[]{:S(2)}, u32[]{:S(2)}) collective-permute-start(f32[24,8,256]{2,1,0:T(8,128)} %copy-done.7), channel_id=1, source_target_pairs={{4,0},{8,4},{12,8},{5,1},{9,5},{13,9},{6,2},{10,6},{14,10},{7,3},{... | collective-permute-start | bytes 589832 | tf_op jit(solution)/shard_map/ppermute | solution.py:743
  33.7 2.8 %shard_map.115 = (f32[256,256]{1,0:T(8,128)S(1)}, f32[256,64]{1,0:T(8,128)S(1)}, f32[256,320]{1,0:T(8,128)S(1)}) custom-call(s32[1]{0:T(128)} %bitcast.refs_0_, f32[1,32,32]{2,1,0:T(8,128)S(1)} %copy-done.3, f32[1,8,32]{2,1,0:T(8,128)S(1)} %bitcast.12), custom_call_target="tpu_custom_call" | custom-call | bytes 660484 | tf_op jit(solution)/shard_map/pallas_call | solution.py:201
  36.5 0.8 copy-done.1
  37.3 2.2 %shard_map.118.refs_1_ = f32[64,256]{1,0:T(8,128)S(1)} custom-call(s32[1]{0:T(128)} %bitcast.2.refs_0_, s32[16,128]{1,0:T(8,128)S(1)} %bitcast.10, s32[16,128]{1,0:T(8,128)S(1)} %bitcast.13), custom_call_target="tpu_custom_call" | custom-call | bytes 81924 | tf_op jit(solution)/shard_map/pallas_call | solution.py:201
  39.5 3.7 %shard_map.116 = (f32[32,32,384]{2,1,0:T(8,128)S(1)}, f32[4,8,32,384]{3,2,1,0:T(8,128)S(1)}, f32[32,16,384]{2,1,0:T(8,128)S(1)}) custom-call(s32[1]{0:T(128)} %bitcast.refs_0_, f32[1,32,32,256]{3,2,1,0:T(8,128)} %refs_1_.4, f32[28,32,256]{2,1,0:T(8,128)S(1)} %get-tuple-element.38.refs_2_.refs_4_, f32[28,32,256]{2,1,0:T(8,128)S(1)} %collective-permute-done.refs_3_.refs_5_, ...), custom_call_target="tpu_custom_call" | custom-call | bytes 7634948 | tf_op jit(solution)/shard_map/pallas_call | solution.py:201
  43.2 0.0 collective-permute-done.5.refs_9_
  43.3 6.1 %collective-permute-done.6.refs_10_ = f32[24,8,256]{2,1,0:T(8,128)S(1)} collective-permute-done((f32[24,8,256]{2,1,0:T(8,128)}, f32[24,8,256]{2,1,0:T(8,128)S(1)}, u32[]{:S(2)}, u32[]{:S(2)}) %collective-permute-start.6) | collective-permute-done | bytes 196640 | tf_op jit(solution)/shard_map/ppermute | solution.py:743
  49.4 5.7 %shard_map.117 = (f32[32,32,256]{2,1,0:T(8,128)}, f32[40,384]{1,0:T(8,128)S(1)}) custom-call(s32[1]{0:T(128)} %bitcast.refs_0_, f32[32,32,384]{2,1,0:T(8,128)S(1)} %get-tuple-element.54.refs_1_, f32[4,8,32,384]{3,2,1,0:T(8,128)S(1)} %get-tuple-element.55.refs_2_, f32[32,16,384]{2,1,0:T(8,128)S(1)} %get-tuple-element.56.refs_3_, ...), custom_call_target="tpu_custom_call" | custom-call | bytes 8089604 | tf_op jit(solution)/shard_map/pallas_call | solution.py:201
  55.0 0.0 copy-start
  55.0 0.6 all-to-all-done
  55.6 0.4 shard_map.119
  56.0 1.3 %collective-permute-start.7 = (f32[8,32,256]{2,1,0:T(8,128)S(1)}, f32[8,32,256]{2,1,0:T(8,128)S(1)}, u32[]{:S(2)}, u32[]{:S(2)}) collective-permute-start(f32[8,32,256]{2,1,0:T(8,128)S(1)} %get-tuple-element.64.refs_0_.refs_4_), channel_id=1, source_target_pairs={{0,16},{1,17},{2,18},{3,19},{4,20},{5,21},{6,22},{7,23},{8,24},{9,... | collective-permute-start | bytes 786440 | tf_op jit(solution)/shard_map/ppermute | solution.py:908
  57.3 1.3 %collective-permute-start.10 = (f32[32,128]{1,0:T(8,128)S(1)}, f32[32,128]{1,0:T(8,128)S(1)}, u32[]{:S(2)}, u32[]{:S(2)}) collective-permute-start(f32[32,128]{1,0:T(8,128)S(1)} %get-tuple-element.66), channel_id=1, source_target_pairs={{0,19},{1,16},{2,17},{3,18},{4,23},{5,20},{6,21},{7,22},{8,27},{9,... | collective-permute-start | bytes 49160 | tf_op jit(solution)/shard_map/ppermute | solution.py:745
  58.6 4.5 %collective-permute-start.11 = (f32[32,128]{1,0:T(8,128)S(1)}, f32[32,128]{1,0:T(8,128)S(1)}, u32[]{:S(2)}, u32[]{:S(2)}) collective-permute-start(f32[32,128]{1,0:T(8,128)S(1)} %get-tuple-element.66), channel_id=1, source_target_pairs={{16,19},{17,16},{18,17},{19,18},{20,23},{21,20},{22,21},{23,22},{2... | collective-permute-start | bytes 49160 | tf_op jit(solution)/shard_map/ppermute | solution.py:745
  63.1 1.3 %collective-permute-start.8 = (f32[32,128]{1,0:T(8,128)S(1)}, f32[32,128]{1,0:T(8,128)S(1)}, u32[]{:S(2)}, u32[]{:S(2)}) collective-permute-start(f32[32,128]{1,0:T(8,128)S(1)} %get-tuple-element.65), channel_id=1, source_target_pairs={{0,17},{1,18},{2,19},{3,16},{4,21},{5,22},{6,23},{7,20},{8,25},{9,... | collective-permute-start | bytes 49160 | tf_op jit(solution)/shard_map/ppermute | solution.py:745
  64.4 1.9 %collective-permute-start.9 = (f32[32,128]{1,0:T(8,128)S(1)}, f32[32,128]{1,0:T(8,128)S(1)}, u32[]{:S(2)}, u32[]{:S(2)}) collective-permute-start(f32[32,128]{1,0:T(8,128)S(1)} %get-tuple-element.65), channel_id=1, source_target_pairs={{16,17},{17,18},{18,19},{19,16},{20,21},{21,22},{22,23},{23,20},{2... | collective-permute-start | bytes 49160 | tf_op jit(solution)/shard_map/ppermute | solution.py:745
  66.3 0.0 collective-permute-done.10.refs_4_
  66.3 0.0 collective-permute-done.11.refs_5_
  66.4 3.6 %collective-permute-done.8.refs_2_ = f32[32,128]{1,0:T(8,128)S(1)} collective-permute-done((f32[32,128]{1,0:T(8,128)S(1)}, f32[32,128]{1,0:T(8,128)S(1)}, u32[]{:S(2)}, u32[]{:S(2)}) %collective-permute-start.8) | collective-permute-done | bytes 16416 | tf_op jit(solution)/shard_map/ppermute | solution.py:745
  70.0 0.7 collective-permute-done.9.refs_3_
  70.7 0.0 collective-permute-done.7.refs_1_.refs_5_
  70.7 2.7 %collective-permute-start.12 = (f32[4,8,256]{2,1,0:T(8,128)S(1)}, f32[4,8,256]{2,1,0:T(8,128)S(1)}, u32[]{:S(2)}, u32[]{:S(2)}) collective-permute-start(f32[4,8,256]{2,1,0:T(8,128)S(1)} %get-tuple-element.69), channel_id=1, source_target_pairs={{16,20},{20,24},{24,28},{17,21},{21,25},{25,29},{18,22},{22,26},{2... | collective-permute-start | bytes 98312 | tf_op jit(solution)/shard_map/ppermute | solution.py:745
  73.4 1.3 %collective-permute-start.13 = (f32[4,8,256]{2,1,0:T(8,128)S(1)}, f32[4,8,256]{2,1,0:T(8,128)S(1)}, u32[]{:S(2)}, u32[]{:S(2)}) collective-permute-start(f32[4,8,256]{2,1,0:T(8,128)S(1)} %get-tuple-element.70), channel_id=1, source_target_pairs={{20,16},{24,20},{28,24},{21,17},{25,21},{29,25},{22,18},{26,22},{3... | collective-permute-start | bytes 98312 | tf_op jit(solution)/shard_map/ppermute | solution.py:745
  74.7 0.0 collective-permute-done.12.refs_8_
  74.8 3.3 %collective-permute-done.13.refs_9_ = f32[4,8,256]{2,1,0:T(8,128)S(1)} collective-permute-done((f32[4,8,256]{2,1,0:T(8,128)S(1)}, f32[4,8,256]{2,1,0:T(8,128)S(1)}, u32[]{:S(2)}, u32[]{:S(2)}) %collective-permute-start.13) | collective-permute-done | bytes 32800 | tf_op jit(solution)/shard_map/ppermute | solution.py:745
  78.1 2.5 %shard_map.121 = f32[1,32,32,256]{3,2,1,0:T(8,128)} custom-call(s32[1]{0:T(128)} %bitcast.refs_0_, f32[32,32,256]{2,1,0:T(8,128)S(1)} %copy-done, f32[40,384]{1,0:T(8,128)S(1)} %get-tuple-element.60.refs_3_.refs_2_, f32[256,320]{1,0:T(8,128)S(1)} %copy-done.2, f32[8,32,256]{2,1,0:T(8,128)S(1)} %get-tuple-element.64.refs_0_.refs_4_, ...), custom_call_target="tpu_custom_call" | custom-call | bytes 3108868 | tf_op jit(solution)/shard_map/pallas_call | solution.py:201
  (13 shorter events, 0.1 us)
Async XLA Ops:
  2.9 2.5 %collective-permute-start = (f32[28,32,256]{2,1,0:T(8,128)S(1)}, f32[28,32,256]{2,1,0:T(8,128)S(1)}, u32[]{:S(2)}, u32[]{:S(2)}) collective-permute-start(f32[28,32,256]{2,1,0:T(8,128)S(1)} %get-tuple-element.38.refs_2_.refs_4_), channel_id=1, source_target_pairs={{0,16},{16,0},{1,17},{17,1},{2,18},{18,2},{3,19},{19,3},{4,20},{20... | collective-permute-start | bytes 2752520 | tf_op jit(solution)/shard_map/ppermute | solution.py:808
  6.0 6.0 %collective-permute-start.1 = (f32[32,384]{1,0:T(8,128)S(1)}, f32[32,384]{1,0:T(8,128)S(1)}, u32[]{:S(2)}, u32[]{:S(2)}) collective-permute-start(f32[32,384]{1,0:T(8,128)S(1)} %get-tuple-element.43), channel_id=1, source_target_pairs={{0,1},{1,2},{2,3},{3,0},{4,5},{5,6},{6,7},{7,4},{8,9},{9,10},{10,1... | collective-permute-start | bytes 147464 | tf_op jit(solution)/shard_map/ppermute | solution.py:743
  8.5 3.5 %collective-permute-start.2 = (f32[32,384]{1,0:T(8,128)S(1)}, f32[32,384]{1,0:T(8,128)S(1)}, u32[]{:S(2)}, u32[]{:S(2)}) collective-permute-start(f32[32,384]{1,0:T(8,128)S(1)} %get-tuple-element.44), channel_id=1, source_target_pairs={{0,3},{1,0},{2,1},{3,2},{4,7},{5,4},{6,5},{7,6},{8,11},{9,8},{10,9... | collective-permute-start | bytes 147464 | tf_op jit(solution)/shard_map/ppermute | solution.py:743
  12.0 5.6 %collective-permute-start.3 = (f32[7,8,256]{2,1,0:T(8,128)S(1)}, f32[7,8,256]{2,1,0:T(8,128)S(1)}, u32[]{:S(2)}, u32[]{:S(2)}) collective-permute-start(f32[7,8,256]{2,1,0:T(8,128)S(1)} %get-tuple-element.46), channel_id=1, source_target_pairs={{0,4},{4,8},{8,12},{1,5},{5,9},{9,13},{2,6},{6,10},{10,14},{3,7},{... | collective-permute-start | bytes 172040 | tf_op jit(solution)/shard_map/ppermute | solution.py:743
  15.2 5.5 %collective-permute-start.4 = (f32[7,8,256]{2,1,0:T(8,128)S(1)}, f32[7,8,256]{2,1,0:T(8,128)S(1)}, u32[]{:S(2)}, u32[]{:S(2)}) collective-permute-start(f32[7,8,256]{2,1,0:T(8,128)S(1)} %get-tuple-element.47), channel_id=1, source_target_pairs={{4,0},{8,4},{12,8},{5,1},{9,5},{13,9},{6,2},{10,6},{14,10},{7,3},{... | collective-permute-start | bytes 172040 | tf_op jit(solution)/shard_map/ppermute | solution.py:743
  17.6 5.3 %copy-start.7 = (f32[24,8,256]{2,1,0:T(8,128)}, f32[24,8,256]{2,1,0:T(8,128)S(1)}, u32[]{:S(2)}) copy-start(f32[24,8,256]{2,1,0:T(8,128)S(1)} %get-tuple-element.58) | copy-start | bytes 589828
  17.6 5.4 %copy-start.8 = (f32[24,8,256]{2,1,0:T(8,128)}, f32[24,8,256]{2,1,0:T(8,128)S(1)}, u32[]{:S(2)}) copy-start(f32[24,8,256]{2,1,0:T(8,128)S(1)} %get-tuple-element.57) | copy-start | bytes 589828
  22.9 10.8 %copy-start.3 = (f32[1,32,32]{2,1,0:T(8,128)S(1)}, f32[1,32,32]{2,1,0:T(8,128)}, u32[]{:S(2)}) copy-start(f32[1,32,32]{2,1,0:T(8,128)} %refs_1_.3) | copy-start | bytes 12292
  22.9 10.8 %copy-start.5 = (f32[1,32,8]{1,2,0:T(8,128)S(1)}, f32[1,32,8]{1,2,0:T(8,128)}, u32[]{:S(2)}) copy-start(f32[1,32,8]{1,2,0:T(8,128)} %param.14) | copy-start | bytes 3076
  22.9 14.4 %copy-start.4 = (s32[2048,1]{0,1:T(1,128)S(1)}, s32[2048,1]{0,1:T(1,128)}, u32[]{:S(2)}) copy-start(s32[2048,1]{0,1:T(1,128)} %param.19) | copy-start | bytes 24580
  22.9 14.4 %copy-start.6 = (s32[2048]{0:T(1024)S(1)}, s32[2048]{0:T(1024)}, u32[]{:S(2)}) copy-start(s32[2048]{0:T(1024)} %param.21) | copy-start | bytes 24580
  23.0 32.6 %all-to-all-start = ((f32[16,16,1024]{2,1,0:T(8,128)}), f32[16,16,1024]{2,1,0:T(8,128)S(1)}, u32[]{:S(2)}, u32[]{:S(2)}) async-start(f32[16,16,1024]{2,1,0:T(8,128)} %bitcast.14), calls=%async_computation | async-start | bytes 2097152 | tf_op jit(solution)/shard_map/all_to_all | solution.py:855
  28.9 14.3 %collective-permute-start.5 = (f32[24,8,256]{2,1,0:T(8,128)}, f32[24,8,256]{2,1,0:T(8,128)S(1)}, u32[]{:S(2)}, u32[]{:S(2)}) collective-permute-start(f32[24,8,256]{2,1,0:T(8,128)} %copy-done.8), channel_id=1, source_target_pairs={{0,4},{4,8},{8,12},{1,5},{5,9},{9,13},{2,6},{6,10},{10,14},{3,7},{... | collective-permute-start | bytes 589832 | tf_op jit(solution)/shard_map/ppermute | solution.py:743
  32.2 17.1 %collective-permute-start.6 = (f32[24,8,256]{2,1,0:T(8,128)}, f32[24,8,256]{2,1,0:T(8,128)S(1)}, u32[]{:S(2)}, u32[]{:S(2)}) collective-permute-start(f32[24,8,256]{2,1,0:T(8,128)} %copy-done.7), channel_id=1, source_target_pairs={{4,0},{8,4},{12,8},{5,1},{9,5},{13,9},{6,2},{10,6},{14,10},{7,3},{... | collective-permute-start | bytes 589832 | tf_op jit(solution)/shard_map/ppermute | solution.py:743
  36.5 0.8 copy-start.1
  55.0 23.1 %copy-start = (f32[32,32,256]{2,1,0:T(8,128)S(1)}, f32[32,32,256]{2,1,0:T(8,128)}, u32[]{:S(2)}) copy-start(f32[32,32,256]{2,1,0:T(8,128)} %get-tuple-element.59.refs_1_) | copy-start | bytes 3145732
  55.0 23.1 %copy-start.2 = (f32[256,320]{1,0:T(8,128)S(1)}, f32[256,320]{1,0:T(8,128)}, u32[]{:S(2)}) copy-start(f32[256,320]{1,0:T(8,128)} %copy-done.1) | copy-start | bytes 983044
  56.0 14.7 %collective-permute-start.7 = (f32[8,32,256]{2,1,0:T(8,128)S(1)}, f32[8,32,256]{2,1,0:T(8,128)S(1)}, u32[]{:S(2)}, u32[]{:S(2)}) collective-permute-start(f32[8,32,256]{2,1,0:T(8,128)S(1)} %get-tuple-element.64.refs_0_.refs_4_), channel_id=1, source_target_pairs={{0,16},{1,17},{2,18},{3,19},{4,20},{5,21},{6,22},{7,23},{8,24},{9,... | collective-permute-start | bytes 786440 | tf_op jit(solution)/shard_map/ppermute | solution.py:908
  57.3 9.0 %collective-permute-start.10 = (f32[32,128]{1,0:T(8,128)S(1)}, f32[32,128]{1,0:T(8,128)S(1)}, u32[]{:S(2)}, u32[]{:S(2)}) collective-permute-start(f32[32,128]{1,0:T(8,128)S(1)} %get-tuple-element.66), channel_id=1, source_target_pairs={{0,19},{1,16},{2,17},{3,18},{4,23},{5,20},{6,21},{7,22},{8,27},{9,... | collective-permute-start | bytes 49160 | tf_op jit(solution)/shard_map/ppermute | solution.py:745
  58.6 7.7 %collective-permute-start.11 = (f32[32,128]{1,0:T(8,128)S(1)}, f32[32,128]{1,0:T(8,128)S(1)}, u32[]{:S(2)}, u32[]{:S(2)}) collective-permute-start(f32[32,128]{1,0:T(8,128)S(1)} %get-tuple-element.66), channel_id=1, source_target_pairs={{16,19},{17,16},{18,17},{19,18},{20,23},{21,20},{22,21},{23,22},{2... | collective-permute-start | bytes 49160 | tf_op jit(solution)/shard_map/ppermute | solution.py:745
  63.1 6.9 %collective-permute-start.8 = (f32[32,128]{1,0:T(8,128)S(1)}, f32[32,128]{1,0:T(8,128)S(1)}, u32[]{:S(2)}, u32[]{:S(2)}) collective-permute-start(f32[32,128]{1,0:T(8,128)S(1)} %get-tuple-element.65), channel_id=1, source_target_pairs={{0,17},{1,18},{2,19},{3,16},{4,21},{5,22},{6,23},{7,20},{8,25},{9,... | collective-permute-start | bytes 49160 | tf_op jit(solution)/shard_map/ppermute | solution.py:745
  64.4 6.3 %collective-permute-start.9 = (f32[32,128]{1,0:T(8,128)S(1)}, f32[32,128]{1,0:T(8,128)S(1)}, u32[]{:S(2)}, u32[]{:S(2)}) collective-permute-start(f32[32,128]{1,0:T(8,128)S(1)} %get-tuple-element.65), channel_id=1, source_target_pairs={{16,17},{17,18},{18,19},{19,16},{20,21},{21,22},{22,23},{23,20},{2... | collective-permute-start | bytes 49160 | tf_op jit(solution)/shard_map/ppermute | solution.py:745
  70.7 4.0 %collective-permute-start.12 = (f32[4,8,256]{2,1,0:T(8,128)S(1)}, f32[4,8,256]{2,1,0:T(8,128)S(1)}, u32[]{:S(2)}, u32[]{:S(2)}) collective-permute-start(f32[4,8,256]{2,1,0:T(8,128)S(1)} %get-tuple-element.69), channel_id=1, source_target_pairs={{16,20},{20,24},{24,28},{17,21},{21,25},{25,29},{18,22},{22,26},{2... | collective-permute-start | bytes 98312 | tf_op jit(solution)/shard_map/ppermute | solution.py:745
  73.4 4.7 %collective-permute-start.13 = (f32[4,8,256]{2,1,0:T(8,128)S(1)}, f32[4,8,256]{2,1,0:T(8,128)S(1)}, u32[]{:S(2)}, u32[]{:S(2)}) collective-permute-start(f32[4,8,256]{2,1,0:T(8,128)S(1)} %get-tuple-element.70), channel_id=1, source_target_pairs={{20,16},{24,20},{28,24},{21,17},{25,21},{29,25},{22,18},{26,22},{3... | collective-permute-start | bytes 98312 | tf_op jit(solution)/shard_map/ppermute | solution.py:745
